TPU v7x, 32 devices: a whole 2x2x4 slice. The times are simulated.
32 devices in a mesh: tile: 4 (over y, core), plane: 8 (over z, x).
Axes of the slice: x: 2, y: 2, z: 4, core: 2. Of those that a mesh axis runs over, the one named last changes fastest.
Arguments:
- observed: float32 [2, 8, 256, 256], P(None, 'plane', 'tile'), may hold values from 0.5 to 4
- intersection_strip: float32 [2, 8, 128, 256], P(None, 'plane', 'tile'), may hold values from 0.5 to 4
- axial_taps: float32 [2, 41], replicated, may hold values from 0.05 to 1
- lateral_taps: float32 [2, 15], replicated, may hold values from 0.05 to 1
- extents: int32 [4], P('tile'), may hold values from 1 to 32, as said below
- section_skews: int32 [4], P('tile'), may hold values from 0 to 255
Outputs:
- estimate: float32 [2, 8, 256, 256], P(None, 'plane', 'tile')
Inputs may be any that keep to these rules, and one draw needn't show every extreme that they name: `extents`: entry 0 is not used; the largest of the entries 1 to 3 is 32.
All inputs are finite; a program needn't handle non-finite values.
Results may differ from a plain program's by a relative error of at most 0.00005.
Values sent between devices are 32-bit elements; how exact they have to be, the bound alone decides.
No kernel may reach another device: no remote copies, remote signals or barrier semaphores. Data moves between devices by JAX's collectives and lax.ppermute only.
A program may use at most 64 MiB of HBM per device.

v0:
```python
import jax
import jax.numpy as jnp
from jax import lax
from jax.sharding import PartitionSpec as P

ITERS = 2


highest = lax.Precision.HIGHEST


def with_halo(block, sides, width):
    for axis, dim in sides:
        count = lax.axis_size(axis)
        forward = [(i, i + 1) for i in range(count - 1)]
        backward = [(target, source) for source, target in forward]
        low = lax.ppermute(
            lax.slice_in_dim(block, block.shape[dim] - width, None, axis=dim), axis, forward
        )
        high = lax.ppermute(lax.slice_in_dim(block, 0, width, axis=dim), axis, backward)
        block = jnp.concatenate([low, block, high], axis=dim)
    return block


def from_behind(array, axis, by):
    length = lax.axis_size(axis)
    pairs = [(i, i + by) for i in range(length) if 0 <= i + by < length]
    return lax.ppermute(array, axis, pairs)


def band_matrix(kernel, row_count, col_count, offset):
    offsets = (
        jnp.arange(col_count, dtype=jnp.int32)[None, :]
        - jnp.arange(row_count, dtype=jnp.int32)[:, None]
        + offset
    )
    tap_ids = jnp.arange(kernel.shape[1], dtype=jnp.int32)
    one_hot = jnp.where(offsets[:, :, None] == tap_ids[None, None, :], 1.0, 0.0).astype(jnp.float32)
    return jnp.einsum("ck,rsk->crs", kernel, one_hot, precision=highest)


def blur_rows_x(volume, x_band):
    chans, planes, rowsn, voxels = volume.shape
    blocks = volume.reshape(chans, planes, rowsn, voxels // 128, 128)
    padded = jnp.pad(blocks, ((0, 0), (0, 0), (0, 0), (1, 1), (0, 0)))
    window = jnp.concatenate(
        [padded[:, :, :, :-2], padded[:, :, :, 1:-1], padded[:, :, :, 2:]], axis=4
    )
    result = jnp.einsum("czynw,cow->czyno", window, x_band, precision=highest)
    return result.reshape(chans, planes, rowsn, voxels)


def blur_rows_y(volume, y_band, half_width):
    padded = with_halo(volume, (("tile", 2),), half_width)
    return jnp.einsum("cyp,czpx->czyx", y_band, padded, precision=highest)


def axial_pass(pencils, z_band):
    return jnp.einsum("cij,cjw->ciw", z_band, pencils, precision=highest)


def to_pencils(volume):
    chans, planes, rowsn, voxels = volume.shape
    return lax.all_to_all(
        volume.reshape(chans, planes, rowsn * voxels),
        "plane",
        split_axis=2,
        concat_axis=1,
        tiled=True,
    )


def to_planes(pencils, row_count, col_count):
    flattened = lax.all_to_all(pencils, "plane", split_axis=1, concat_axis=2, tiled=True)
    return flattened.reshape(flattened.shape[0], flattened.shape[1], row_count, col_count)


def shards(observed, intersection_strip, axial_taps, lateral_taps, extents, section_skews):
    chans, planes, row_count, col_count = observed.shape
    strip_count = intersection_strip.shape[2]
    received = from_behind(intersection_strip, "tile", 1)
    turned = jnp.roll(received, section_skews[0], axis=3)
    reach_rows = jnp.where(lax.axis_index("tile") == 0, 0, extents[0])
    inside = (jnp.arange(strip_count, dtype=jnp.int32) < reach_rows)[None, None, :, None]
    top_rows = observed[:, :, :strip_count]
    joined_obs = jnp.concatenate(
        [jnp.where(inside, 0.5 * (top_rows + turned), top_rows), observed[:, :, strip_count:]],
        axis=2,
    )
    axial_width = axial_taps.shape[1]
    lateral_width = lateral_taps.shape[1]
    axial_half = axial_width // 2
    lateral_half = lateral_width // 2
    total_planes = planes * lax.axis_size("plane")
    axial_flip = jnp.flip(axial_taps, axis=1)
    lateral_flip = jnp.flip(lateral_taps, axis=1)
    z_forward = band_matrix(axial_taps, total_planes, total_planes, axial_half)
    z_adjoint = band_matrix(axial_flip, total_planes, total_planes, axial_half)
    y_forward = band_matrix(lateral_taps, row_count, row_count + 2 * lateral_half, 0)
    y_adjoint = band_matrix(lateral_flip, row_count, row_count + 2 * lateral_half, 0)
    x_forward = band_matrix(lateral_taps, 128, 384, lateral_half - 128)
    x_adjoint = band_matrix(lateral_flip, 128, 384, lateral_half - 128)
    estimate = joined_obs
    joined_pencils = to_pencils(joined_obs)
    for sweep in range(ITERS):
        lateral_done = blur_rows_y(blur_rows_x(estimate, x_forward), y_forward, lateral_half)
        blurred = axial_pass(to_pencils(lateral_done), z_forward)
        quotient = joined_pencils / blurred
        spread_back = to_planes(axial_pass(quotient, z_adjoint), row_count, col_count)
        estimate = estimate * blur_rows_x(
            blur_rows_y(spread_back, y_adjoint, lateral_half), x_adjoint
        )
    return estimate


def solution(mesh):
    in_specs = (
        P(None, "plane", "tile", None),
        P(None, "plane", "tile", None),
        P(),
        P(),
        P("tile"),
        P("tile"),
    )
    out_specs = P(None, "plane", "tile", None)
    return jax.shard_map(shards, mesh=mesh, in_specs=in_specs, out_specs=out_specs, check_vma=False)
```

profile of v0, /device:TPU:1, one launch (start us, length us, event | category | flops | bytes accessed | tf_op | source)
XLA Modules:
  0.0 424.1 jit_solution(6670936615190586260)
XLA Ops:
  0.0 4.5 %collective-permute-start = (f32[2,1,32,256]{3,2,0,1:T(8,128)}, f32[2,1,32,256]{3,2,0,1:T(8,128)S(1)}, u32[]{:S(2)}, u32[]{:S(2)}) collective-permute-start(f32[2,1,32,256]{3,2,0,1:T(8,128)} %bitcast.134), channel_id=1, source_target_pairs={{0,8},{8,16},{16,24},{1,9},{9,17},{17,25},{2,10},{10,18},{18,26},{... | collective-permute-start | bytes 196616 | tf_op jit(solution)/shard_map/ppermute | solution.py:28
  5.9 3.3 fusion.10
  11.6 4.6 %copy.89 = f32[2,1,64,256]{0,3,2,1:T(8,128)} copy(f32[2,1,64,256]{3,2,0,1:T(8,128)S(1)} %pad_maximum_fusion) | data formatting | bytes 262144 | tf_op jit(solution)/shard_map/reshape | solution.py:65
  17.1 1.9 collective-permute-start.1
  19.1 2.4 collective-permute-start.2
  21.9 74.4 %reduce = f32[16384,2]{1,0:T(8,128)} reduce(f32[16384,1,2]{2,1,0:T(1,128)} %bitcast.123, f32[]{:T(128)} %broadcast.47), dimensions={1}, to_apply=%bitcast.107.reduce_sub_computation | reduce | bytes 262148
  96.3 8.2 %reshape.225 = f32[8,1,4096]{2,1,0:T(1,128)} reshape(f32[16384,2]{1,0:T(8,128)} %reduce) | data formatting | bytes 262144
  104.5 5.8 %all-to-all-start = ((f32[8,1,4096]{2,1,0:T(1,128)}), f32[8,1,4096]{2,1,0:T(1,128)S(1)}, u32[]{:S(2)}, u32[]{:S(2)}) async-start(f32[8,1,4096]{2,1,0:T(1,128)} %reshape.225), calls=%async_computation | async-start | bytes 262144 | tf_op jit(solution)/shard_map/all_to_all | solution.py:64
  110.7 4.6 %copy.93 = f32[2,1,64,256]{0,3,2,1:T(8,128)} copy(f32[2,1,64,256]{3,2,0,1:T(8,128)S(1)} %convolution_bitcast_fusion.3) | data formatting | bytes 262144 | tf_op jit(solution)/shard_map/reshape | solution.py:65
  115.3 74.4 %reduce.2 = f32[16384,2]{1,0:T(8,128)} reduce(f32[16384,1,2]{2,1,0:T(1,128)} %bitcast.124, f32[]{:T(128)} %broadcast.47), dimensions={1}, to_apply=%bitcast.109.reduce_sub_computation | reduce | bytes 262148
  189.7 8.2 %reshape.227 = f32[8,1,4096]{2,1,0:T(1,128)} reshape(f32[16384,2]{1,0:T(8,128)} %reduce.2) | data formatting | bytes 262144
  197.9 5.9 %all-to-all-start.1 = ((f32[8,1,4096]{2,1,0:T(1,128)}), f32[8,1,4096]{2,1,0:T(1,128)S(1)}, u32[]{:S(2)}, u32[]{:S(2)}) async-start(f32[8,1,4096]{2,1,0:T(1,128)} %reshape.227), calls=%async_computation.1 | async-start | bytes 262144 | tf_op jit(solution)/shard_map/all_to_all | solution.py:64
  206.0 16.5 %reshape.226 = f32[16384,1,2]{2,1,0:T(1,128)} reshape(f32[8,4096]{1,0:T(8,128)S(1)} %reduce.1) | data formatting | bytes 262144
  222.5 5.4 %copy.90 = f32[2,8,2048]{2,1,0:T(8,128)S(1)} copy(f32[2,8,2048]{0,2,1:T(8,128)} %bitcast.126) | data formatting | bytes 262144 | tf_op jit(solution)/shard_map/all_to_all | solution.py:64
  228.7 16.5 %reshape.228 = f32[16384,1,2]{2,1,0:T(1,128)} reshape(f32[8,4096]{1,0:T(8,128)S(1)} %reduce.3) | data formatting | bytes 262144
  245.2 5.2 %copy.94 = f32[2,8,2048]{2,1,0:T(8,128)S(1)} copy(f32[2,8,2048]{0,2,1:T(8,128)} %bitcast.127) | data formatting | bytes 262144 | tf_op jit(solution)/shard_map/all_to_all | solution.py:64
  251.7 5.4 %all-to-all-start.2 = ((f32[2,8,2048]{2,0,1:T(2,128)}), f32[2,8,2048]{2,0,1:T(2,128)S(1)}, u32[]{:S(2)}, u32[]{:S(2)}) async-start(f32[2,8,2048]{2,0,1:T(2,128)} %copy.61), calls=%async_computation.2 | async-start | bytes 262144 | tf_op jit(solution)/shard_map/all_to_all | solution.py:74
  257.8 5.6 %all-to-all-done.2 = f32[2,8,2048]{2,0,1:T(2,128)S(1)} async-done(((f32[2,8,2048]{2,0,1:T(2,128)}), f32[2,8,2048]{2,0,1:T(2,128)S(1)}, u32[]{:S(2)}, u32[]{:S(2)}) %all-to-all-start.2) | async-done | bytes 131104 | tf_op jit(solution)/shard_map/all_to_all | solution.py:74
  263.5 5.7 %collective-permute-start.3 = (f32[2,1,7,256]{3,2,0,1:T(8,128)S(1)}, f32[2,1,7,256]{3,2,0,1:T(8,128)S(1)}, u32[]{:S(2)}, u32[]{:S(2)}) collective-permute-start(f32[2,1,7,256]{3,2,0,1:T(8,128)S(1)} %get-tuple-element.15), channel_id=1, source_target_pairs={{0,8},{8,16},{16,24},{1,9},{9,17},{17,25},{2,10},{10,18},{18,26},{... | collective-permute-start | bytes 43016 | tf_op jit(solution)/shard_map/ppermute | solution.py:17
  269.2 2.1 collective-permute-start.4
  271.4 2.6 fusion.13
  276.2 3.5 collective-permute-start.5
  281.6 3.1 collective-permute-done.6
  285.1 4.6 %copy.99 = f32[2,1,64,256]{0,3,2,1:T(8,128)} copy(f32[2,1,64,256]{3,2,0,1:T(8,128)S(1)} %convolution_bitcast_fusion.1) | data formatting | bytes 262144 | tf_op jit(solution)/shard_map/reshape | solution.py:65
  289.7 74.4 %reduce.4 = f32[16384,2]{1,0:T(8,128)} reduce(f32[16384,1,2]{2,1,0:T(1,128)} %bitcast.125, f32[]{:T(128)} %broadcast.47), dimensions={1}, to_apply=%bitcast.111.reduce_sub_computation | reduce | bytes 262148
  364.1 7.6 %reshape.229 = f32[8,1,4096]{2,1,0:T(1,128)S(1)} reshape(f32[16384,2]{1,0:T(8,128)} %reduce.4) | data formatting | bytes 262144
  371.7 8.8 %all_to_all.54 = f32[8,1,4096]{2,1,0:T(1,128)S(1)} all-to-all(f32[8,1,4096]{2,1,0:T(1,128)S(1)} %reshape.229), channel_id=1, replica_groups=mesh['tile'=4,'plane'=8] {'plane'}, dimensions={0} | all-to-all | bytes 262144 | tf_op jit(solution)/shard_map/all_to_all | solution.py:64
  381.4 16.5 %reshape.230 = f32[16384,1,2]{2,1,0:T(1,128)} reshape(f32[8,4096]{1,0:T(8,128)S(1)} %reduce.5) | data formatting | bytes 262144
  397.9 5.2 %copy.100 = f32[2,8,2048]{2,1,0:T(8,128)S(1)} copy(f32[2,8,2048]{0,2,1:T(8,128)} %bitcast.128) | data formatting | bytes 262144 | tf_op jit(solution)/shard_map/all_to_all | solution.py:64
  403.7 9.4 %all_to_all.55 = f32[2,8,2048]{2,0,1:T(2,128)S(1)} all-to-all(f32[2,8,2048]{2,0,1:T(2,128)S(1)} %copy.77), channel_id=1, replica_groups=mesh['tile'=4,'plane'=8] {'plane'}, dimensions={1} | all-to-all | bytes 262144 | tf_op jit(solution)/shard_map/all_to_all | solution.py:74
  413.2 3.4 collective-permute-start.7
  418.9 2.9 collective-permute-done.8
  (75 shorter events, 18.9 us)
Async XLA Ops:
  0.0 10.4 %collective-permute-start = (f32[2,1,32,256]{3,2,0,1:T(8,128)}, f32[2,1,32,256]{3,2,0,1:T(8,128)S(1)}, u32[]{:S(2)}, u32[]{:S(2)}) collective-permute-start(f32[2,1,32,256]{3,2,0,1:T(8,128)} %bitcast.134), channel_id=1, source_target_pairs={{0,8},{8,16},{16,24},{1,9},{9,17},{17,25},{2,10},{10,18},{18,26},{... | collective-permute-start | bytes 196616 | tf_op jit(solution)/shard_map/ppermute | solution.py:28
  17.1 93.2 %collective-permute-start.1 = (f32[2,1,7,256]{3,2,0,1:T(8,128)S(1)}, f32[2,1,7,256]{3,2,0,1:T(8,128)S(1)}, u32[]{:S(2)}, u32[]{:S(2)}) collective-permute-start(f32[2,1,7,256]{3,2,0,1:T(8,128)S(1)} %get-tuple-element.17), channel_id=1, source_target_pairs={{0,8},{8,16},{16,24},{1,9},{9,17},{17,25},{2,10},{10,18},{18,26},{... | collective-permute-start | bytes 43016 | tf_op jit(solution)/shard_map/ppermute | solution.py:17
  19.1 91.3 %collective-permute-start.2 = (f32[2,1,7,256]{3,2,0,1:T(8,128)S(1)}, f32[2,1,7,256]{3,2,0,1:T(8,128)S(1)}, u32[]{:S(2)}, u32[]{:S(2)}) collective-permute-start(f32[2,1,7,256]{3,2,0,1:T(8,128)S(1)} %get-tuple-element.18), channel_id=1, source_target_pairs={{8,0},{16,8},{24,16},{9,1},{17,9},{25,17},{10,2},{18,10},{26,18},{... | collective-permute-start | bytes 43016 | tf_op jit(solution)/shard_map/ppermute | solution.py:20
  104.5 93.3 %all-to-all-start = ((f32[8,1,4096]{2,1,0:T(1,128)}), f32[8,1,4096]{2,1,0:T(1,128)S(1)}, u32[]{:S(2)}, u32[]{:S(2)}) async-start(f32[8,1,4096]{2,1,0:T(1,128)} %reshape.225), calls=%async_computation | async-start | bytes 262144 | tf_op jit(solution)/shard_map/all_to_all | solution.py:64
  189.7 14.1 %copy-start = (f32[2,41]{1,0:T(2,128)S(1)}, f32[2,41]{1,0:T(2,128)}, u32[]{:S(2)}) copy-start(f32[2,41]{1,0:T(2,128)} %param.8) | copy-start | bytes 988
  197.9 30.0 %all-to-all-start.1 = ((f32[8,1,4096]{2,1,0:T(1,128)}), f32[8,1,4096]{2,1,0:T(1,128)S(1)}, u32[]{:S(2)}, u32[]{:S(2)}) async-start(f32[8,1,4096]{2,1,0:T(1,128)} %reshape.227), calls=%async_computation.1 | async-start | bytes 262144 | tf_op jit(solution)/shard_map/all_to_all | solution.py:64
  245.2 12.0 %copy-start.1 = (f32[2,15]{1,0:T(2,128)S(1)}, f32[2,15]{1,0:T(2,128)}, u32[]{:S(2)}) copy-start(f32[2,15]{1,0:T(2,128)} %param.9) | copy-start | bytes 364
  251.7 11.7 %all-to-all-start.2 = ((f32[2,8,2048]{2,0,1:T(2,128)}), f32[2,8,2048]{2,0,1:T(2,128)S(1)}, u32[]{:S(2)}, u32[]{:S(2)}) async-start(f32[2,8,2048]{2,0,1:T(2,128)} %copy.61), calls=%async_computation.2 | async-start | bytes 262144 | tf_op jit(solution)/shard_map/all_to_all | solution.py:74
  263.5 10.6 %collective-permute-start.3 = (f32[2,1,7,256]{3,2,0,1:T(8,128)S(1)}, f32[2,1,7,256]{3,2,0,1:T(8,128)S(1)}, u32[]{:S(2)}, u32[]{:S(2)}) collective-permute-start(f32[2,1,7,256]{3,2,0,1:T(8,128)S(1)} %get-tuple-element.15), channel_id=1, source_target_pairs={{0,8},{8,16},{16,24},{1,9},{9,17},{17,25},{2,10},{10,18},{18,26},{... | collective-permute-start | bytes 43016 | tf_op jit(solution)/shard_map/ppermute | solution.py:17
  269.2 5.1 %collective-permute-start.4 = (f32[2,1,7,256]{3,2,0,1:T(8,128)S(1)}, f32[2,1,7,256]{3,2,0,1:T(8,128)S(1)}, u32[]{:S(2)}, u32[]{:S(2)}) collective-permute-start(f32[2,1,7,256]{3,2,0,1:T(8,128)S(1)} %get-tuple-element.16), channel_id=1, source_target_pairs={{8,0},{16,8},{24,16},{9,1},{17,9},{25,17},{10,2},{18,10},{26,18},{... | collective-permute-start | bytes 43016 | tf_op jit(solution)/shard_map/ppermute | solution.py:20
  276.2 5.4 %collective-permute-start.5 = (f32[2,1,7,256]{3,2,0,1:T(8,128)S(1)}, f32[2,1,7,256]{3,2,0,1:T(8,128)S(1)}, u32[]{:S(2)}, u32[]{:S(2)}) collective-permute-start(f32[2,1,7,256]{3,2,0,1:T(8,128)S(1)} %get-tuple-element.9), channel_id=1, source_target_pairs={{0,8},{8,16},{16,24},{1,9},{9,17},{17,25},{2,10},{10,18},{18,26},{... | collective-permute-start | bytes 43016 | tf_op jit(solution)/shard_map/ppermute | solution.py:17
  279.7 5.1 %collective-permute-start.6 = (f32[2,1,7,256]{3,2,0,1:T(8,128)S(1)}, f32[2,1,7,256]{3,2,0,1:T(8,128)S(1)}, u32[]{:S(2)}, u32[]{:S(2)}) collective-permute-start(f32[2,1,7,256]{3,2,0,1:T(8,128)S(1)} %get-tuple-element.10), channel_id=1, source_target_pairs={{8,0},{16,8},{24,16},{9,1},{17,9},{25,17},{10,2},{18,10},{26,18},{... | collective-permute-start | bytes 43016 | tf_op jit(solution)/shard_map/ppermute | solution.py:20
  413.2 5.6 %collective-permute-start.7 = (f32[2,1,7,256]{3,2,0,1:T(8,128)S(1)}, f32[2,1,7,256]{3,2,0,1:T(8,128)S(1)}, u32[]{:S(2)}, u32[]{:S(2)}) collective-permute-start(f32[2,1,7,256]{3,2,0,1:T(8,128)S(1)} %get-tuple-element.7), channel_id=1, source_target_pairs={{0,8},{8,16},{16,24},{1,9},{9,17},{17,25},{2,10},{10,18},{18,26},{... | collective-permute-start | bytes 43016 | tf_op jit(solution)/shard_map/ppermute | solution.py:17
  416.7 5.1 %collective-permute-start.8 = (f32[2,1,7,256]{3,2,0,1:T(8,128)S(1)}, f32[2,1,7,256]{3,2,0,1:T(8,128)S(1)}, u32[]{:S(2)}, u32[]{:S(2)}) collective-permute-start(f32[2,1,7,256]{3,2,0,1:T(8,128)S(1)} %get-tuple-element.8), channel_id=1, source_target_pairs={{8,0},{16,8},{24,16},{9,1},{17,9},{25,17},{10,2},{18,10},{26,18},{... | collective-permute-start | bytes 43016 | tf_op jit(solution)/shard_map/ppermute | solution.py:20
where the time goes:
time: 433 us; the launch traced here: 424 us
  other arithmetic  227 us (52%)
  local copies, waits for them, and re-layouts  106 us (24%)
  starting transfers between devices  44.5 us (10%)
  blocking collectives  18.2 us (4%)
  matrix products  13.6 us (3%)
  waiting for transfers between devices  11.8 us (3%)
    unnamed x3, other arithmetic  223 us
    unnamed x11, local copies, waits for them, and re-layouts  74 us
    all_to_all x3, local copies, waits for them, and re-layouts, to_pencils(): lax.all_to_all(volume.reshape(chans, planes, rowsn * voxels), 'plane', sp...  15.8 us
    ppermute x4, starting transfers between devices, with_halo(): lax.ppermute(lax.slice_in_dim(block, block.shape[dim] - width, None, axis...  14.5 us
    reshape x3, local copies, waits for them, and re-layouts, to_pencils(): volume.reshape(chans, planes, rowsn * voxels)  13.9 us
    all_to_all x2, starting transfers between devices, to_pencils(): lax.all_to_all(volume.reshape(chans, planes, rowsn * voxels), 'plane', sp...  11.6 us
    all_to_all x1, blocking collectives, to_planes(): lax.all_to_all(pencils, 'plane', split_axis=1, concat_axis=2, tiled=True)  9.38 us
    dot_general x6, matrix products, band_matrix(): return jnp.einsum('ck,rsk->crs', kernel, one_hot, precision=highest)  8.85 us
  transfers between devices with their start and end apart: 12, of which 4 were waited for; matrix products, arithmetic and copies ran while one was open for 48% of the time, Pallas kernels for 0%

commit v1 on v0

v1 whole, which is shorter than its diff:
```python
import jax
import jax.numpy as jnp
from jax import lax
from jax.experimental import pallas as pl
from jax.experimental.pallas import tpu as pltpu
from jax.sharding import PartitionSpec as P

ITERS = 2
LANES = 128
GROUP = 8
VMEM_LIMIT = 48 * 1024 * 1024


def params():
    return pltpu.CompilerParams(vmem_limit_bytes=VMEM_LIMIT)


def in_vmem():
    return pl.BlockSpec(memory_space=pltpu.VMEM)


def in_smem():
    return pl.BlockSpec(memory_space=pltpu.SMEM)


def pack_kernel(place, following, own, strip, below, above, windows, rows, *, reach, blocks, row_blocks):
    chans, _, row_count, voxels = own.shape
    strip_rows = strip.shape[2]
    lane = lax.broadcasted_iota(jnp.int32, (1, LANES), 1)
    tall = lax.broadcasted_iota(jnp.int32, (strip_rows, voxels), 0)
    edge = LANES // 4
    block_rows = row_count // row_blocks
    window_rows = block_rows + 2 * reach
    for c in range(chans):
        rows[c, 0:reach, :] = below[c, 0, below.shape[2] - reach :, :]
        turned = pltpu.roll(below[c, 0, 0:strip_rows, :], place[1], 1)
        top = own[c, 0, 0:strip_rows, :]
        rows[c, reach : reach + strip_rows, :] = jnp.where(tall < place[0], 0.5 * (top + turned), top)
        rows[c, reach + strip_rows : reach + row_count, :] = own[c, 0, strip_rows:, :]
        turned = pltpu.roll(strip[c, 0], following[1], 1)
        top = above[c, 0, 0:strip_rows, :]
        after = jnp.where(tall < following[0], 0.5 * (top + turned), top)
        rows[c, reach + row_count : row_count + 2 * reach, :] = after[0:reach]
        whole = rows[c, 0 : row_count + 2 * reach, :]
        left, right = whole[:, :LANES], whole[:, LANES:]
        left_up, left_down = pltpu.roll(left, edge, 1), pltpu.roll(left, LANES - edge, 1)
        right_up, right_down = pltpu.roll(right, edge, 1), pltpu.roll(right, LANES - edge, 1)
        low, high = lane < edge, lane < LANES - edge
        cut = (
            jnp.where(low, 0.0, left_up),
            jnp.where(high, left_down, right_down),
            jnp.where(low, left_up, right_up),
            jnp.where(high, right_down, 0.0),
        )
        for b in range(row_blocks):
            for j in range(blocks):
                start = b * block_rows
                windows[(c * row_blocks + b) * blocks + j] = cut[j][start : start + window_rows]


def split(value):
    high = value.astype(jnp.bfloat16)
    low = (value - high.astype(jnp.float32)).astype(jnp.bfloat16)
    return high, low


def deconvolve_kernel(chan, axial, lateral, windows, result, bands, blurred, spread, estimate, *, reach, out_rows):
    planes, window_rows, _ = windows.shape
    axial_half, lateral_half = axial.shape[1] // 2, lateral.shape[1] // 2
    lateral_width = lateral.shape[1]
    c = chan[0]
    lateral_taps = [lateral[c, j] for j in range(lateral_width)]
    offset = lax.broadcasted_iota(jnp.int32, (LANES, LANES), 0) - lax.broadcasted_iota(jnp.int32, (LANES, LANES), 1)
    for which in range(2):
        band = jnp.zeros((LANES, LANES), jnp.float32)
        for j in range(lateral_width):
            tap = lateral_taps[j if which == 0 else lateral_width - 1 - j]
            band = jnp.where(offset == j - lateral_half, tap, band)
        high, low = split(band)
        bands[which, 0:LANES, 0:LANES] = high
        bands[which, 0:LANES, LANES:] = low
        bands[which, LANES:, 0:LANES] = high
        bands[which, LANES:, LANES:] = jnp.zeros_like(high)

    def along_x(value, which):
        both = jnp.concatenate(split(value), axis=1)
        product = jnp.dot(both, bands[which], preferred_element_type=jnp.float32)
        return product[:, :LANES] + product[:, LANES:]

    def along_y(source, q, g, flipped):
        total = None
        for j in range(lateral_width):
            tap = lateral_taps[lateral_width - 1 - j if flipped else j]
            term = tap * source[q, pl.ds(g * GROUP + j, GROUP), :]
            total = term if total is None else total + term
        return total

    def along_z(values, flipped):
        out = []
        for p in range(planes):
            total = None
            for q in range(planes):
                at = (p - q if flipped else q - p) + axial_half
                if 0 <= at < 2 * axial_half + 1:
                    term = axial[c, at] * values[q]
                    total = term if total is None else total + term
            out.append(total)
        return out

    def groups(rows):
        return -(-rows // GROUP)

    rows_left = window_rows
    origin = 0
    for sweep in range(ITERS):
        if sweep == 0:
            flat = windows[...].reshape(planes * window_rows, LANES)
            blurred[:, 0:window_rows, :] = along_x(flat, 0).reshape(planes, window_rows, LANES)
            blurred[:, window_rows:, :] = jnp.zeros((planes, blurred.shape[1] - window_rows, LANES), jnp.float32)
        else:
            tall = groups(rows_left) * GROUP
            flat = estimate[:, 0:tall, :].reshape(planes * tall, LANES)
            blurred[:, 0:tall, :] = along_x(flat, 0).reshape(planes, tall, LANES)
        rows_left -= 2 * lateral_half
        origin += lateral_half

        def forward(g, carry, origin=origin):
            mixed = along_z([along_y(blurred, q, g, False) for q in range(planes)], False)
            at = pl.ds(pl.multiple_of(g * GROUP, GROUP), GROUP)
            quotient = []
            for p in range(planes):
                joined = windows[p, pl.ds(g * GROUP + origin, GROUP), :]
                quotient.append(joined / jnp.where(joined > 0.0, mixed[p], 1.0))
            back = along_z(quotient, True)
            for p in range(planes):
                spread[p, at, :] = back[p]
            return carry

        forward_groups = groups(rows_left)
        last = (window_rows - origin) // GROUP
        lax.fori_loop(0, min(forward_groups, last), forward, 0)
        rows_left -= 2 * lateral_half
        origin += lateral_half

        def backward(g, carry):
            at = pl.ds(pl.multiple_of(g * GROUP, GROUP), GROUP)
            for q in range(planes):
                blurred[q, at, :] = along_y(spread, q, g, True)
            return carry

        tall = groups(rows_left) * GROUP
        lax.fori_loop(0, groups(rows_left), backward, 0)
        factor = along_x(blurred[:, 0:tall, :].reshape(planes * tall, LANES), 1).reshape(planes, tall, LANES)
        before = windows[:, origin : origin + tall, :] if sweep == 0 else estimate[:, lateral_half * 2 : lateral_half * 2 + tall, :]
        estimate[:, 0:tall, :] = before * factor
    half = out_rows // 2
    side = (LANES - LANES // 2) // 2
    lane = lax.broadcasted_iota(jnp.int32, (1, LANES), 1)
    for p in range(planes):
        first = pltpu.roll(estimate[p, 0:half, :], LANES - side, 1)
        second = pltpu.roll(estimate[p, half:out_rows, :], side, 1)
        result[p] = jnp.where(lane < LANES // 2, first, second)


def unpack_kernel(received, out, *, blocks, row_blocks):
    chans, _, row_count, voxels = out.shape
    half = received.shape[1]
    lane = lax.broadcasted_iota(jnp.int32, (1, LANES), 1)
    for c in range(chans):
        for b in range(row_blocks):
            for pair in range(blocks // 2):
                at = (c * row_blocks + b) * blocks + 2 * pair
                even, odd = received[at], received[at + 1]
                row = b * 2 * half
                columns = slice(pair * LANES, (pair + 1) * LANES)
                out[c, 0, row : row + half, columns] = jnp.where(lane < LANES // 2, even, pltpu.roll(odd, LANES // 2, 1))
                out[c, 0, row + half : row + 2 * half, columns] = jnp.where(lane < LANES // 2, pltpu.roll(even, LANES // 2, 1), odd)


def shards(observed, intersection_strip, axial_taps, lateral_taps, extents, section_skews):
    chans, _, row_count, voxels = observed.shape
    strip_rows = intersection_strip.shape[2]
    planes = lax.axis_size("plane")
    tiles = lax.axis_size("tile")
    lateral_half = lateral_taps.shape[1] // 2
    reach = 2 * ITERS * lateral_half
    blocks = voxels // (LANES // 2)
    row_blocks = planes // (chans * blocks)
    out_rows = row_count // row_blocks
    window_rows = out_rows + 2 * reach
    up = [(i, i + 1) for i in range(tiles - 1)]
    down = [(i + 1, i) for i in range(tiles - 1)]

    numbers = jnp.concatenate([extents, section_skews])
    marks = jnp.broadcast_to(numbers.astype(jnp.float32)[None, None, :, None], (chans, 1, 2, voxels))
    below = lax.ppermute(jnp.concatenate([intersection_strip, observed[:, :, row_count - strip_rows :]], axis=2), "tile", up)
    above = lax.ppermute(jnp.concatenate([observed[:, :, :strip_rows], marks], axis=2), "tile", down)
    following = above[0, 0, strip_rows:, 0].astype(jnp.int32)
    first_tile = lax.axis_index("tile") == 0
    place = jnp.where(jnp.stack([first_tile, False]), 0, numbers)

    windows = pl.pallas_call(
        lambda *refs: pack_kernel(*refs, reach=reach, blocks=blocks, row_blocks=row_blocks),
        out_shape=jax.ShapeDtypeStruct((planes, window_rows, LANES), jnp.float32),
        in_specs=[in_smem(), in_smem()] + [in_vmem()] * 4,
        out_specs=in_vmem(),
        scratch_shapes=[pltpu.VMEM((chans, row_count + 2 * reach, voxels), jnp.float32)],
        compiler_params=params(),
        name="pack",
    )(place, following, observed, intersection_strip, below, above)
    windows = lax.all_to_all(windows, "plane", 0, 0, tiled=True)

    channel = (lax.axis_index("plane") // (planes // chans)).astype(jnp.int32).reshape(1)
    padded = window_rows + 2 * GROUP
    result = pl.pallas_call(
        lambda *refs: deconvolve_kernel(*refs, reach=reach, out_rows=out_rows),
        out_shape=jax.ShapeDtypeStruct((planes, out_rows // 2, LANES), jnp.float32),
        in_specs=[in_smem()] * 3 + [in_vmem()],
        out_specs=in_vmem(),
        scratch_shapes=[
            pltpu.VMEM((2, 2 * LANES, 2 * LANES), jnp.bfloat16),
            pltpu.VMEM((planes, padded, LANES), jnp.float32),
            pltpu.VMEM((planes, padded, LANES), jnp.float32),
            pltpu.VMEM((planes, padded, LANES), jnp.float32),
        ],
        compiler_params=params(),
        name="deconvolve",
    )(channel, axial_taps, lateral_taps, windows)
    received = lax.all_to_all(result, "plane", 0, 0, tiled=True)
    return pl.pallas_call(
        lambda *refs: unpack_kernel(*refs, blocks=blocks, row_blocks=row_blocks),
        out_shape=jax.ShapeDtypeStruct(observed.shape, jnp.float32),
        in_specs=[in_vmem()],
        out_specs=in_vmem(),
        compiler_params=params(),
        name="unpack",
    )(received)


def solution(mesh):
    in_specs = (
        P(None, "plane", "tile", None),
        P(None, "plane", "tile", None),
        P(),
        P(),
        P("tile"),
        P("tile"),
    )
    out_specs = P(None, "plane", "tile", None)
    return jax.shard_map(shards, mesh=mesh, in_specs=in_specs, out_specs=out_specs, check_vma=False)
```

time: 433 us -> 48.7 us (0.11)
  the two profiles are of different devices: /device:TPU:1 before, /device:TPU:0 now
where the time goes in v1:
time: 48.7 us; the launch traced here: 48.4 us
  waiting for transfers between devices  15.1 us (31%)
  starting transfers between devices  11.7 us (24%)
  blocking collectives  11.5 us (24%)
  Pallas kernels  7.32 us (15%)
  between operations  1.38 us (3%)
  local copies, waits for them, and re-layouts  0.99 us (2%)
    all_to_all x1, waiting for transfers between devices, shards(): windows = lax.all_to_all(windows, 'plane', 0, 0, tiled=True)  14.4 us
    all_to_all x1, blocking collectives, shards(): received = lax.all_to_all(result, 'plane', 0, 0, tiled=True)  11.5 us
    all_to_all x1, starting transfers between devices, shards(): windows = lax.all_to_all(windows, 'plane', 0, 0, tiled=True)  7.25 us
    pallas_call x1, Pallas kernels, shards(): pl.pallas_call(lambda *refs: deconvolve_kernel(*refs, reach=reach, out_ro...  4.91 us
    ppermute x1, starting transfers between devices, shards(): lax.ppermute(jnp.concatenate([intersection_strip, observed[:, :, row_coun...  3.17 us
    pallas_call x1, Pallas kernels, shards(): pl.pallas_call(lambda *refs: pack_kernel(*refs, reach=reach, blocks=block...  1.66 us
    ppermute x1, starting transfers between devices, shards(): lax.ppermute(jnp.concatenate([observed[:, :, :strip_rows], marks], axis=2...  1.28 us
  transfers between devices with their start and end apart: 3, of which 2 were waited for; matrix products, arithmetic and copies ran while one was open for 0% of the time, Pallas kernels for 0%

profile of v1, /device:TPU:0, one launch (start us, length us, event | category | flops | bytes accessed | tf_op | source)
XLA Modules:
  0.0 48.4 jit_solution(369060627614445763)
XLA Ops:
  1.3 0.9 %fusion.2 = (f32[2,1,32,256]{3,2,1,0:T(8,128)S(1)}, f32[2,1,32,256]{3,2,1,0:T(8,128)S(1)}) fusion(f32[2,1,64,256]{3,2,1,0:T(8,128)} %refs_2_.2), kind=kLoop, calls=%fused_computation.7 | loop fusion | bytes 262144 | tf_op jit(solution)/shard_map/slice | solution.py:196
  2.2 0.1 fusion.1
  2.3 0.1 pad.3.clone
  2.3 0.0 copy-start.1
  2.3 0.1 pad_maximum_fusion.1
  2.4 1.3 %collective-permute-start = (f32[2,1,34,256]{3,2,1,0:T(8,128)S(1)}, f32[2,1,34,256]{3,2,1,0:T(8,128)S(1)}, u32[]{:S(2)}, u32[]{:S(2)}) collective-permute-start(f32[2,1,34,256]{3,2,1,0:T(8,128)S(1)} %pad_maximum_fusion.1), channel_id=1, source_target_pairs={{8,0},{16,8},{24,16},{9,1},{17,9},{25,17},{10,2},{18,10},{26,18},{... | collective-permute-start | bytes 208904 | tf_op jit(solution)/shard_map/ppermute | solution.py:197
  3.7 0.0 copy-done.1
  3.7 0.0 copy-start
  3.8 3.2 %collective-permute-start.1 = (f32[2,1,64,256]{3,2,1,0:T(8,128)S(1)}, f32[2,1,64,256]{3,2,1,0:T(8,128)S(1)}, u32[]{:S(2)}, u32[]{:S(2)}) collective-permute-start(f32[2,1,64,256]{3,2,1,0:T(8,128)S(1)} %pad_maximum_fusion), channel_id=1, source_target_pairs={{0,8},{8,16},{16,24},{1,9},{9,17},{17,25},{2,10},{10,18},{18,26},{... | collective-permute-start | bytes 393224 | tf_op jit(solution)/shard_map/ppermute | solution.py:196
  6.9 0.1 add_select_fusion.refs_0_
  7.0 0.0 collective-permute-done.refs_5_
  7.0 0.1 fusion.refs_1_
  7.1 0.8 %collective-permute-done.1.refs_4_ = f32[2,1,64,256]{3,2,1,0:T(8,128)S(1)} collective-permute-done((f32[2,1,64,256]{3,2,1,0:T(8,128)S(1)}, f32[2,1,64,256]{3,2,1,0:T(8,128)S(1)}, u32[]{:S(2)}, u32[]{:S(2)}) %collective-permute-start.1) | collective-permute-done | bytes 131104 | tf_op jit(solution)/shard_map/ppermute | solution.py:196
  7.9 0.0 copy-done
  7.9 1.7 %pack.1 = f32[8,120,128]{2,1,0:T(8,128)} custom-call(s32[2]{0:T(128)S(1)} %add_select_fusion.refs_0_, s32[2]{0:T(128)S(1)} %fusion.refs_1_, f32[2,1,64,256]{3,2,1,0:T(8,128)S(1)} %copy-done, f32[2,1,32,256]{3,2,1,0:T(8,128)S(1)} %copy-done.1, f32[2,1,64,256]{3,2,1,0:T(8,128)S(1)} %collective-permute-done.1.refs_4_, ...), custom_call_target="tpu_custom_call" | custom-call | tf_op jit(solution)/shard_map/pack/pallas_call | solution.py:202
  9.6 7.3 %all-to-all-start = ((f32[8,120,128]{2,1,0:T(8,128)}), f32[8,120,128]{2,1,0:T(8,128)S(1)}, u32[]{:S(2)}, u32[]{:S(2)}) async-start(f32[8,120,128]{2,1,0:T(8,128)} %pack.1), calls=%async_computation | async-start | bytes 983040 | tf_op jit(solution)/shard_map/all_to_all | solution.py:211
  16.8 0.0 copy-start.3
  16.8 0.0 copy-start.2
  16.8 14.4 %all-to-all-done.refs_3_ = f32[8,120,128]{2,1,0:T(8,128)S(1)} async-done(((f32[8,120,128]{2,1,0:T(8,128)}), f32[8,120,128]{2,1,0:T(8,128)S(1)}, u32[]{:S(2)}, u32[]{:S(2)}) %all-to-all-start) | async-done | bytes 491552 | tf_op jit(solution)/shard_map/all_to_all | solution.py:211
  31.2 0.0 copy-done.3
  31.2 0.0 copy-done.2
  31.2 4.9 %deconvolve.1 = f32[8,32,128]{2,1,0:T(8,128)S(1)} custom-call(s32[1]{0:T(128)} %bitcast.refs_0_, f32[2,41]{1,0:T(2,128)S(1)} %copy-done.2, f32[2,15]{1,0:T(2,128)S(1)} %copy-done.3, f32[8,120,128]{2,1,0:T(8,128)S(1)} %all-to-all-done.refs_3_), custom_call_target="tpu_custom_call" | custom-call | tf_op jit(solution)/shard_map/deconvolve/pallas_call | solution.py:215
  36.1 11.5 %all_to_all.10.refs_0_ = f32[8,32,128]{2,1,0:T(8,128)S(1)} all-to-all(f32[8,32,128]{2,1,0:T(8,128)S(1)} %deconvolve.1), channel_id=1, replica_groups=mesh['tile'=4,'plane'=8] {'plane'}, dimensions={0} | all-to-all | bytes 262144 | tf_op jit(solution)/shard_map/all_to_all | solution.py:229
  47.6 0.8 %unpack.1 = f32[2,1,64,256]{3,2,1,0:T(8,128)} custom-call(f32[8,32,128]{2,1,0:T(8,128)S(1)} %all_to_all.10.refs_0_), custom_call_target="tpu_custom_call" | custom-call | tf_op jit(solution)/shard_map/unpack/pallas_call | solution.py:230
  (1 shorter events, 0.0 us)
Async XLA Ops:
  2.3 1.4 %copy-start.1 = (f32[2,1,32,256]{3,2,1,0:T(8,128)S(1)}, f32[2,1,32,256]{3,2,1,0:T(8,128)}, u32[]{:S(2)}) copy-start(f32[2,1,32,256]{3,2,1,0:T(8,128)} %refs_3_.1) | copy-start | bytes 196612
  2.4 4.6 %collective-permute-start = (f32[2,1,34,256]{3,2,1,0:T(8,128)S(1)}, f32[2,1,34,256]{3,2,1,0:T(8,128)S(1)}, u32[]{:S(2)}, u32[]{:S(2)}) collective-permute-start(f32[2,1,34,256]{3,2,1,0:T(8,128)S(1)} %pad_maximum_fusion.1), channel_id=1, source_target_pairs={{8,0},{16,8},{24,16},{9,1},{17,9},{25,17},{10,2},{18,10},{26,18},{... | collective-permute-start | bytes 208904 | tf_op jit(solution)/shard_map/ppermute | solution.py:197
  3.7 4.2 %copy-start = (f32[2,1,64,256]{3,2,1,0:T(8,128)S(1)}, f32[2,1,64,256]{3,2,1,0:T(8,128)}, u32[]{:S(2)}) copy-start(f32[2,1,64,256]{3,2,1,0:T(8,128)} %refs_2_.2) | copy-start | bytes 393220
  3.8 4.1 %collective-permute-start.1 = (f32[2,1,64,256]{3,2,1,0:T(8,128)S(1)}, f32[2,1,64,256]{3,2,1,0:T(8,128)S(1)}, u32[]{:S(2)}, u32[]{:S(2)}) collective-permute-start(f32[2,1,64,256]{3,2,1,0:T(8,128)S(1)} %pad_maximum_fusion), channel_id=1, source_target_pairs={{0,8},{8,16},{16,24},{1,9},{9,17},{17,25},{2,10},{10,18},{18,26},{... | collective-permute-start | bytes 393224 | tf_op jit(solution)/shard_map/ppermute | solution.py:196
  9.6 21.6 %all-to-all-start = ((f32[8,120,128]{2,1,0:T(8,128)}), f32[8,120,128]{2,1,0:T(8,128)S(1)}, u32[]{:S(2)}, u32[]{:S(2)}) async-start(f32[8,120,128]{2,1,0:T(8,128)} %pack.1), calls=%async_computation | async-start | bytes 983040 | tf_op jit(solution)/shard_map/all_to_all | solution.py:211
  16.8 14.4 %copy-start.3 = (f32[2,15]{1,0:T(2,128)S(1)}, f32[2,15]{1,0:T(2,128)}, u32[]{:S(2)}) copy-start(f32[2,15]{1,0:T(2,128)} %refs_2_.3) | copy-start | bytes 364
  16.8 14.4 %copy-start.2 = (f32[2,41]{1,0:T(2,128)S(1)}, f32[2,41]{1,0:T(2,128)}, u32[]{:S(2)}) copy-start(f32[2,41]{1,0:T(2,128)} %refs_1_.1) | copy-start | bytes 988

commit v2 on v1

--- a/solution.py
+++ b/solution.py
@@ -23,7 +23,23 @@
     return pl.BlockSpec(memory_space=pltpu.SMEM)
 
 
-def pack_kernel(place, following, own, strip, below, above, windows, rows, *, reach, blocks, row_blocks):
+def payload_kernel(facts, own, strip, to_core, to_chip):
+    strip_rows = strip.shape[2]
+    lower = facts[0] == 1
+    numbers = jnp.where(
+        lax.broadcasted_iota(jnp.int32, strip.shape, 3) < LANES,
+        facts[1].astype(jnp.float32),
+        facts[2].astype(jnp.float32),
+    )
+    up = (strip[...], own[:, :, own.shape[2] - strip_rows :, :])
+    down = (own[:, :, :strip_rows, :], numbers)
+    for k in range(2):
+        at = slice(k * strip_rows, (k + 1) * strip_rows)
+        to_core[:, :, at, :] = jnp.where(lower, down[k], up[k])
+        to_chip[:, :, at, :] = jnp.where(lower, up[k], down[k])
+
+
+def pack_kernel(facts, following, own, strip, core, chip, windows, rows, *, reach, blocks, row_blocks):
     chans, _, row_count, voxels = own.shape
     strip_rows = strip.shape[2]
     lane = lax.broadcasted_iota(jnp.int32, (1, LANES), 1)
@@ -31,15 +47,18 @@
     edge = LANES // 4
     block_rows = row_count // row_blocks
     window_rows = block_rows + 2 * reach
+    lower = facts[0] == 1
     for c in range(chans):
-        rows[c, 0:reach, :] = below[c, 0, below.shape[2] - reach :, :]
-        turned = pltpu.roll(below[c, 0, 0:strip_rows, :], place[1], 1)
+        strip_before = jnp.where(lower, core[c, 0, :strip_rows, :], chip[c, 0, :strip_rows, :])
+        rows_before = jnp.where(lower, core[c, 0, strip_rows:, :], chip[c, 0, strip_rows:, :])
+        rows_after = jnp.where(lower, chip[c, 0, :strip_rows, :], core[c, 0, :strip_rows, :])
+        rows[c, 0:reach, :] = rows_before[strip_rows - reach :]
+        turned = pltpu.roll(strip_before, facts[2], 1)
         top = own[c, 0, 0:strip_rows, :]
-        rows[c, reach : reach + strip_rows, :] = jnp.where(tall < place[0], 0.5 * (top + turned), top)
+        rows[c, reach : reach + strip_rows, :] = jnp.where(tall < facts[1], 0.5 * (top + turned), top)
         rows[c, reach + strip_rows : reach + row_count, :] = own[c, 0, strip_rows:, :]
         turned = pltpu.roll(strip[c, 0], following[1], 1)
-        top = above[c, 0, 0:strip_rows, :]
-        after = jnp.where(tall < following[0], 0.5 * (top + turned), top)
+        after = jnp.where(tall < following[0], 0.5 * (rows_after + turned), rows_after)
         rows[c, reach + row_count : row_count + 2 * reach, :] = after[0:reach]
         whole = rows[c, 0 : row_count + 2 * reach, :]
         left, right = whole[:, :LANES], whole[:, LANES:]
@@ -188,16 +207,24 @@
     row_blocks = planes // (chans * blocks)
     out_rows = row_count // row_blocks
     window_rows = out_rows + 2 * reach
-    up = [(i, i + 1) for i in range(tiles - 1)]
-    down = [(i + 1, i) for i in range(tiles - 1)]
-
-    numbers = jnp.concatenate([extents, section_skews])
-    marks = jnp.broadcast_to(numbers.astype(jnp.float32)[None, None, :, None], (chans, 1, 2, voxels))
-    below = lax.ppermute(jnp.concatenate([intersection_strip, observed[:, :, row_count - strip_rows :]], axis=2), "tile", up)
-    above = lax.ppermute(jnp.concatenate([observed[:, :, :strip_rows], marks], axis=2), "tile", down)
-    following = above[0, 0, strip_rows:, 0].astype(jnp.int32)
-    first_tile = lax.axis_index("tile") == 0
-    place = jnp.where(jnp.stack([first_tile, False]), 0, numbers)
+    cores = [(i, i ^ 1) for i in range(tiles)]
+    chips = [pair for i in range(1, tiles - 1, 2) for pair in ((i, i + 1), (i + 1, i))]
+
+    tile = lax.axis_index("tile")
+    facts = jnp.stack([tile % 2, jnp.where(tile == 0, 0, extents[0]), section_skews[0]]).astype(jnp.int32)
+    payload = jax.ShapeDtypeStruct((chans, 1, 2 * strip_rows, voxels), jnp.float32)
+    to_core, to_chip = pl.pallas_call(
+        payload_kernel,
+        out_shape=(payload, payload),
+        in_specs=[in_smem(), in_vmem(), in_vmem()],
+        out_specs=(in_vmem(), in_vmem()),
+        compiler_params=params(),
+        name="payload",
+    )(facts, observed, intersection_strip)
+    core = lax.ppermute(to_core, "tile", cores)
+    chip = lax.ppermute(to_chip, "tile", chips)
+    marks = jnp.where(tile % 2 == 0, core[0, 0, strip_rows, ::LANES], chip[0, 0, strip_rows, ::LANES])
+    following = marks.astype(jnp.int32)
 
     windows = pl.pallas_call(
         lambda *refs: pack_kernel(*refs, reach=reach, blocks=blocks, row_blocks=row_blocks),
@@ -207,7 +234,7 @@
         scratch_shapes=[pltpu.VMEM((chans, row_count + 2 * reach, voxels), jnp.float32)],
         compiler_params=params(),
         name="pack",
-    )(place, following, observed, intersection_strip, below, above)
+    )(facts, following, observed, intersection_strip, core, chip)
     windows = lax.all_to_all(windows, "plane", 0, 0, tiled=True)
 
     channel = (lax.axis_index("plane") // (planes // chans)).astype(jnp.int32).reshape(1)

time: 48.7 us -> 45.6 us (0.936)
  waiting for transfers between devices: 15.1 us -> 10.5 us
  blocking collectives: 11.5 us -> 15.2 us
  starting transfers between devices: 11.7 us -> 8.34 us
  local copies, waits for them, and re-layouts: 0.99 us -> 1.94 us
  Pallas kernels: 7.32 us -> 7.91 us
    all_to_all x1, waiting for transfers between devices: 14.4 us -> 10.2 us  [shards(): windows = lax.all_to_all(windows, 'plane', 0, 0, tiled=True)]
    all_to_all x1, blocking collectives: 11.5 us -> 15.2 us  [shards(): received = lax.all_to_all(result, 'plane', 0, 0, tiled=True)]
    ppermute x2, starting transfers between devices: 4.45 us -> 1.17 us  [the longest x1 0.66 us: shards(): chip = lax.ppermute(to_chip, 'tile', chips)]
    unnamed x8 -> x12, local copies, waits for them, and re-layouts: 0.02 us -> 1.76 us
    slice x1 -> x2, local copies, waits for them, and re-layouts: 0.89 us -> 0.17 us  [the longest x1 0.09 us: shards(): core[0, 0, strip_rows, ::LANES]]
    pallas_call x0 -> x1, Pallas kernels: none -> 0.56 us  [shards(): pl.pallas_call(payload_kernel, out_shape=(payload, payload), in_specs=[in...]
where the time goes in v2:
time: 45.6 us; the launch traced here: 45.3 us
  blocking collectives  15.2 us (33%)
  waiting for transfers between devices  10.5 us (23%)
  starting transfers between devices  8.34 us (18%)
  Pallas kernels  7.91 us (17%)
  local copies, waits for them, and re-layouts  1.94 us (4%)
  between operations  1.36 us (3%)
    all_to_all x1, blocking collectives, shards(): received = lax.all_to_all(result, 'plane', 0, 0, tiled=True)  15.2 us
    all_to_all x1, waiting for transfers between devices, shards(): windows = lax.all_to_all(windows, 'plane', 0, 0, tiled=True)  10.2 us
    all_to_all x1, starting transfers between devices, shards(): windows = lax.all_to_all(windows, 'plane', 0, 0, tiled=True)  7.16 us
    pallas_call x1, Pallas kernels, shards(): pl.pallas_call(lambda *refs: deconvolve_kernel(*refs, reach=reach, out_ro...  4.9 us
    unnamed x12, local copies, waits for them, and re-layouts  1.76 us
    pallas_call x1, Pallas kernels, shards(): pl.pallas_call(lambda *refs: pack_kernel(*refs, reach=reach, blocks=block...  1.68 us
  transfers between devices with their start and end apart: 3, of which 2 were waited for; matrix products, arithmetic and copies ran while one was open for 0% of the time, Pallas kernels for 0%

profile of v2, /device:TPU:0, one launch (start us, length us, event | category | flops | bytes accessed | tf_op | source)
XLA Modules:
  0.0 45.3 jit_solution(16965866696982555826)
XLA Ops:
  1.3 0.1 pad_add_fusion.facts.refs_0_
  1.4 0.0 copy-start
  1.4 0.9 %copy-done = f32[2,1,64,256]{3,2,1,0:T(8,128)S(1)} copy-done((f32[2,1,64,256]{3,2,1,0:T(8,128)S(1)}, f32[2,1,64,256]{3,2,1,0:T(8,128)}, u32[]{:S(2)}) %copy-start) | copy-done | bytes 131096
  2.3 0.0 copy-start.2
  2.3 0.8 %copy-done.2 = f32[2,1,32,256]{3,2,1,0:T(8,128)S(1)} copy-done((f32[2,1,32,256]{3,2,1,0:T(8,128)S(1)}, f32[2,1,32,256]{3,2,1,0:T(8,128)}, u32[]{:S(2)}) %copy-start.2) | copy-done | bytes 65560
  3.1 0.0 copy-start.1
  3.1 0.0 copy-start.3
  3.1 0.6 %payload.1 = (f32[2,1,64,256]{3,2,1,0:T(8,128)S(1)}, f32[2,1,64,256]{3,2,1,0:T(8,128)S(1)}) custom-call(s32[3]{0:T(128)S(1)} %pad_add_fusion.facts.refs_0_, f32[2,1,64,256]{3,2,1,0:T(8,128)S(1)} %copy-done, f32[2,1,32,256]{3,2,1,0:T(8,128)S(1)} %copy-done.2), custom_call_target="tpu_custom_call" | custom-call | tf_op jit(solution)/shard_map/payload/pallas_call | solution.py:216
  3.7 0.5 %collective-permute-start = (f32[2,1,64,256]{3,2,1,0:T(8,128)S(1)}, f32[2,1,64,256]{3,2,1,0:T(8,128)S(1)}, u32[]{:S(2)}, u32[]{:S(2)}) collective-permute-start(f32[2,1,64,256]{3,2,1,0:T(8,128)S(1)} %get-tuple-element.7), channel_id=1, source_target_pairs={{0,8},{8,0},{16,24},{24,16},{1,9},{9,1},{17,25},{25,17},{2,10},{10... | collective-permute-start | bytes 393224 | tf_op jit(solution)/shard_map/ppermute | solution.py:224
  4.2 0.7 %collective-permute-start.1 = (f32[2,1,64,256]{3,2,1,0:T(8,128)S(1)}, f32[2,1,64,256]{3,2,1,0:T(8,128)S(1)}, u32[]{:S(2)}, u32[]{:S(2)}) collective-permute-start(f32[2,1,64,256]{3,2,1,0:T(8,128)S(1)} %get-tuple-element.8), channel_id=1, source_target_pairs={{8,16},{16,8},{9,17},{17,9},{10,18},{18,10},{11,19},{19,11},{12,20... | collective-permute-start | bytes 393224 | tf_op jit(solution)/shard_map/ppermute | solution.py:225
  4.9 0.3 collective-permute-done.refs_4_
  5.2 0.1 slice.6
  5.3 0.0 collective-permute-done.1.refs_5_
  5.3 0.1 slice.7
  5.4 0.0 copy-done.1
  5.4 0.0 copy-done.3
  5.4 1.7 %pack.1 = f32[8,120,128]{2,1,0:T(8,128)} custom-call(s32[3]{0:T(128)S(1)} %pad_add_fusion.facts.refs_0_, s32[2]{0:T(128)S(1)} %fusion.1.refs_1_, f32[2,1,64,256]{3,2,1,0:T(8,128)S(1)} %copy-done.1, f32[2,1,32,256]{3,2,1,0:T(8,128)S(1)} %copy-done.3, f32[2,1,64,256]{3,2,1,0:T(8,128)S(1)} %collective-permute-done.refs_4_, ...), custom_call_target="tpu_custom_call" | custom-call | tf_op jit(solution)/shard_map/pack/pallas_call | solution.py:229
  7.1 7.2 %all-to-all-start = ((f32[8,120,128]{2,1,0:T(8,128)}), f32[8,120,128]{2,1,0:T(8,128)S(1)}, u32[]{:S(2)}, u32[]{:S(2)}) async-start(f32[8,120,128]{2,1,0:T(8,128)} %pack.1), calls=%async_computation | async-start | bytes 983040 | tf_op jit(solution)/shard_map/all_to_all | solution.py:238
  14.2 0.0 copy-start.5
  14.3 0.0 copy-start.4
  14.3 10.2 %all-to-all-done.refs_3_ = f32[8,120,128]{2,1,0:T(8,128)S(1)} async-done(((f32[8,120,128]{2,1,0:T(8,128)}), f32[8,120,128]{2,1,0:T(8,128)S(1)}, u32[]{:S(2)}, u32[]{:S(2)}) %all-to-all-start) | async-done | bytes 491552 | tf_op jit(solution)/shard_map/all_to_all | solution.py:238
  24.4 0.0 copy-done.5
  24.4 0.0 copy-done.4
  24.4 4.9 %deconvolve.1 = f32[8,32,128]{2,1,0:T(8,128)S(1)} custom-call(s32[1]{0:T(128)} %bitcast.refs_0_, f32[2,41]{1,0:T(2,128)S(1)} %copy-done.4, f32[2,15]{1,0:T(2,128)S(1)} %copy-done.5, f32[8,120,128]{2,1,0:T(8,128)S(1)} %all-to-all-done.refs_3_), custom_call_target="tpu_custom_call" | custom-call | tf_op jit(solution)/shard_map/deconvolve/pallas_call | solution.py:242
  29.3 15.2 %all_to_all.10.refs_0_ = f32[8,32,128]{2,1,0:T(8,128)S(1)} all-to-all(f32[8,32,128]{2,1,0:T(8,128)S(1)} %deconvolve.1), channel_id=1, replica_groups=mesh['tile'=4,'plane'=8] {'plane'}, dimensions={0} | all-to-all | bytes 262144 | tf_op jit(solution)/shard_map/all_to_all | solution.py:256
  44.5 0.8 %unpack.1 = f32[2,1,64,256]{3,2,1,0:T(8,128)} custom-call(f32[8,32,128]{2,1,0:T(8,128)S(1)} %all_to_all.10.refs_0_), custom_call_target="tpu_custom_call" | custom-call | tf_op jit(solution)/shard_map/unpack/pallas_call | solution.py:257
  (1 shorter events, 0.0 us)
Async XLA Ops:
  1.4 0.9 %copy-start = (f32[2,1,64,256]{3,2,1,0:T(8,128)S(1)}, f32[2,1,64,256]{3,2,1,0:T(8,128)}, u32[]{:S(2)}) copy-start(f32[2,1,64,256]{3,2,1,0:T(8,128)} %refs_2_.2) | copy-start | bytes 393220
  2.3 0.8 %copy-start.2 = (f32[2,1,32,256]{3,2,1,0:T(8,128)S(1)}, f32[2,1,32,256]{3,2,1,0:T(8,128)}, u32[]{:S(2)}) copy-start(f32[2,1,32,256]{3,2,1,0:T(8,128)} %refs_3_.1) | copy-start | bytes 196612
  3.1 2.3 %copy-start.1 = (f32[2,1,64,256]{3,2,1,0:T(8,128)S(1)}, f32[2,1,64,256]{3,2,1,0:T(8,128)}, u32[]{:S(2)}) copy-start(f32[2,1,64,256]{3,2,1,0:T(8,128)} %refs_2_.2) | copy-start | bytes 393220
  3.1 2.3 %copy-start.3 = (f32[2,1,32,256]{3,2,1,0:T(8,128)S(1)}, f32[2,1,32,256]{3,2,1,0:T(8,128)}, u32[]{:S(2)}) copy-start(f32[2,1,32,256]{3,2,1,0:T(8,128)} %refs_3_.1) | copy-start | bytes 196612
  3.7 1.5 %collective-permute-start = (f32[2,1,64,256]{3,2,1,0:T(8,128)S(1)}, f32[2,1,64,256]{3,2,1,0:T(8,128)S(1)}, u32[]{:S(2)}, u32[]{:S(2)}) collective-permute-start(f32[2,1,64,256]{3,2,1,0:T(8,128)S(1)} %get-tuple-element.7), channel_id=1, source_target_pairs={{0,8},{8,0},{16,24},{24,16},{1,9},{9,1},{17,25},{25,17},{2,10},{10... | collective-permute-start | bytes 393224 | tf_op jit(solution)/shard_map/ppermute | solution.py:224
  4.2 1.1 %collective-permute-start.1 = (f32[2,1,64,256]{3,2,1,0:T(8,128)S(1)}, f32[2,1,64,256]{3,2,1,0:T(8,128)S(1)}, u32[]{:S(2)}, u32[]{:S(2)}) collective-permute-start(f32[2,1,64,256]{3,2,1,0:T(8,128)S(1)} %get-tuple-element.8), channel_id=1, source_target_pairs={{8,16},{16,8},{9,17},{17,9},{10,18},{18,10},{11,19},{19,11},{12,20... | collective-permute-start | bytes 393224 | tf_op jit(solution)/shard_map/ppermute | solution.py:225
  7.1 17.3 %all-to-all-start = ((f32[8,120,128]{2,1,0:T(8,128)}), f32[8,120,128]{2,1,0:T(8,128)S(1)}, u32[]{:S(2)}, u32[]{:S(2)}) async-start(f32[8,120,128]{2,1,0:T(8,128)} %pack.1), calls=%async_computation | async-start | bytes 983040 | tf_op jit(solution)/shard_map/all_to_all | solution.py:238
  14.2 10.2 %copy-start.5 = (f32[2,15]{1,0:T(2,128)S(1)}, f32[2,15]{1,0:T(2,128)}, u32[]{:S(2)}) copy-start(f32[2,15]{1,0:T(2,128)} %refs_2_.3) | copy-start | bytes 364
  14.3 10.2 %copy-start.4 = (f32[2,41]{1,0:T(2,128)S(1)}, f32[2,41]{1,0:T(2,128)}, u32[]{:S(2)}) copy-start(f32[2,41]{1,0:T(2,128)} %refs_1_.1) | copy-start | bytes 988

commit v3 on v2

v3 whole, which is shorter than its diff:
```python
import jax
import jax.numpy as jnp
from jax import lax
from jax.experimental import pallas as pl
from jax.experimental.pallas import tpu as pltpu
from jax.sharding import PartitionSpec as P

ITERS = 2
LANES = 128
GROUP = 8
VMEM_LIMIT = 48 * 1024 * 1024


def params():
    return pltpu.CompilerParams(vmem_limit_bytes=VMEM_LIMIT)


def in_vmem():
    return pl.BlockSpec(memory_space=pltpu.VMEM)


def in_smem():
    return pl.BlockSpec(memory_space=pltpu.SMEM)


def payload_kernel(facts, own, strip, to_core, to_chip, sems):
    strip_rows = strip.shape[2]
    low, high = slice(0, strip_rows), slice(strip_rows, 2 * strip_rows)

    def fill(up, down):
        copies = []
        for c in range(strip.shape[0]):
            pieces = (
                (strip.at[c], up.at[c, :, low, :]),
                (own.at[c, :, own.shape[2] - strip_rows :, :], up.at[c, :, high, :]),
                (own.at[c, :, low, :], down.at[c, :, low, :]),
            )
            for source, target in pieces:
                copies.append(pltpu.make_async_copy(source, target, sems.at[len(copies)]))
        for copy in copies:
            copy.start()
        column = lax.broadcasted_iota(jnp.int32, strip.shape, 3)
        down[:, :, high, :] = jnp.where(column < LANES, facts[1], facts[2]).astype(jnp.float32)
        for copy in copies:
            copy.wait()

    @pl.when(facts[0] == 1)
    def _():
        fill(to_chip, to_core)

    @pl.when(facts[0] == 0)
    def _():
        fill(to_core, to_chip)


def pack_kernel(facts, to_core, to_chip, core, chip, windows, rows, *, reach, blocks, row_blocks):
    chans, _, row_count, voxels = core.shape
    strip_rows = row_count // 2
    lane = lax.broadcasted_iota(jnp.int32, (1, LANES), 1)
    tall = lax.broadcasted_iota(jnp.int32, (strip_rows, voxels), 0)
    edge = LANES // 4
    block_rows = row_count // row_blocks
    window_rows = block_rows + 2 * reach
    lower = facts[0] == 1

    def pick(low, high, c, part):
        at = slice(part * strip_rows, (part + 1) * strip_rows)
        return jnp.where(lower, low[c, 0, at, :], high[c, 0, at, :])

    numbers = pick(chip, core, 0, 1)[0:GROUP].astype(jnp.int32)
    next_extent, next_skew = jnp.max(numbers[:, :LANES]), jnp.max(numbers[:, LANES:])
    for c in range(chans):
        rows[c, 0:reach, :] = pick(core, chip, c, 1)[strip_rows - reach :]
        turned = pltpu.roll(pick(core, chip, c, 0), facts[2], 1)
        top = pick(to_core, to_chip, c, 0)
        rows[c, reach : reach + strip_rows, :] = jnp.where(tall < facts[1], 0.5 * (top + turned), top)
        rows[c, reach + strip_rows : reach + row_count, :] = pick(to_chip, to_core, c, 1)
        turned = pltpu.roll(pick(to_chip, to_core, c, 0), next_skew, 1)
        top = pick(chip, core, c, 0)
        after = jnp.where(tall < next_extent, 0.5 * (top + turned), top)
        rows[c, reach + row_count : row_count + 2 * reach, :] = after[0:reach]
        whole = rows[c, 0 : row_count + 2 * reach, :]
        left, right = whole[:, :LANES], whole[:, LANES:]
        left_up, left_down = pltpu.roll(left, edge, 1), pltpu.roll(left, LANES - edge, 1)
        right_up, right_down = pltpu.roll(right, edge, 1), pltpu.roll(right, LANES - edge, 1)
        low, high = lane < edge, lane < LANES - edge
        cut = (
            jnp.where(low, 0.0, left_up),
            jnp.where(high, left_down, right_down),
            jnp.where(low, left_up, right_up),
            jnp.where(high, right_down, 0.0),
        )
        for b in range(row_blocks):
            for j in range(blocks):
                start = b * block_rows
                windows[(c * row_blocks + b) * blocks + j] = cut[j][start : start + window_rows]


def split(value):
    high = value.astype(jnp.bfloat16)
    low = (value - high.astype(jnp.float32)).astype(jnp.bfloat16)
    return high, low


def stages(window_rows, lateral_half):
    def tiled(rows):
        return -(-rows // 16) * 16

    return [
        (tiled(window_rows - 2 * k * lateral_half), tiled(window_rows - 2 * (k + 1) * lateral_half))
        for k in range(2 * ITERS)
    ]


def bands_kernel(chan, axial, lateral, along_z, along_x, *along_y, spans):
    width = lateral.shape[1]
    taps = [lateral[chan[0], j] for j in range(width)]
    for j in range(axial.shape[1]):
        along_z[j] = jnp.full((GROUP, LANES), axial[chan[0], j], jnp.float32)
    offset = lax.broadcasted_iota(jnp.int32, (LANES, LANES), 0) - lax.broadcasted_iota(jnp.int32, (LANES, LANES), 1)

    def band(order, where, first):
        total = jnp.zeros((LANES, LANES), jnp.float32)
        for j in range(width):
            total = jnp.where(where == j + first, order[j], total)
        return split(total)

    for which in range(2):
        order = taps if which == 0 else taps[::-1]
        high, low = band(order, offset, -(width // 2))
        along_x[which, :LANES, :LANES] = high
        along_x[which, :LANES, LANES:] = low
        along_x[which, LANES:, :LANES] = high
        along_x[which, LANES:, LANES:] = jnp.zeros_like(low)
        high, low = band(order, -offset, 0)
        for k in range(which, len(spans), 2):
            read, written = spans[k]
            top, bottom = high[:written, :read], low[:written, :read]
            along_y[k][:written] = jnp.concatenate([top, top], axis=1)
            along_y[k][written:] = jnp.concatenate([bottom, jnp.zeros_like(bottom)], axis=1)


def deconvolve_kernel(windows, axial, x_bands, *refs, spans, lateral_half, out_rows):
    y_bands, (result, blurred, estimate) = refs[: len(spans)], refs[len(spans) :]
    planes, window_rows, _ = windows.shape
    axial_half = axial.shape[0] // 2
    columns = [slice(q * LANES, (q + 1) * LANES) for q in range(planes)]

    def along_x(values, which):
        out = []
        for q in range(0, planes, 2):
            pair = jnp.concatenate(values[q : q + 2], axis=0)
            product = jnp.dot(jnp.concatenate(split(pair), axis=1), x_bands[which], preferred_element_type=jnp.float32)
            product = product[:, :LANES] + product[:, LANES:]
            out += [product[: pair.shape[0] // 2], product[pair.shape[0] // 2 :]]
        return out

    def along_y(k):
        read, written = spans[k]
        for q in range(0, planes, 2):
            pair = slice(q * LANES, (q + 2) * LANES)
            both = jnp.concatenate(split(blurred[0:read, pair]), axis=0)
            product = jnp.dot(y_bands[k][...], both, preferred_element_type=jnp.float32)
            blurred[0:written, pair] = product[:written] + product[written:]

    def along_z(values, flipped):
        out = []
        for p in range(planes):
            total = None
            for q in range(planes):
                at = (p - q if flipped else q - p) + axial_half
                if 0 <= at < 2 * axial_half + 1:
                    term = axial[at] * values[q]
                    total = term if total is None else total + term
            out.append(total)
        return out

    origin = 0
    for sweep in range(ITERS):
        read, written = spans[2 * sweep]
        if sweep == 0:
            values = along_x([windows[p] for p in range(planes)], 0)
            blurred[window_rows:read, :] = jnp.zeros((read - window_rows, planes * LANES), jnp.float32)
        else:
            values = along_x([estimate[0:read, columns[p]] for p in range(planes)], 0)
        for p in range(planes):
            blurred[0 : values[p].shape[0], columns[p]] = values[p]
        along_y(2 * sweep)
        origin += lateral_half
        for row in range(0, written, GROUP):
            at = slice(row, row + GROUP)
            mixed = along_z([blurred[at, columns[q]] for q in range(planes)], False)
            quotient = []
            for p in range(planes):
                joined = windows[p, row + origin : row + origin + GROUP, :]
                quotient.append(joined / jnp.where(joined > 0.0, mixed[p], 1.0))
            back = along_z(quotient, True)
            for p in range(planes):
                blurred[at, columns[p]] = back[p]
        read, written = spans[2 * sweep + 1]
        along_y(2 * sweep + 1)
        origin += lateral_half
        factor = along_x([blurred[0:written, columns[p]] for p in range(planes)], 1)
        for p in range(planes):
            if sweep == 0:
                before = windows[p, origin : origin + written, :]
            else:
                before = estimate[2 * lateral_half : 2 * lateral_half + written, columns[p]]
            estimate[0:written, columns[p]] = before * factor[p]
    half = out_rows // 2
    side = (LANES - LANES // 2) // 2
    lane = lax.broadcasted_iota(jnp.int32, (1, LANES), 1)
    for p in range(planes):
        first = pltpu.roll(estimate[0:half, columns[p]], LANES - side, 1)
        second = pltpu.roll(estimate[half:out_rows, columns[p]], side, 1)
        result[p] = jnp.where(lane < LANES // 2, first, second)


def unpack_kernel(received, out, *, blocks, row_blocks):
    chans, _, row_count, voxels = out.shape
    half = received.shape[1]
    lane = lax.broadcasted_iota(jnp.int32, (1, LANES), 1)
    for c in range(chans):
        for b in range(row_blocks):
            for pair in range(blocks // 2):
                at = (c * row_blocks + b) * blocks + 2 * pair
                even, odd = received[at], received[at + 1]
                row = b * 2 * half
                columns = slice(pair * LANES, (pair + 1) * LANES)
                out[c, 0, row : row + half, columns] = jnp.where(lane < LANES // 2, even, pltpu.roll(odd, LANES // 2, 1))
                out[c, 0, row + half : row + 2 * half, columns] = jnp.where(lane < LANES // 2, pltpu.roll(even, LANES // 2, 1), odd)


def shards(observed, intersection_strip, axial_taps, lateral_taps, extents, section_skews):
    chans, _, row_count, voxels = observed.shape
    strip_rows = intersection_strip.shape[2]
    planes = lax.axis_size("plane")
    tiles = lax.axis_size("tile")
    lateral_half = lateral_taps.shape[1] // 2
    reach = 2 * ITERS * lateral_half
    blocks = voxels // (LANES // 2)
    row_blocks = planes // (chans * blocks)
    out_rows = row_count // row_blocks
    window_rows = out_rows + 2 * reach
    cores = [(i, i ^ 1) for i in range(tiles)]
    chips = [pair for i in range(1, tiles - 1, 2) for pair in ((i, i + 1), (i + 1, i))]

    tile = lax.axis_index("tile")
    facts = jnp.stack([tile % 2, jnp.where(tile == 0, 0, extents[0]), section_skews[0]]).astype(jnp.int32)
    payload = jax.ShapeDtypeStruct((chans, 1, 2 * strip_rows, voxels), jnp.float32)
    to_core, to_chip = pl.pallas_call(
        payload_kernel,
        out_shape=(payload, payload),
        in_specs=[in_smem(), pl.BlockSpec(memory_space=pltpu.HBM), pl.BlockSpec(memory_space=pltpu.HBM)],
        out_specs=(in_vmem(), in_vmem()),
        scratch_shapes=[pltpu.SemaphoreType.DMA((3 * chans,))],
        compiler_params=params(),
        name="payload",
    )(facts, pltpu.with_memory_space_constraint(observed, pltpu.HBM), pltpu.with_memory_space_constraint(intersection_strip, pltpu.HBM))
    chip = lax.ppermute(to_chip, "tile", chips)
    core = lax.ppermute(to_core, "tile", cores)
    windows = pl.pallas_call(
        lambda *refs: pack_kernel(*refs, reach=reach, blocks=blocks, row_blocks=row_blocks),
        out_shape=jax.ShapeDtypeStruct((planes, window_rows, LANES), jnp.float32),
        in_specs=[in_smem()] + [in_vmem()] * 4,
        out_specs=in_vmem(),
        scratch_shapes=[pltpu.VMEM((chans, row_count + 2 * reach, voxels), jnp.float32)],
        compiler_params=params(),
        name="pack",
    )(facts, to_core, to_chip, core, chip)
    windows = lax.all_to_all(windows, "plane", 0, 0, tiled=True)

    channel = (lax.axis_index("plane") // (planes // chans)).astype(jnp.int32).reshape(1)
    spans = stages(window_rows, lateral_half)
    bands = pl.pallas_call(
        lambda *refs: bands_kernel(*refs, spans=spans),
        out_shape=[
            jax.ShapeDtypeStruct((axial_taps.shape[1], GROUP, LANES), jnp.float32),
            jax.ShapeDtypeStruct((2, 2 * LANES, 2 * LANES), jnp.bfloat16),
        ]
        + [jax.ShapeDtypeStruct((2 * written, 2 * read), jnp.bfloat16) for read, written in spans],
        in_specs=[in_smem()] * 3,
        out_specs=[in_vmem()] * (2 + len(spans)),
        cost_estimate=pl.CostEstimate(flops=1 << 20, bytes_accessed=1 << 20, transcendentals=0),
        compiler_params=params(),
        name="bands",
    )(channel, axial_taps, lateral_taps)
    result = pl.pallas_call(
        lambda *refs: deconvolve_kernel(*refs, spans=spans, lateral_half=lateral_half, out_rows=out_rows),
        out_shape=jax.ShapeDtypeStruct((planes, out_rows // 2, LANES), jnp.float32),
        in_specs=[in_vmem()] * (3 + len(spans)),
        out_specs=in_vmem(),
        scratch_shapes=[
            pltpu.VMEM((spans[0][0], planes * LANES), jnp.float32),
            pltpu.VMEM((spans[1][1], planes * LANES), jnp.float32),
        ],
        compiler_params=params(),
        name="deconvolve",
    )(windows, *bands)
    received = lax.all_to_all(result, "plane", 0, 0, tiled=True)
    return pl.pallas_call(
        lambda *refs: unpack_kernel(*refs, blocks=blocks, row_blocks=row_blocks),
        out_shape=jax.ShapeDtypeStruct(observed.shape, jnp.float32),
        in_specs=[in_vmem()],
        out_specs=in_vmem(),
        compiler_params=params(),
        name="unpack",
    )(received)


def solution(mesh):
    in_specs = (
        P(None, "plane", "tile", None),
        P(None, "plane", "tile", None),
        P(),
        P(),
        P("tile"),
        P("tile"),
    )
    out_specs = P(None, "plane", "tile", None)
    return jax.shard_map(shards, mesh=mesh, in_specs=in_specs, out_specs=out_specs, check_vma=False)
```

time: 45.6 us -> 42 us (0.921)
  waiting for transfers between devices: 10.5 us -> 8.94 us
  local copies, waits for them, and re-layouts: 1.94 us -> 0.68 us
  Pallas kernels: 7.91 us -> 7.24 us
    pallas_call x1 -> x2, Pallas kernels: 4.9 us -> 3.27 us  [the longest x1 2.42 us: shards(): pl.pallas_call(lambda *refs: deconvolve_kernel(*refs, spans=spans, latera...]
    all_to_all x1, waiting for transfers between devices: 10.2 us -> 8.62 us  [shards(): windows = lax.all_to_all(windows, 'plane', 0, 0, tiled=True)]
    unnamed x12 -> x4, local copies, waits for them, and re-layouts: 1.76 us -> 0.68 us
    pallas_call x1, Pallas kernels: 0.56 us -> 1.45 us  [shards(): pl.pallas_call(payload_kernel, out_shape=(payload, payload), in_specs=[in...]
  transfers between devices with their start and end apart: 3 -> 3, of which waited for: 2 -> 2; matrix products, arithmetic and copies ran while one was open for 0% -> 0% of each run, Pallas kernels for 0% -> 2%
where the time goes in v3:
time: 42 us; the launch traced here: 41.6 us
  blocking collectives  15 us (36%)
  waiting for transfers between devices  8.94 us (21%)
  starting transfers between devices  8.34 us (20%)
  Pallas kernels  7.24 us (17%)
  between operations  1.36 us (3%)
  local copies, waits for them, and re-layouts  0.68 us (2%)
    all_to_all x1, blocking collectives, shards(): received = lax.all_to_all(result, 'plane', 0, 0, tiled=True)  15 us
    all_to_all x1, waiting for transfers between devices, shards(): windows = lax.all_to_all(windows, 'plane', 0, 0, tiled=True)  8.62 us
    all_to_all x1, starting transfers between devices, shards(): windows = lax.all_to_all(windows, 'plane', 0, 0, tiled=True)  7.17 us
    pallas_call x1, Pallas kernels, shards(): pl.pallas_call(lambda *refs: deconvolve_kernel(*refs, spans=spans, latera...  2.42 us
    pallas_call x1, Pallas kernels, shards(): pl.pallas_call(lambda *refs: pack_kernel(*refs, reach=reach, blocks=block...  1.77 us
    pallas_call x1, Pallas kernels, shards(): pl.pallas_call(payload_kernel, out_shape=(payload, payload), in_specs=[in...  1.45 us
    pallas_call x1, Pallas kernels, shards(): pl.pallas_call(lambda *refs: bands_kernel(*refs, spans=spans), out_shape=...  0.86 us
  transfers between devices with their start and end apart: 3, of which 2 were waited for; matrix products, arithmetic and copies ran while one was open for 0% of the time, Pallas kernels for 2%

profile of v3, /device:TPU:0, one launch (start us, length us, event | category | flops | bytes accessed | tf_op | source)
XLA Modules:
  0.0 41.6 jit_solution(9543071052400549489)
XLA Ops:
  1.3 0.1 pad_add_fusion.facts.refs_0_
  1.4 1.4 %payload.1 = (f32[2,1,64,256]{3,2,1,0:T(8,128)S(1)}, f32[2,1,64,256]{3,2,1,0:T(8,128)S(1)}) custom-call(s32[3]{0:T(128)S(1)} %pad_add_fusion.facts.refs_0_, f32[2,1,64,256]{3,2,1,0:T(8,128)} %own.1, f32[2,1,32,256]{3,2,1,0:T(8,128)} %strip.1), custom_call_target="tpu_custom_call" | custom-call | tf_op jit(solution)/shard_map/payload/pallas_call | solution.py:251
  2.8 0.5 %collective-permute-start = (f32[2,1,64,256]{3,2,1,0:T(8,128)S(1)}, f32[2,1,64,256]{3,2,1,0:T(8,128)S(1)}, u32[]{:S(2)}, u32[]{:S(2)}) collective-permute-start(f32[2,1,64,256]{3,2,1,0:T(8,128)S(1)} %get-tuple-element.13.refs_1_), channel_id=1, source_target_pairs={{0,8},{8,0},{16,24},{24,16},{1,9},{9,1},{17,25},{25,17},{2,10},{10... | collective-permute-start | bytes 393224 | tf_op jit(solution)/shard_map/ppermute | solution.py:261
  3.3 0.7 %collective-permute-start.1 = (f32[2,1,64,256]{3,2,1,0:T(8,128)S(1)}, f32[2,1,64,256]{3,2,1,0:T(8,128)S(1)}, u32[]{:S(2)}, u32[]{:S(2)}) collective-permute-start(f32[2,1,64,256]{3,2,1,0:T(8,128)S(1)} %get-tuple-element.14.refs_2_), channel_id=1, source_target_pairs={{8,16},{16,8},{9,17},{17,9},{10,18},{18,10},{11,19},{19,11},{12,20... | collective-permute-start | bytes 393224 | tf_op jit(solution)/shard_map/ppermute | solution.py:260
  4.0 0.3 collective-permute-done.refs_3_
  4.3 0.0 collective-permute-done.1.refs_4_
  4.3 1.8 %pack.1 = f32[8,120,128]{2,1,0:T(8,128)} custom-call(s32[3]{0:T(128)S(1)} %pad_add_fusion.facts.refs_0_, f32[2,1,64,256]{3,2,1,0:T(8,128)S(1)} %get-tuple-element.13.refs_1_, f32[2,1,64,256]{3,2,1,0:T(8,128)S(1)} %get-tuple-element.14.refs_2_, f32[2,1,64,256]{3,2,1,0:T(8,128)S(1)} %collective-permute-done.refs_3_, ...), custom_call_target="tpu_custom_call" | custom-call | tf_op jit(solution)/shard_map/pack/pallas_call | solution.py:262
  6.1 7.2 %all-to-all-start = ((f32[8,120,128]{2,1,0:T(8,128)}), f32[8,120,128]{2,1,0:T(8,128)S(1)}, u32[]{:S(2)}, u32[]{:S(2)}) async-start(f32[8,120,128]{2,1,0:T(8,128)} %pack.1), calls=%async_computation | async-start | bytes 983040 | tf_op jit(solution)/shard_map/all_to_all | solution.py:271
  13.3 0.0 copy-start.1
  13.3 0.0 copy-start
  13.3 0.7 %copy-done.1 = f32[2,15]{1,0:T(2,128)S(1)} copy-done((f32[2,15]{1,0:T(2,128)S(1)}, f32[2,15]{1,0:T(2,128)}, u32[]{:S(2)}) %copy-start.1) | copy-done | bytes 144
  13.9 0.0 copy-done
  14.0 0.9 %bands.1 = (f32[41,8,128]{2,1,0:T(8,128)S(1)}, bf16[2,256,256]{2,1,0:T(8,128)(2,1)S(1)}, bf16[224,256]{1,0:T(8,128)(2,1)S(1)}, bf16[192,224]{1,0:T(8,128)(2,1)S(...) custom-call(s32[1]{0:T(128)} %bitcast.3.refs_0_, f32[2,41]{1,0:T(2,128)S(1)} %copy-done, f32[2,15]{1,0:T(2,128)S(1)} %copy-done.1), custom_call_target="tpu_custom_call" | custom-call | flops 1048576 | bytes 1048576 | tf_op jit(solution)/shard_map/bands/pallas_call | solution.py:275
  14.8 8.6 %all-to-all-done.refs_0_ = f32[8,120,128]{2,1,0:T(8,128)S(1)} async-done(((f32[8,120,128]{2,1,0:T(8,128)}), f32[8,120,128]{2,1,0:T(8,128)S(1)}, u32[]{:S(2)}, u32[]{:S(2)}) %all-to-all-start) | async-done | bytes 491552 | tf_op jit(solution)/shard_map/all_to_all | solution.py:271
  23.4 2.4 %deconvolve.1 = f32[8,32,128]{2,1,0:T(8,128)S(1)} custom-call(f32[8,120,128]{2,1,0:T(8,128)S(1)} %all-to-all-done.refs_0_, f32[41,8,128]{2,1,0:T(8,128)S(1)} %get-tuple-element.15.refs_1_, bf16[2,256,256]{2,1,0:T(8,128)(2,1)S(1)} %get-tuple-element.16.refs_2_, bf16[224,256]{1,0:T(8,128)(2,1)S(1)} %get-tuple-element.17.refs_3_, ...), custom_call_target="tpu_custom_call" | custom-call | tf_op jit(solution)/shard_map/deconvolve/pallas_call | solution.py:288
  25.9 15.0 %all_to_all.10.refs_0_ = f32[8,32,128]{2,1,0:T(8,128)S(1)} all-to-all(f32[8,32,128]{2,1,0:T(8,128)S(1)} %deconvolve.1), channel_id=1, replica_groups=mesh['tile'=4,'plane'=8] {'plane'}, dimensions={0} | all-to-all | bytes 262144 | tf_op jit(solution)/shard_map/all_to_all | solution.py:300
  40.9 0.8 %unpack.1 = f32[2,1,64,256]{3,2,1,0:T(8,128)} custom-call(f32[8,32,128]{2,1,0:T(8,128)S(1)} %all_to_all.10.refs_0_), custom_call_target="tpu_custom_call" | custom-call | tf_op jit(solution)/shard_map/unpack/pallas_call | solution.py:301
Async XLA Ops:
  2.8 1.5 %collective-permute-start = (f32[2,1,64,256]{3,2,1,0:T(8,128)S(1)}, f32[2,1,64,256]{3,2,1,0:T(8,128)S(1)}, u32[]{:S(2)}, u32[]{:S(2)}) collective-permute-start(f32[2,1,64,256]{3,2,1,0:T(8,128)S(1)} %get-tuple-element.13.refs_1_), channel_id=1, source_target_pairs={{0,8},{8,0},{16,24},{24,16},{1,9},{9,1},{17,25},{25,17},{2,10},{10... | collective-permute-start | bytes 393224 | tf_op jit(solution)/shard_map/ppermute | solution.py:261
  3.3 1.0 %collective-permute-start.1 = (f32[2,1,64,256]{3,2,1,0:T(8,128)S(1)}, f32[2,1,64,256]{3,2,1,0:T(8,128)S(1)}, u32[]{:S(2)}, u32[]{:S(2)}) collective-permute-start(f32[2,1,64,256]{3,2,1,0:T(8,128)S(1)} %get-tuple-element.14.refs_2_), channel_id=1, source_target_pairs={{8,16},{16,8},{9,17},{17,9},{10,18},{18,10},{11,19},{19,11},{12,20... | collective-permute-start | bytes 393224 | tf_op jit(solution)/shard_map/ppermute | solution.py:260
  6.1 17.4 %all-to-all-start = ((f32[8,120,128]{2,1,0:T(8,128)}), f32[8,120,128]{2,1,0:T(8,128)S(1)}, u32[]{:S(2)}, u32[]{:S(2)}) async-start(f32[8,120,128]{2,1,0:T(8,128)} %pack.1), calls=%async_computation | async-start | bytes 983040 | tf_op jit(solution)/shard_map/all_to_all | solution.py:271
  13.3 0.7 %copy-start.1 = (f32[2,15]{1,0:T(2,128)S(1)}, f32[2,15]{1,0:T(2,128)}, u32[]{:S(2)}) copy-start(f32[2,15]{1,0:T(2,128)} %refs_2_.1) | copy-start | bytes 364
  13.3 0.7 %copy-start = (f32[2,41]{1,0:T(2,128)S(1)}, f32[2,41]{1,0:T(2,128)}, u32[]{:S(2)}) copy-start(f32[2,41]{1,0:T(2,128)} %refs_1_.1) | copy-start | bytes 988

commit v4 on v3

v4 whole, which is shorter than its diff:
```python
import jax
import jax.numpy as jnp
from jax import lax
from jax.experimental import pallas as pl
from jax.experimental.pallas import tpu as pltpu
from jax.sharding import PartitionSpec as P

ITERS = 2
LANES = 128
GROUP = 8
VMEM_LIMIT = 48 * 1024 * 1024


def params():
    return pltpu.CompilerParams(vmem_limit_bytes=VMEM_LIMIT)


def in_vmem():
    return pl.BlockSpec(memory_space=pltpu.VMEM)


def in_smem():
    return pl.BlockSpec(memory_space=pltpu.SMEM)


def split(value):
    high = value.astype(jnp.bfloat16)
    low = (value - high.astype(jnp.float32)).astype(jnp.bfloat16)
    return high, low


def payload_kernel(own, strip, extents, skews, to_core, to_chip, sems):
    strip_rows = strip.shape[2]
    tile = lax.axis_index("tile")
    low, high = slice(0, strip_rows), slice(strip_rows, 2 * strip_rows)

    def fill(up, down):
        pieces = []
        for c in range(strip.shape[0]):
            pieces += [
                (strip.at[c], up.at[c, :, low, :]),
                (own.at[c, :, own.shape[2] - strip_rows :, :], up.at[c, :, high, :]),
                (own.at[c, :, low, :], down.at[c, :, low, :]),
            ]
        copies = [pltpu.make_async_copy(source, target, sems.at[i]) for i, (source, target) in enumerate(pieces)]
        for copy in copies:
            copy.start()
        extent = jnp.where(tile == 0, 0, extents[0])
        column = lax.broadcasted_iota(jnp.int32, strip.shape, 3)
        down[:, :, high, :] = jnp.where(column < LANES, extent, skews[0]).astype(jnp.float32)
        for copy in copies:
            copy.wait()

    @pl.when(tile % 2 == 1)
    def _():
        fill(to_chip, to_core)

    @pl.when(tile % 2 == 0)
    def _():
        fill(to_core, to_chip)


def pack_kernel(to_core, to_chip, core, chip, _, windows, *, blocks):
    chans, _, row_count, voxels = core.shape
    half = row_count // 2
    block = voxels // blocks
    lane = lax.broadcasted_iota(jnp.int32, (1, LANES), 1)
    tall = lax.broadcasted_iota(jnp.int32, (half, voxels), 0)
    lower = lax.axis_index("tile") % 2 == 1

    def pick(low, high, c, part):
        at = slice(part * half, (part + 1) * half)
        return jnp.where(lower, low[c, 0, at, :], high[c, 0, at, :])

    def numbers(low, high):
        both = pick(low, high, 0, 1)[0:GROUP].astype(jnp.int32)
        return jnp.max(both[:, :LANES]), jnp.max(both[:, LANES:])

    extent, skew = numbers(to_core, to_chip)
    next_extent, next_skew = numbers(chip, core)
    for c in range(chans):
        turned = pltpu.roll(pick(core, chip, c, 0), skew, 1)
        top = pick(to_core, to_chip, c, 0)
        top = jnp.where(tall < extent, 0.5 * (top + turned), top)
        bottom = pick(to_chip, to_core, c, 1)
        turned = pltpu.roll(pick(to_chip, to_core, c, 0), next_skew, 1)
        after = chip[c, 0, :half, :]
        after = jnp.where(tall < next_extent, 0.5 * (after + turned), after)
        before = chip[c, 0, half:, :]
        rows = [jnp.where(lower, top, bottom), jnp.where(lower, bottom, top), jnp.where(lower, after, before)]
        rows = jnp.concatenate(rows, axis=0)
        for j in range(blocks):
            start = j * block - (LANES - LANES // 2) // 2
            window = pltpu.roll(rows, -start % voxels, 1)[:, :LANES]
            inside = (lane >= -start) & (lane < voxels - start)
            windows[c * blocks + j] = jnp.where(inside, window, 0.0)


def stages(window_rows, lateral_half, skipped):
    def tiled(rows):
        return -(-rows // 16) * 16

    counts = [window_rows] + [window_rows - 2 * skipped - 2 * k * lateral_half for k in range(1, 2 * ITERS + 1)]
    return [(tiled(read), tiled(written)) for read, written in zip(counts[:-1], counts[1:])]


def bands_kernel(axial, lateral, along_z, along_x, *along_y, spans, skipped, blocks):
    width = lateral.shape[1]
    chan = lax.axis_index("plane") // blocks
    taps = [lateral[chan, j] for j in range(width)]
    for j in range(axial.shape[1]):
        along_z[j] = jnp.full((GROUP, LANES), axial[chan, j], jnp.float32)
    offset = lax.broadcasted_iota(jnp.int32, (LANES, LANES), 0) - lax.broadcasted_iota(jnp.int32, (LANES, LANES), 1)

    def band(order, where, first):
        total = jnp.zeros((LANES, LANES), jnp.float32)
        for j in range(width):
            total = jnp.where(where == j + first, order[j], total)
        return split(total)

    for which in range(2):
        order = taps if which == 0 else taps[::-1]
        high, low = band(order, offset, -(width // 2))
        along_x[which, :LANES, :LANES] = high
        along_x[which, :LANES, LANES:] = low
        along_x[which, LANES:, :LANES] = high
        along_x[which, LANES:, LANES:] = jnp.zeros_like(low)
        for k in range(which, len(spans), 2):
            read, written = spans[k]
            high, low = band(order, -offset, skipped if k == 0 else 0)
            top, bottom = high[:written, :read], low[:written, :read]
            along_y[k][:written] = jnp.concatenate([top, top], axis=1)
            along_y[k][written:] = jnp.concatenate([bottom, jnp.zeros_like(bottom)], axis=1)


def deconvolve_kernel(own, core, axial, x_bands, *refs, spans, lateral_half, skipped, blocks):
    y_bands, (result, windows, blurred, estimate) = refs[: len(spans)], refs[len(spans) :]
    planes, window_rows, _ = windows.shape
    half = core.shape[1]
    out_rows = 2 * half
    axial_half = axial.shape[0] // 2
    columns = [slice(q * LANES, (q + 1) * LANES) for q in range(planes)]
    lower = lax.axis_index("tile") % 2 == 1
    for place, piece in enumerate((core[...], *(own[:, i * half : (i + 1) * half, :] for i in range(3)))):
        at = jnp.where(lower, place, 3 - place) * half
        windows[:, pl.ds(pl.multiple_of(at, half), half), :] = piece

    def along_x(values, which):
        out = []
        for q in range(0, planes, 2):
            pair = jnp.concatenate(values[q : q + 2], axis=0)
            product = jnp.dot(jnp.concatenate(split(pair), axis=1), x_bands[which], preferred_element_type=jnp.float32)
            product = product[:, :LANES] + product[:, LANES:]
            out += [product[: pair.shape[0] // 2], product[pair.shape[0] // 2 :]]
        return out

    def along_y(k):
        read, written = spans[k]
        for q in range(0, planes, 2):
            pair = slice(q * LANES, (q + 2) * LANES)
            both = jnp.concatenate(split(blurred[0:read, pair]), axis=0)
            product = jnp.dot(y_bands[k][...], both, preferred_element_type=jnp.float32)
            blurred[0:written, pair] = product[:written] + product[written:]

    def along_z(values, flipped):
        out = []
        for p in range(planes):
            total = None
            for q in range(planes):
                at = (p - q if flipped else q - p) + axial_half
                if 0 <= at < 2 * axial_half + 1:
                    term = axial[at] * values[q]
                    total = term if total is None else total + term
            out.append(total)
        return out

    origin = skipped
    for sweep in range(ITERS):
        read, written = spans[2 * sweep]
        source = [windows[p] if sweep == 0 else estimate[0:read, columns[p]] for p in range(planes)]
        for p, value in enumerate(along_x(source, 0)):
            blurred[0:read, columns[p]] = value
        along_y(2 * sweep)
        origin += lateral_half
        for row in range(0, written, GROUP):
            at = slice(row, row + GROUP)
            mixed = along_z([blurred[at, columns[q]] for q in range(planes)], False)
            quotient = []
            for p in range(planes):
                joined = windows[p, row + origin : row + origin + GROUP, :]
                quotient.append(joined / jnp.where(joined > 0.0, mixed[p], 1.0))
            back = along_z(quotient, True)
            for p in range(planes):
                blurred[at, columns[p]] = back[p]
        read, written = spans[2 * sweep + 1]
        along_y(2 * sweep + 1)
        origin += lateral_half
        factor = along_x([blurred[0:written, columns[p]] for p in range(planes)], 1)
        for p in range(planes):
            if sweep == 0:
                before = windows[p, origin : origin + written, :]
            else:
                before = estimate[2 * lateral_half : 2 * lateral_half + written, columns[p]]
            estimate[0:written, columns[p]] = before * factor[p]
    voxels = 2 * LANES // blocks
    parts = LANES // voxels
    tall = out_rows // parts
    side = (LANES - LANES // 2) // 2
    lane = lax.broadcasted_iota(jnp.int32, (1, LANES), 1)
    for p in range(planes):
        packed = None
        for m in range(parts):
            piece = pltpu.roll(estimate[m * tall : (m + 1) * tall, columns[p]], (m * voxels - side) % LANES, 1)
            packed = piece if packed is None else jnp.where(lane < m * voxels, packed, piece)
        result[p] = packed


def unpack_kernel(received, out, *, blocks):
    chans, _, row_count, voxels = out.shape
    block = voxels // blocks
    parts = LANES // block
    tall = row_count // parts
    lane = lax.broadcasted_iota(jnp.int32, (1, LANES), 1)
    for c in range(chans):
        for column in range(0, voxels, LANES):
            first = c * blocks + column // block
            for m in range(parts):
                whole = None
                for i in range(parts):
                    value = received[first + i]
                    piece = value if i == m else pltpu.roll(value, (i - m) * block % LANES, 1)
                    whole = piece if whole is None else jnp.where(lane < i * block, whole, piece)
                out[c, 0, m * tall : (m + 1) * tall, column : column + LANES] = whole


def shards(observed, intersection_strip, axial_taps, lateral_taps, extents, section_skews):
    chans, _, row_count, voxels = observed.shape
    planes = lax.axis_size("plane")
    tiles = lax.axis_size("tile")
    half = row_count // 2
    blocks = planes // chans
    lateral_half = lateral_taps.shape[1] // 2
    skipped = half - 2 * ITERS * lateral_half
    window_rows = row_count + 2 * half
    cores = [(i, i ^ 1) for i in range(tiles)]
    chips = [pair for i in range(1, tiles - 1, 2) for pair in ((i, i + 1), (i + 1, i))]

    payload = jax.ShapeDtypeStruct((chans, 1, 2 * half, voxels), jnp.float32)
    to_core, to_chip = pl.pallas_call(
        payload_kernel,
        out_shape=(payload, payload),
        in_specs=[pl.BlockSpec(memory_space=pltpu.HBM)] * 2 + [in_smem()] * 2,
        out_specs=(in_vmem(), in_vmem()),
        scratch_shapes=[pltpu.SemaphoreType.DMA((3 * chans,))],
        compiler_params=params(),
        name="payload",
    )(*(pltpu.with_memory_space_constraint(array, pltpu.HBM) for array in (observed, intersection_strip)), extents, section_skews)
    chip = lax.ppermute(to_chip, "tile", chips)
    core = lax.ppermute(to_core, "tile", cores)
    spans = stages(window_rows, lateral_half, skipped)
    bands = pl.pallas_call(
        lambda *refs: bands_kernel(*refs, spans=spans, skipped=skipped, blocks=blocks),
        out_shape=[
            jax.ShapeDtypeStruct((axial_taps.shape[1], GROUP, LANES), jnp.float32),
            jax.ShapeDtypeStruct((2, 2 * LANES, 2 * LANES), jnp.bfloat16),
        ]
        + [jax.ShapeDtypeStruct((2 * written, 2 * read), jnp.bfloat16) for read, written in spans],
        in_specs=[in_smem()] * 2,
        out_specs=[in_vmem()] * (2 + len(spans)),
        cost_estimate=pl.CostEstimate(flops=1 << 20, bytes_accessed=1 << 20, transcendentals=0),
        compiler_params=params(),
        name="bands",
    )(axial_taps, lateral_taps)
    windows = pl.pallas_call(
        lambda *refs: pack_kernel(*refs, blocks=blocks),
        out_shape=jax.ShapeDtypeStruct((planes, row_count + half, LANES), jnp.float32),
        in_specs=[in_vmem()] * 4 + [pl.BlockSpec(memory_space=pl.ANY)],
        out_specs=in_vmem(),
        compiler_params=params(),
        name="pack",
    )(to_core, to_chip, core, chip, bands[0])
    windows = lax.all_to_all(windows, "plane", 0, 0, tiled=True)

    across = lax.ppermute(windows[:, :half, :], "tile", cores)
    result = pl.pallas_call(
        lambda *refs: deconvolve_kernel(
            *refs, spans=spans, lateral_half=lateral_half, skipped=skipped, blocks=blocks
        ),
        out_shape=jax.ShapeDtypeStruct((planes, row_count * voxels // blocks // LANES, LANES), jnp.float32),
        in_specs=[in_vmem()] * (4 + len(spans)),
        out_specs=in_vmem(),
        scratch_shapes=[
            pltpu.VMEM((planes, window_rows, LANES), jnp.float32),
            pltpu.VMEM((spans[0][0], planes * LANES), jnp.float32),
            pltpu.VMEM((spans[1][1], planes * LANES), jnp.float32),
        ],
        compiler_params=params(),
        name="deconvolve",
    )(windows, across, *bands)
    received = lax.all_to_all(result, "plane", 0, 0, tiled=True)
    return pl.pallas_call(
        lambda *refs: unpack_kernel(*refs, blocks=blocks),
        out_shape=jax.ShapeDtypeStruct(observed.shape, jnp.float32),
        in_specs=[in_vmem()],
        out_specs=in_vmem(),
        compiler_params=params(),
        name="unpack",
    )(received)


def solution(mesh):
    in_specs = (
        P(None, "plane", "tile", None),
        P(None, "plane", "tile", None),
        P(),
        P(),
        P("tile"),
        P("tile"),
    )
    out_specs = P(None, "plane", "tile", None)
    return jax.shard_map(shards, mesh=mesh, in_specs=in_specs, out_specs=out_specs, check_vma=False)
```

time: 42 us -> 39.9 us (0.950)
  blocking collectives: 15 us -> 26.8 us
  waiting for transfers between devices: 8.94 us -> 0.99 us
  starting transfers between devices: 8.34 us -> 4.93 us
  Pallas kernels: 7.24 us -> 5.5 us
  local copies, waits for them, and re-layouts: 0.68 us -> 0.02 us
    all_to_all x0 -> x1, blocking collectives: none -> 16.1 us  [shards(): windows = lax.all_to_all(windows, 'plane', 0, 0, tiled=True)]
    all_to_all x1 -> x0, waiting for transfers between devices: 8.62 us -> none  [shards(): windows = lax.all_to_all(windows, 'plane', 0, 0, tiled=True)]
    all_to_all x1 -> x0, starting transfers between devices: 7.17 us -> none  [shards(): windows = lax.all_to_all(windows, 'plane', 0, 0, tiled=True)]
    all_to_all x1, blocking collectives: 15 us -> 10.7 us  [shards(): received = lax.all_to_all(result, 'plane', 0, 0, tiled=True)]
    ppermute x0 -> x1, starting transfers between devices: none -> 3.76 us  [shards(): across = lax.ppermute(windows[:, :half, :], 'tile', cores)]
    pallas_call x4, Pallas kernels: 4.82 us -> 3.05 us  [the longest x1 0.92 us: shards(): pl.pallas_call(lambda *refs: bands_kernel(*refs, spans=spans, skipped=ski...]
    ppermute x0 -> x1, waiting for transfers between devices: none -> 0.99 us  [shards(): across = lax.ppermute(windows[:, :half, :], 'tile', cores)]
    unnamed x4, local copies, waits for them, and re-layouts: 0.68 us -> 0.01 us
  transfers between devices with their start and end apart: 3 -> 3, of which waited for: 2 -> 1; matrix products, arithmetic and copies ran while one was open for 0% -> 0% of each run, Pallas kernels for 2% -> 2%
where the time goes in v4:
time: 39.9 us; the launch traced here: 39.6 us
  blocking collectives  26.8 us (67%)
  Pallas kernels  5.5 us (14%)
  starting transfers between devices  4.93 us (12%)
  between operations  1.39 us (3%)
  waiting for transfers between devices  0.99 us (2%)
    all_to_all x1, blocking collectives, shards(): windows = lax.all_to_all(windows, 'plane', 0, 0, tiled=True)  16.1 us
    all_to_all x1, blocking collectives, shards(): received = lax.all_to_all(result, 'plane', 0, 0, tiled=True)  10.7 us
    ppermute x1, starting transfers between devices, shards(): across = lax.ppermute(windows[:, :half, :], 'tile', cores)  3.76 us
    pallas_call x1, Pallas kernels, shards(): pl.pallas_call(lambda *refs: deconvolve_kernel(*refs, spans=spans, latera...  2.45 us
    ppermute x1, waiting for transfers between devices, shards(): across = lax.ppermute(windows[:, :half, :], 'tile', cores)  0.99 us
    pallas_call x1, Pallas kernels, shards(): pl.pallas_call(lambda *refs: bands_kernel(*refs, spans=spans, skipped=ski...  0.92 us
    pallas_call x1, Pallas kernels, shards(): pl.pallas_call(payload_kernel, out_shape=(payload, payload), in_specs=[pl...  0.91 us
  transfers between devices with their start and end apart: 3, of which 1 were waited for; matrix products, arithmetic and copies ran while one was open for 0% of the time, Pallas kernels for 2%

profile of v4, /device:TPU:0, one launch (start us, length us, event | category | flops | bytes accessed | tf_op | source)
XLA Modules:
  0.0 39.6 jit_solution(312338239272995239)
XLA Ops:
  1.3 0.9 %payload.1 = (f32[2,1,64,256]{3,2,1,0:T(8,128)S(1)}, f32[2,1,64,256]{3,2,1,0:T(8,128)S(1)}) custom-call(f32[2,1,64,256]{3,2,1,0:T(8,128)} %own.1, f32[2,1,32,256]{3,2,1,0:T(8,128)} %strip.1, s32[1]{0:T(128)S(6)} %copy.7.extents, s32[1]{0:T(128)S(6)} %copy.8.skews), custom_call_target="tpu_custom_call" | custom-call | tf_op jit(solution)/shard_map/payload/pallas_call | solution.py:249
  2.2 0.0 copy-start.1
  2.2 0.0 copy-start
  2.2 0.5 %collective-permute-start = (f32[2,1,64,256]{3,2,1,0:T(8,128)S(1)}, f32[2,1,64,256]{3,2,1,0:T(8,128)S(1)}, u32[]{:S(2)}, u32[]{:S(2)}) collective-permute-start(f32[2,1,64,256]{3,2,1,0:T(8,128)S(1)} %get-tuple-element.13.refs_0_), channel_id=1, source_target_pairs={{0,8},{8,0},{16,24},{24,16},{1,9},{9,1},{17,25},{25,17},{2,10},{10... | collective-permute-start | bytes 393224 | tf_op jit(solution)/shard_map/ppermute | solution.py:259
  2.8 0.7 %collective-permute-start.1 = (f32[2,1,64,256]{3,2,1,0:T(8,128)S(1)}, f32[2,1,64,256]{3,2,1,0:T(8,128)S(1)}, u32[]{:S(2)}, u32[]{:S(2)}) collective-permute-start(f32[2,1,64,256]{3,2,1,0:T(8,128)S(1)} %get-tuple-element.14.refs_1_), channel_id=1, source_target_pairs={{8,16},{16,8},{9,17},{17,9},{10,18},{18,10},{11,19},{19,11},{12,20... | collective-permute-start | bytes 393224 | tf_op jit(solution)/shard_map/ppermute | solution.py:258
  3.4 0.0 copy-done.1
  3.4 0.0 copy-done
  3.4 0.9 %bands.1 = (f32[41,8,128]{2,1,0:T(8,128)S(1)}, bf16[2,256,256]{2,1,0:T(8,128)(2,1)S(1)}, bf16[224,256]{1,0:T(8,128)(2,1)S(1)}, bf16[192,224]{1,0:T(8,128)(2,1)S(...) custom-call(f32[2,41]{1,0:T(2,128)S(1)} %copy-done, f32[2,15]{1,0:T(2,128)S(1)} %copy-done.1), custom_call_target="tpu_custom_call" | custom-call | flops 1048576 | bytes 1048576 | tf_op jit(solution)/shard_map/bands/pallas_call | solution.py:261
  4.4 0.0 collective-permute-done.refs_2_
  4.4 0.0 collective-permute-done.1.refs_3_
  4.4 0.5 %pack.1 = f32[8,96,128]{2,1,0:T(8,128)S(1)} custom-call(f32[2,1,64,256]{3,2,1,0:T(8,128)S(1)} %get-tuple-element.13.refs_0_, f32[2,1,64,256]{3,2,1,0:T(8,128)S(1)} %get-tuple-element.14.refs_1_, f32[2,1,64,256]{3,2,1,0:T(8,128)S(1)} %collective-permute-done.refs_2_, f32[2,1,64,256]{3,2,1,0:T(8,128)S(1)} %collective-permute-done.1.refs_3_, ...), custom_call_target="tpu_custom_call" | custom-call | tf_op jit(solution)/shard_map/pack/pallas_call | solution.py:274
  4.9 16.1 %all_to_all.10.refs_0_ = f32[8,96,128]{2,1,0:T(8,128)S(1)} all-to-all(f32[8,96,128]{2,1,0:T(8,128)S(1)} %pack.1), channel_id=1, replica_groups=mesh['tile'=4,'plane'=8] {'plane'}, dimensions={0} | all-to-all | bytes 786432 | tf_op jit(solution)/shard_map/all_to_all | solution.py:282
  21.0 3.8 %collective-permute-start.2 = (f32[8,32,128]{2,1,0:T(8,128)S(1)}, f32[8,32,128]{2,1,0:T(8,128)S(1)}, u32[]{:S(2)}, u32[]{:S(2)}) collective-permute-start(f32[8,32,128]{2,1,0:T(8,128)S(1)} %slice.4), channel_id=1, source_target_pairs={{0,8},{8,0},{16,24},{24,16},{1,9},{9,1},{17,25},{25,17},{2,10},{10... | collective-permute-start | bytes 393224 | tf_op jit(solution)/shard_map/ppermute | solution.py:284
  24.7 1.0 %collective-permute-done.2.refs_1_ = f32[8,32,128]{2,1,0:T(8,128)S(1)} collective-permute-done((f32[8,32,128]{2,1,0:T(8,128)S(1)}, f32[8,32,128]{2,1,0:T(8,128)S(1)}, u32[]{:S(2)}, u32[]{:S(2)}) %collective-permute-start.2) | collective-permute-done | bytes 131104 | tf_op jit(solution)/shard_map/ppermute | solution.py:284
  25.7 2.4 %deconvolve.1 = f32[8,32,128]{2,1,0:T(8,128)S(1)} custom-call(f32[8,96,128]{2,1,0:T(8,128)S(1)} %all_to_all.10.refs_0_, f32[8,32,128]{2,1,0:T(8,128)S(1)} %collective-permute-done.2.refs_1_, f32[41,8,128]{2,1,0:T(8,128)S(1)} %get-tuple-element.15.refs_4_.refs_2_, bf16[2,256,256]{2,1,0:T(8,128)(2,1)S(1)} %get-tuple-element.16.refs_3_, ...), custom_call_target="tpu_custom_call" | custom-call | tf_op jit(solution)/shard_map/deconvolve/pallas_call | solution.py:285
  28.2 10.7 %all_to_all.11.refs_0_ = f32[8,32,128]{2,1,0:T(8,128)S(1)} all-to-all(f32[8,32,128]{2,1,0:T(8,128)S(1)} %deconvolve.1), channel_id=1, replica_groups=mesh['tile'=4,'plane'=8] {'plane'}, dimensions={0} | all-to-all | bytes 262144 | tf_op jit(solution)/shard_map/all_to_all | solution.py:300
  38.9 0.8 %unpack.1 = f32[2,1,64,256]{3,2,1,0:T(8,128)} custom-call(f32[8,32,128]{2,1,0:T(8,128)S(1)} %all_to_all.11.refs_0_), custom_call_target="tpu_custom_call" | custom-call | tf_op jit(solution)/shard_map/unpack/pallas_call | solution.py:301
  (1 shorter events, 0.0 us)
Async XLA Ops:
  2.2 1.2 %copy-start.1 = (f32[2,15]{1,0:T(2,128)S(1)}, f32[2,15]{1,0:T(2,128)}, u32[]{:S(2)}) copy-start(f32[2,15]{1,0:T(2,128)} %refs_1_.1) | copy-start | bytes 364
  2.2 1.2 %copy-start = (f32[2,41]{1,0:T(2,128)S(1)}, f32[2,41]{1,0:T(2,128)}, u32[]{:S(2)}) copy-start(f32[2,41]{1,0:T(2,128)} %refs_0_.1) | copy-start | bytes 988
  2.2 2.1 %collective-permute-start = (f32[2,1,64,256]{3,2,1,0:T(8,128)S(1)}, f32[2,1,64,256]{3,2,1,0:T(8,128)S(1)}, u32[]{:S(2)}, u32[]{:S(2)}) collective-permute-start(f32[2,1,64,256]{3,2,1,0:T(8,128)S(1)} %get-tuple-element.13.refs_0_), channel_id=1, source_target_pairs={{0,8},{8,0},{16,24},{24,16},{1,9},{9,1},{17,25},{25,17},{2,10},{10... | collective-permute-start | bytes 393224 | tf_op jit(solution)/shard_map/ppermute | solution.py:259
  2.8 1.6 %collective-permute-start.1 = (f32[2,1,64,256]{3,2,1,0:T(8,128)S(1)}, f32[2,1,64,256]{3,2,1,0:T(8,128)S(1)}, u32[]{:S(2)}, u32[]{:S(2)}) collective-permute-start(f32[2,1,64,256]{3,2,1,0:T(8,128)S(1)} %get-tuple-element.14.refs_1_), channel_id=1, source_target_pairs={{8,16},{16,8},{9,17},{17,9},{10,18},{18,10},{11,19},{19,11},{12,20... | collective-permute-start | bytes 393224 | tf_op jit(solution)/shard_map/ppermute | solution.py:258
  21.0 4.7 %collective-permute-start.2 = (f32[8,32,128]{2,1,0:T(8,128)S(1)}, f32[8,32,128]{2,1,0:T(8,128)S(1)}, u32[]{:S(2)}, u32[]{:S(2)}) collective-permute-start(f32[8,32,128]{2,1,0:T(8,128)S(1)} %slice.4), channel_id=1, source_target_pairs={{0,8},{8,0},{16,24},{24,16},{1,9},{9,1},{17,25},{25,17},{2,10},{10... | collective-permute-start | bytes 393224 | tf_op jit(solution)/shard_map/ppermute | solution.py:284

commit v5 on v4

--- a/solution.py
+++ b/solution.py
@@ -96,15 +96,22 @@
             windows[c * blocks + j] = jnp.where(inside, window, 0.0)
 
 
-def stages(window_rows, lateral_half, skipped):
+def stages(row_count, half, lateral_half):
     def tiled(rows):
         return -(-rows // 16) * 16
 
-    counts = [window_rows] + [window_rows - 2 * skipped - 2 * k * lateral_half for k in range(1, 2 * ITERS + 1)]
-    return [(tiled(read), tiled(written)) for read, written in zip(counts[:-1], counts[1:])]
-
-
-def bands_kernel(axial, lateral, along_z, along_x, *along_y, spans, skipped, blocks):
+    known = row_count + half
+    skipped = half - 2 * ITERS * lateral_half
+    out = [(known, known - 16, 0, 0), (half + 16, half, 0, 0)]
+    read, rows, ahead = known + half - 16, known + half - 2 * skipped - 2 * lateral_half, skipped
+    for k in range(1, 2 * ITERS):
+        rows -= 2 * lateral_half
+        out.append((read, tiled(rows), ahead, k % 2))
+        read, ahead = tiled(rows), 0
+    return out
+
+
+def bands_kernel(axial, lateral, along_z, along_x, *along_y, spans, blocks):
     width = lateral.shape[1]
     chan = lax.axis_index("plane") // blocks
     taps = [lateral[chan, j] for j in range(width)]
@@ -112,105 +119,163 @@
         along_z[j] = jnp.full((GROUP, LANES), axial[chan, j], jnp.float32)
     offset = lax.broadcasted_iota(jnp.int32, (LANES, LANES), 0) - lax.broadcasted_iota(jnp.int32, (LANES, LANES), 1)
 
-    def band(order, where, first):
+    def band(flipped, where, first):
+        order = taps[::-1] if flipped else taps
         total = jnp.zeros((LANES, LANES), jnp.float32)
         for j in range(width):
             total = jnp.where(where == j + first, order[j], total)
         return split(total)
 
-    for which in range(2):
-        order = taps if which == 0 else taps[::-1]
-        high, low = band(order, offset, -(width // 2))
-        along_x[which, :LANES, :LANES] = high
-        along_x[which, :LANES, LANES:] = low
-        along_x[which, LANES:, :LANES] = high
-        along_x[which, LANES:, LANES:] = jnp.zeros_like(low)
-        for k in range(which, len(spans), 2):
-            read, written = spans[k]
-            high, low = band(order, -offset, skipped if k == 0 else 0)
-            top, bottom = high[:written, :read], low[:written, :read]
-            along_y[k][:written] = jnp.concatenate([top, top], axis=1)
-            along_y[k][written:] = jnp.concatenate([bottom, jnp.zeros_like(bottom)], axis=1)
-
-
-def deconvolve_kernel(own, core, axial, x_bands, *refs, spans, lateral_half, skipped, blocks):
-    y_bands, (result, windows, blurred, estimate) = refs[: len(spans)], refs[len(spans) :]
-    planes, window_rows, _ = windows.shape
-    half = core.shape[1]
+    for flipped in range(2):
+        high, low = band(flipped, offset, -(width // 2))
+        along_x[flipped, :LANES, :LANES] = high
+        along_x[flipped, :LANES, LANES:] = low
+        along_x[flipped, LANES:, :LANES] = high
+        along_x[flipped, LANES:, LANES:] = jnp.zeros_like(low)
+    made = {}
+    for ref, (read, written, ahead, flipped) in zip(along_y, spans):
+        if (ahead, flipped) not in made:
+            made[ahead, flipped] = band(flipped, -offset, ahead)
+        high, low = made[ahead, flipped]
+        top, bottom = high[:written, :read], low[:written, :read]
+        ref[:written] = jnp.concatenate([top, top], axis=1)
+        ref[written:] = jnp.concatenate([bottom, jnp.zeros_like(bottom)], axis=1)
+
+
+def planes_of(count):
+    return [slice(q * LANES, (q + 1) * LANES) for q in range(count)]
+
+
+def blur_x(values, band):
+    out = []
+    for q in range(0, len(values), 2):
+        pair = jnp.concatenate(values[q : q + 2], axis=0)
+        product = jnp.dot(jnp.concatenate(split(pair), axis=1), band, preferred_element_type=jnp.float32)
+        product = product[:, :LANES] + product[:, LANES:]
+        out += [product[: pair.shape[0] // 2], product[pair.shape[0] // 2 :]]
+    return out
+
+
+def blur_y(work, band, span):
+    read, written = span[:2]
+    for q in range(0, work.shape[1], 2 * LANES):
+        pair = slice(q, q + 2 * LANES)
+        both = jnp.concatenate(split(work[0:read, pair]), axis=0)
+        product = jnp.dot(band[...], both, preferred_element_type=jnp.float32)
+        work[0:written, pair] = product[:written] + product[written:]
+
+
+def blur_z(values, axial, flipped):
+    out = []
+    for p in range(len(values)):
+        total = None
+        for q in range(len(values)):
+            at = (p - q if flipped else q - p) + axial.shape[0] // 2
+            if 0 <= at < axial.shape[0]:
+                term = axial[at] * values[q]
+                total = term if total is None else total + term
+        out.append(total)
+    return out
+
+
+def quotient_along_z(work, joined, origin, axial, written, store):
+    columns = planes_of(joined.shape[0])
+    for row in range(0, written, GROUP):
+        mixed = blur_z([work[row : row + GROUP, lanes] for lanes in columns], axial, False)
+        quotient = []
+        for p, blurred in enumerate(mixed):
+            value = joined[p, row + origin : row + origin + GROUP, :]
+            quotient.append(value / jnp.where(value > 0.0, blurred, 1.0))
+        for lanes, value in zip(columns, blur_z(quotient, axial, True)):
+            store(row, lanes, value)
+
+
+def first_kernel(own, axial, x_bands, y_band, spread, joined, work, *, span, lateral_half):
+    half = own.shape[1] // 3
+    lower = lax.axis_index("tile") % 2 == 1
+    for k in range(3):
+        near, far = own[:, k * half : (k + 1) * half, :], own[:, (2 - k) * half : (3 - k) * half, :]
+        joined[:, k * half : (k + 1) * half, :] = jnp.where(lower, near, far)
+    planes = own.shape[0]
+    columns = planes_of(planes)
+    for lanes, value in zip(columns, blur_x([joined[p] for p in range(planes)], x_bands[0])):
+        work[:, lanes] = value
+    blur_y(work, y_band, span)
+
+    def store(row, lanes, value):
+        spread[row : row + GROUP, lanes] = value
+
+    quotient_along_z(work, joined, lateral_half, axial, span[1], store)
+
+
+def second_kernel(own, core, spread, axial, x_bands, *refs, spans, lateral_half, skipped, blocks):
+    y_bands, (result, joined, border, work, estimate) = refs[: len(spans)], refs[len(spans) :]
+    planes, half, _ = core.shape
     out_rows = 2 * half
-    axial_half = axial.shape[0] // 2
-    columns = [slice(q * LANES, (q + 1) * LANES) for q in range(planes)]
+    columns = planes_of(planes)
     lower = lax.axis_index("tile") % 2 == 1
-    for place, piece in enumerate((core[...], *(own[:, i * half : (i + 1) * half, :] for i in range(3)))):
+    for place, piece in enumerate((core[...], *(own[:, k * half : (k + 1) * half, :] for k in range(3)))):
         at = jnp.where(lower, place, 3 - place) * half
-        windows[:, pl.ds(pl.multiple_of(at, half), half), :] = piece
-
-    def along_x(values, which):
-        out = []
-        for q in range(0, planes, 2):
-            pair = jnp.concatenate(values[q : q + 2], axis=0)
-            product = jnp.dot(jnp.concatenate(split(pair), axis=1), x_bands[which], preferred_element_type=jnp.float32)
-            product = product[:, :LANES] + product[:, LANES:]
-            out += [product[: pair.shape[0] // 2], product[pair.shape[0] // 2 :]]
-        return out
-
-    def along_y(k):
-        read, written = spans[k]
-        for q in range(0, planes, 2):
-            pair = slice(q * LANES, (q + 2) * LANES)
-            both = jnp.concatenate(split(blurred[0:read, pair]), axis=0)
-            product = jnp.dot(y_bands[k][...], both, preferred_element_type=jnp.float32)
-            blurred[0:written, pair] = product[:written] + product[written:]
-
-    def along_z(values, flipped):
-        out = []
-        for p in range(planes):
-            total = None
-            for q in range(planes):
-                at = (p - q if flipped else q - p) + axial_half
-                if 0 <= at < 2 * axial_half + 1:
-                    term = axial[at] * values[q]
-                    total = term if total is None else total + term
-            out.append(total)
-        return out
-
-    origin = skipped
+        joined[:, pl.ds(pl.multiple_of(at, half), half), :] = piece
+
+    border[:, 0:16, :] = jnp.where(lower, core[:, 0:16, :], own[:, half - 16 : half, :])
+    border[:, 16:half, :] = jnp.where(lower, core[:, 16:half, :], core[:, 0 : half - 16, :])
+    border[:, half:, :] = jnp.where(lower, own[:, 0:16, :], core[:, half - 16 :, :])
+    for lanes, value in zip(columns, blur_x([border[p] for p in range(planes)], x_bands[0])):
+        work[0 : half + 16, lanes] = value
+    blur_y(work, y_bands[0], spans[0])
+    first = jnp.where(lower, 0, spread.shape[0])
+
+    def store(row, lanes, value):
+        work[pl.ds(pl.multiple_of(first + row, GROUP), GROUP), lanes] = value
+
+    held = [[work[row : row + GROUP, lanes] for lanes in columns] for row in range(0, half, GROUP)]
+    for i, mixed in enumerate(held):
+        row = i * GROUP
+        quotient = []
+        for p, blurred in enumerate(blur_z(mixed, axial, False)):
+            value = border[p, row + lateral_half : row + lateral_half + GROUP, :]
+            quotient.append(value / jnp.where(value > 0.0, blurred, 1.0))
+        held[i] = blur_z(quotient, axial, True)
+    for i, values in enumerate(held):
+        for lanes, value in zip(columns, values):
+            store(i * GROUP, lanes, value)
+    others = jnp.where(lower, half, 0)
+    work[pl.ds(pl.multiple_of(others, GROUP), spread.shape[0]), :] = spread[...]
+
+    origin = skipped + lateral_half
     for sweep in range(ITERS):
-        read, written = spans[2 * sweep]
-        source = [windows[p] if sweep == 0 else estimate[0:read, columns[p]] for p in range(planes)]
-        for p, value in enumerate(along_x(source, 0)):
-            blurred[0:read, columns[p]] = value
-        along_y(2 * sweep)
+        if sweep > 0:
+            read, written = spans[2 * sweep][:2]
+            source = [estimate[0:read, lanes] for lanes in columns]
+            for lanes, value in zip(columns, blur_x(source, x_bands[0])):
+                work[0:read, lanes] = value
+            blur_y(work, y_bands[2 * sweep], spans[2 * sweep])
+            origin += lateral_half
+
+            def replace(row, lanes, value):
+                work[row : row + GROUP, lanes] = value
+
+            quotient_along_z(work, joined, origin, axial, written, replace)
+        written = spans[2 * sweep + 1][1]
+        blur_y(work, y_bands[2 * sweep + 1], spans[2 * sweep + 1])
         origin += lateral_half
-        for row in range(0, written, GROUP):
-            at = slice(row, row + GROUP)
-            mixed = along_z([blurred[at, columns[q]] for q in range(planes)], False)
-            quotient = []
-            for p in range(planes):
-                joined = windows[p, row + origin : row + origin + GROUP, :]
-                quotient.append(joined / jnp.where(joined > 0.0, mixed[p], 1.0))
-            back = along_z(quotient, True)
-            for p in range(planes):
-                blurred[at, columns[p]] = back[p]
-        read, written = spans[2 * sweep + 1]
-        along_y(2 * sweep + 1)
-        origin += lateral_half
-        factor = along_x([blurred[0:written, columns[p]] for p in range(planes)], 1)
-        for p in range(planes):
+        factor = blur_x([work[0:written, lanes] for lanes in columns], x_bands[1])
+        for p, lanes in enumerate(columns):
             if sweep == 0:
-                before = windows[p, origin : origin + written, :]
+                before = joined[p, origin : origin + written, :]
             else:
-                before = estimate[2 * lateral_half : 2 * lateral_half + written, columns[p]]
-            estimate[0:written, columns[p]] = before * factor[p]
+                before = estimate[2 * lateral_half : 2 * lateral_half + written, lanes]
+            estimate[0:written, lanes] = before * factor[p]
     voxels = 2 * LANES // blocks
     parts = LANES // voxels
     tall = out_rows // parts
     side = (LANES - LANES // 2) // 2
     lane = lax.broadcasted_iota(jnp.int32, (1, LANES), 1)
-    for p in range(planes):
+    for p, lanes in enumerate(columns):
         packed = None
         for m in range(parts):
-            piece = pltpu.roll(estimate[m * tall : (m + 1) * tall, columns[p]], (m * voxels - side) % LANES, 1)
+            piece = pltpu.roll(estimate[m * tall : (m + 1) * tall, lanes], (m * voxels - side) % LANES, 1)
             packed = piece if packed is None else jnp.where(lane < m * voxels, packed, piece)
         result[p] = packed
 
@@ -242,6 +307,7 @@
     lateral_half = lateral_taps.shape[1] // 2
     skipped = half - 2 * ITERS * lateral_half
     window_rows = row_count + 2 * half
+    spans = stages(row_count, half, lateral_half)
     cores = [(i, i ^ 1) for i in range(tiles)]
     chips = [pair for i in range(1, tiles - 1, 2) for pair in ((i, i + 1), (i + 1, i))]
 
@@ -257,14 +323,13 @@
     )(*(pltpu.with_memory_space_constraint(array, pltpu.HBM) for array in (observed, intersection_strip)), extents, section_skews)
     chip = lax.ppermute(to_chip, "tile", chips)
     core = lax.ppermute(to_core, "tile", cores)
-    spans = stages(window_rows, lateral_half, skipped)
     bands = pl.pallas_call(
-        lambda *refs: bands_kernel(*refs, spans=spans, skipped=skipped, blocks=blocks),
+        lambda *refs: bands_kernel(*refs, spans=spans, blocks=blocks),
         out_shape=[
             jax.ShapeDtypeStruct((axial_taps.shape[1], GROUP, LANES), jnp.float32),
             jax.ShapeDtypeStruct((2, 2 * LANES, 2 * LANES), jnp.bfloat16),
         ]
-        + [jax.ShapeDtypeStruct((2 * written, 2 * read), jnp.bfloat16) for read, written in spans],
+        + [jax.ShapeDtypeStruct((2 * written, 2 * read), jnp.bfloat16) for read, written, _, _ in spans],
         in_specs=[in_smem()] * 2,
         out_specs=[in_vmem()] * (2 + len(spans)),
         cost_estimate=pl.CostEstimate(flops=1 << 20, bytes_accessed=1 << 20, transcendentals=0),
@@ -282,21 +347,35 @@
     windows = lax.all_to_all(windows, "plane", 0, 0, tiled=True)
 
     across = lax.ppermute(windows[:, :half, :], "tile", cores)
+    along_z, along_x, *along_y = bands
+    first, *rest = spans
+    spread = pl.pallas_call(
+        lambda *refs: first_kernel(*refs, span=first, lateral_half=lateral_half),
+        out_shape=jax.ShapeDtypeStruct((first[1], planes * LANES), jnp.float32),
+        in_specs=[in_vmem()] * 4,
+        out_specs=in_vmem(),
+        scratch_shapes=[
+            pltpu.VMEM((planes, first[0], LANES), jnp.float32),
+            pltpu.VMEM((first[0], planes * LANES), jnp.float32),
+        ],
+        cost_estimate=pl.CostEstimate(flops=1 << 29, bytes_accessed=1 << 20, transcendentals=0),
+        compiler_params=params(),
+        name="first",
+    )(windows, along_z, along_x, along_y[0])
     result = pl.pallas_call(
-        lambda *refs: deconvolve_kernel(
-            *refs, spans=spans, lateral_half=lateral_half, skipped=skipped, blocks=blocks
-        ),
+        lambda *refs: second_kernel(*refs, spans=rest, lateral_half=lateral_half, skipped=skipped, blocks=blocks),
         out_shape=jax.ShapeDtypeStruct((planes, row_count * voxels // blocks // LANES, LANES), jnp.float32),
-        in_specs=[in_vmem()] * (4 + len(spans)),
+        in_specs=[in_vmem()] * (5 + len(rest)),
         out_specs=in_vmem(),
         scratch_shapes=[
             pltpu.VMEM((planes, window_rows, LANES), jnp.float32),
-            pltpu.VMEM((spans[0][0], planes * LANES), jnp.float32),
-            pltpu.VMEM((spans[1][1], planes * LANES), jnp.float32),
+            pltpu.VMEM((planes, half + 16, LANES), jnp.float32),
+            pltpu.VMEM((window_rows - 16, planes * LANES), jnp.float32),
+            pltpu.VMEM((rest[1][1], planes * LANES), jnp.float32),
         ],
         compiler_params=params(),
-        name="deconvolve",
-    )(windows, across, *bands)
+        name="second",
+    )(windows, across, spread, along_z, along_x, *along_y[1:])
     received = lax.all_to_all(result, "plane", 0, 0, tiled=True)
     return pl.pallas_call(
         lambda *refs: unpack_kernel(*refs, blocks=blocks),

time: 39.9 us -> 39.5 us (0.990)
  waiting for transfers between devices: 0.99 us -> 0.2 us
    ppermute x1, waiting for transfers between devices: 0.99 us -> 0.19 us  [shards(): across = lax.ppermute(windows[:, :half, :], 'tile', cores)]
    pallas_call x2 -> x3, Pallas kernels: 3.36 us -> 3.73 us  [the longest x1 2.05 us: shards(): pl.pallas_call(lambda *refs: second_kernel(*refs, spans=rest, lateral_hal...]
  transfers between devices with their start and end apart: 3 -> 3, of which waited for: 1 -> 1; matrix products, arithmetic and copies ran while one was open for 0% -> 0% of each run, Pallas kernels for 2% -> 4%
where the time goes in v5:
time: 39.5 us; the launch traced here: 39.2 us
  blocking collectives  26.8 us (68%)
  Pallas kernels  5.86 us (15%)
  starting transfers between devices  4.97 us (13%)
  between operations  1.4 us (4%)
    all_to_all x1, blocking collectives, shards(): windows = lax.all_to_all(windows, 'plane', 0, 0, tiled=True)  16.1 us
    all_to_all x1, blocking collectives, shards(): received = lax.all_to_all(result, 'plane', 0, 0, tiled=True)  10.7 us
    ppermute x1, starting transfers between devices, shards(): across = lax.ppermute(windows[:, :half, :], 'tile', cores)  3.8 us
    pallas_call x1, Pallas kernels, shards(): pl.pallas_call(lambda *refs: second_kernel(*refs, spans=rest, lateral_hal...  2.05 us
    pallas_call x1, Pallas kernels, shards(): pl.pallas_call(payload_kernel, out_shape=(payload, payload), in_specs=[pl...  0.91 us
    pallas_call x1, Pallas kernels, shards(): pl.pallas_call(lambda *refs: bands_kernel(*refs, spans=spans, blocks=bloc...  0.89 us
  transfers between devices with their start and end apart: 3, of which 1 were waited for; matrix products, arithmetic and copies ran while one was open for 0% of the time, Pallas kernels for 4%

profile of v5, /device:TPU:0, one launch (start us, length us, event | category | flops | bytes accessed | tf_op | source)
XLA Modules:
  0.0 39.2 jit_solution(13441000609813980203)
XLA Ops:
  1.3 0.9 %payload.1 = (f32[2,1,64,256]{3,2,1,0:T(8,128)S(1)}, f32[2,1,64,256]{3,2,1,0:T(8,128)S(1)}) custom-call(f32[2,1,64,256]{3,2,1,0:T(8,128)} %own.1, f32[2,1,32,256]{3,2,1,0:T(8,128)} %strip.1, s32[1]{0:T(128)S(6)} %copy.7.extents, s32[1]{0:T(128)S(6)} %copy.8.skews), custom_call_target="tpu_custom_call" | custom-call | tf_op jit(solution)/shard_map/payload/pallas_call | solution.py:315
  2.2 0.0 copy-start.1
  2.2 0.0 copy-start
  2.2 0.5 %collective-permute-start = (f32[2,1,64,256]{3,2,1,0:T(8,128)S(1)}, f32[2,1,64,256]{3,2,1,0:T(8,128)S(1)}, u32[]{:S(2)}, u32[]{:S(2)}) collective-permute-start(f32[2,1,64,256]{3,2,1,0:T(8,128)S(1)} %get-tuple-element.14.refs_0_), channel_id=1, source_target_pairs={{0,8},{8,0},{16,24},{24,16},{1,9},{9,1},{17,25},{25,17},{2,10},{10... | collective-permute-start | bytes 393224 | tf_op jit(solution)/shard_map/ppermute | solution.py:325
  2.8 0.7 %collective-permute-start.1 = (f32[2,1,64,256]{3,2,1,0:T(8,128)S(1)}, f32[2,1,64,256]{3,2,1,0:T(8,128)S(1)}, u32[]{:S(2)}, u32[]{:S(2)}) collective-permute-start(f32[2,1,64,256]{3,2,1,0:T(8,128)S(1)} %get-tuple-element.15.refs_1_), channel_id=1, source_target_pairs={{8,16},{16,8},{9,17},{17,9},{10,18},{18,10},{11,19},{19,11},{12,20... | collective-permute-start | bytes 393224 | tf_op jit(solution)/shard_map/ppermute | solution.py:324
  3.4 0.0 copy-done.1
  3.4 0.0 copy-done
  3.4 0.9 %bands.1 = (f32[41,8,128]{2,1,0:T(8,128)S(1)}, bf16[2,256,256]{2,1,0:T(8,128)(2,1)S(1)}, bf16[160,192]{1,0:T(8,128)(2,1)S(1)}, bf16[64,96]{1,0:T(8,128)(2,1)S(1)...) custom-call(f32[2,41]{1,0:T(2,128)S(1)} %copy-done, f32[2,15]{1,0:T(2,128)S(1)} %copy-done.1), custom_call_target="tpu_custom_call" | custom-call | flops 1048576 | bytes 1048576 | tf_op jit(solution)/shard_map/bands/pallas_call | solution.py:326
  4.3 0.0 collective-permute-done.refs_2_
  4.3 0.0 collective-permute-done.1.refs_3_
  4.4 0.5 %pack.1 = f32[8,96,128]{2,1,0:T(8,128)S(1)} custom-call(f32[2,1,64,256]{3,2,1,0:T(8,128)S(1)} %get-tuple-element.14.refs_0_, f32[2,1,64,256]{3,2,1,0:T(8,128)S(1)} %get-tuple-element.15.refs_1_, f32[2,1,64,256]{3,2,1,0:T(8,128)S(1)} %collective-permute-done.refs_2_, f32[2,1,64,256]{3,2,1,0:T(8,128)S(1)} %collective-permute-done.1.refs_3_, ...), custom_call_target="tpu_custom_call" | custom-call | tf_op jit(solution)/shard_map/pack/pallas_call | solution.py:339
  4.8 16.1 %all_to_all.10.refs_0_ = f32[8,96,128]{2,1,0:T(8,128)S(1)} all-to-all(f32[8,96,128]{2,1,0:T(8,128)S(1)} %pack.1), channel_id=1, replica_groups=mesh['tile'=4,'plane'=8] {'plane'}, dimensions={0} | all-to-all | bytes 786432 | tf_op jit(solution)/shard_map/all_to_all | solution.py:347
  20.9 3.8 %collective-permute-start.2 = (f32[8,32,128]{2,1,0:T(8,128)S(1)}, f32[8,32,128]{2,1,0:T(8,128)S(1)}, u32[]{:S(2)}, u32[]{:S(2)}) collective-permute-start(f32[8,32,128]{2,1,0:T(8,128)S(1)} %slice.4), channel_id=1, source_target_pairs={{0,8},{8,0},{16,24},{24,16},{1,9},{9,1},{17,25},{25,17},{2,10},{10... | collective-permute-start | bytes 393224 | tf_op jit(solution)/shard_map/ppermute | solution.py:349
  24.7 0.8 %first.1.refs_2_ = f32[80,1024]{1,0:T(8,128)S(1)} custom-call(f32[8,96,128]{2,1,0:T(8,128)S(1)} %all_to_all.10.refs_0_, f32[41,8,128]{2,1,0:T(8,128)S(1)} %get-tuple-element.16.refs_4_.refs_1_.refs_3_, bf16[2,256,256]{2,1,0:T(8,128)(2,1)S(1)} %get-tuple-element.17.refs_2_.refs_4_, bf16[160,192]{1,0:T(8,128)(2,1)S(1)} %get-tuple-element.18.refs_3_), custom_call_target="tpu_custom_call" | custom-call | flops 536870912 | bytes 1048576 | tf_op jit(solution)/shard_map/first/pallas_call | solution.py:352
  25.5 0.2 collective-permute-done.2.refs_1_
  25.7 2.1 %second.1 = f32[8,32,128]{2,1,0:T(8,128)S(1)} custom-call(f32[8,96,128]{2,1,0:T(8,128)S(1)} %all_to_all.10.refs_0_, f32[8,32,128]{2,1,0:T(8,128)S(1)} %collective-permute-done.2.refs_1_, f32[80,1024]{1,0:T(8,128)S(1)} %first.1.refs_2_, f32[41,8,128]{2,1,0:T(8,128)S(1)} %get-tuple-element.16.refs_4_.refs_1_.refs_3_, ...), custom_call_target="tpu_custom_call" | custom-call | tf_op jit(solution)/shard_map/second/pallas_call | solution.py:365
  27.8 10.7 %all_to_all.11.refs_0_ = f32[8,32,128]{2,1,0:T(8,128)S(1)} all-to-all(f32[8,32,128]{2,1,0:T(8,128)S(1)} %second.1), channel_id=1, replica_groups=mesh['tile'=4,'plane'=8] {'plane'}, dimensions={0} | all-to-all | bytes 262144 | tf_op jit(solution)/shard_map/all_to_all | solution.py:379
  38.4 0.8 %unpack.1 = f32[2,1,64,256]{3,2,1,0:T(8,128)} custom-call(f32[8,32,128]{2,1,0:T(8,128)S(1)} %all_to_all.11.refs_0_), custom_call_target="tpu_custom_call" | custom-call | tf_op jit(solution)/shard_map/unpack/pallas_call | solution.py:380
  (1 shorter events, 0.0 us)
Async XLA Ops:
  2.2 1.2 %copy-start.1 = (f32[2,15]{1,0:T(2,128)S(1)}, f32[2,15]{1,0:T(2,128)}, u32[]{:S(2)}) copy-start(f32[2,15]{1,0:T(2,128)} %refs_1_.1) | copy-start | bytes 364
  2.2 1.2 %copy-start = (f32[2,41]{1,0:T(2,128)S(1)}, f32[2,41]{1,0:T(2,128)}, u32[]{:S(2)}) copy-start(f32[2,41]{1,0:T(2,128)} %refs_0_.1) | copy-start | bytes 988
  2.2 2.1 %collective-permute-start = (f32[2,1,64,256]{3,2,1,0:T(8,128)S(1)}, f32[2,1,64,256]{3,2,1,0:T(8,128)S(1)}, u32[]{:S(2)}, u32[]{:S(2)}) collective-permute-start(f32[2,1,64,256]{3,2,1,0:T(8,128)S(1)} %get-tuple-element.14.refs_0_), channel_id=1, source_target_pairs={{0,8},{8,0},{16,24},{24,16},{1,9},{9,1},{17,25},{25,17},{2,10},{10... | collective-permute-start | bytes 393224 | tf_op jit(solution)/shard_map/ppermute | solution.py:325
  2.8 1.6 %collective-permute-start.1 = (f32[2,1,64,256]{3,2,1,0:T(8,128)S(1)}, f32[2,1,64,256]{3,2,1,0:T(8,128)S(1)}, u32[]{:S(2)}, u32[]{:S(2)}) collective-permute-start(f32[2,1,64,256]{3,2,1,0:T(8,128)S(1)} %get-tuple-element.15.refs_1_), channel_id=1, source_target_pairs={{8,16},{16,8},{9,17},{17,9},{10,18},{18,10},{11,19},{19,11},{12,20... | collective-permute-start | bytes 393224 | tf_op jit(solution)/shard_map/ppermute | solution.py:324
  20.9 4.8 %collective-permute-start.2 = (f32[8,32,128]{2,1,0:T(8,128)S(1)}, f32[8,32,128]{2,1,0:T(8,128)S(1)}, u32[]{:S(2)}, u32[]{:S(2)}) collective-permute-start(f32[8,32,128]{2,1,0:T(8,128)S(1)} %slice.4), channel_id=1, source_target_pairs={{0,8},{8,0},{16,24},{24,16},{1,9},{9,1},{17,25},{25,17},{2,10},{10... | collective-permute-start | bytes 393224 | tf_op jit(solution)/shard_map/ppermute | solution.py:349

commit v6 on v5

--- a/solution.py
+++ b/solution.py
@@ -111,9 +111,12 @@
     return out
 
 
-def bands_kernel(axial, lateral, along_z, along_x, *along_y, spans, blocks):
+def bands_kernel(axial, lateral, along_z, along_x, *along_y, spans, blocks, order):
     width = lateral.shape[1]
-    chan = lax.axis_index("plane") // blocks
+    plane = lax.axis_index("plane")
+    chan = jnp.int32(0)
+    for place, owner in enumerate(order):
+        chan = jnp.where(plane == owner, place // blocks, chan)
     taps = [lateral[chan, j] for j in range(width)]
     for j in range(axial.shape[1]):
         along_z[j] = jnp.full((GROUP, LANES), axial[chan, j], jnp.float32)
@@ -165,12 +168,12 @@
         work[0:written, pair] = product[:written] + product[written:]
 
 
-def blur_z(values, axial, flipped):
+def blur_z(values, axial, flipped, order):
     out = []
     for p in range(len(values)):
         total = None
         for q in range(len(values)):
-            at = (p - q if flipped else q - p) + axial.shape[0] // 2
+            at = (order[p] - order[q] if flipped else order[q] - order[p]) + axial.shape[0] // 2
             if 0 <= at < axial.shape[0]:
                 term = axial[at] * values[q]
                 total = term if total is None else total + term
@@ -178,19 +181,19 @@
     return out
 
 
-def quotient_along_z(work, joined, origin, axial, written, store):
+def quotient_along_z(work, joined, origin, axial, order, written, store):
     columns = planes_of(joined.shape[0])
     for row in range(0, written, GROUP):
-        mixed = blur_z([work[row : row + GROUP, lanes] for lanes in columns], axial, False)
+        mixed = blur_z([work[row : row + GROUP, lanes] for lanes in columns], axial, False, order)
         quotient = []
         for p, blurred in enumerate(mixed):
             value = joined[p, row + origin : row + origin + GROUP, :]
             quotient.append(value / jnp.where(value > 0.0, blurred, 1.0))
-        for lanes, value in zip(columns, blur_z(quotient, axial, True)):
+        for lanes, value in zip(columns, blur_z(quotient, axial, True, order)):
             store(row, lanes, value)
 
 
-def first_kernel(own, axial, x_bands, y_band, spread, joined, work, *, span, lateral_half):
+def first_kernel(own, axial, x_bands, y_band, spread, joined, work, *, span, lateral_half, order):
     half = own.shape[1] // 3
     lower = lax.axis_index("tile") % 2 == 1
     for k in range(3):
@@ -205,10 +208,10 @@
     def store(row, lanes, value):
         spread[row : row + GROUP, lanes] = value
 
-    quotient_along_z(work, joined, lateral_half, axial, span[1], store)
-
-
-def second_kernel(own, core, spread, axial, x_bands, *refs, spans, lateral_half, skipped, blocks):
+    quotient_along_z(work, joined, lateral_half, axial, order, span[1], store)
+
+
+def second_kernel(own, core, spread, axial, x_bands, *refs, spans, lateral_half, skipped, blocks, order, sent):
     y_bands, (result, joined, border, work, estimate) = refs[: len(spans)], refs[len(spans) :]
     planes, half, _ = core.shape
     out_rows = 2 * half
@@ -233,10 +236,10 @@
     for i, mixed in enumerate(held):
         row = i * GROUP
         quotient = []
-        for p, blurred in enumerate(blur_z(mixed, axial, False)):
+        for p, blurred in enumerate(blur_z(mixed, axial, False, order)):
             value = border[p, row + lateral_half : row + lateral_half + GROUP, :]
             quotient.append(value / jnp.where(value > 0.0, blurred, 1.0))
-        held[i] = blur_z(quotient, axial, True)
+        held[i] = blur_z(quotient, axial, True, order)
     for i, values in enumerate(held):
         for lanes, value in zip(columns, values):
             store(i * GROUP, lanes, value)
@@ -256,7 +259,7 @@
             def replace(row, lanes, value):
                 work[row : row + GROUP, lanes] = value
 
-            quotient_along_z(work, joined, origin, axial, written, replace)
+            quotient_along_z(work, joined, origin, axial, order, written, replace)
         written = spans[2 * sweep + 1][1]
         blur_y(work, y_bands[2 * sweep + 1], spans[2 * sweep + 1])
         origin += lateral_half
@@ -277,10 +280,10 @@
         for m in range(parts):
             piece = pltpu.roll(estimate[m * tall : (m + 1) * tall, lanes], (m * voxels - side) % LANES, 1)
             packed = piece if packed is None else jnp.where(lane < m * voxels, packed, piece)
-        result[p] = packed
-
-
-def unpack_kernel(received, out, *, blocks):
+        result[sent.index(order[p])] = packed
+
+
+def unpack_kernel(received, out, *, blocks, order, sent):
     chans, _, row_count, voxels = out.shape
     block = voxels // blocks
     parts = LANES // block
@@ -292,10 +295,16 @@
             for m in range(parts):
                 whole = None
                 for i in range(parts):
-                    value = received[first + i]
+                    value = received[sent.index(order[first + i])]
                     piece = value if i == m else pltpu.roll(value, (i - m) * block % LANES, 1)
                     whole = piece if whole is None else jnp.where(lane < i * block, whole, piece)
                 out[c, 0, m * tall : (m + 1) * tall, column : column + LANES] = whole
+
+
+def group_orders(planes):
+    if planes == 8:
+        return [5, 1, 0, 2, 7, 4, 3, 6], [5, 1, 0, 2, 7, 4, 3, 6]
+    return list(range(planes)), list(range(planes))
 
 
 def shards(observed, intersection_strip, axial_taps, lateral_taps, extents, section_skews):
@@ -304,6 +313,7 @@
     tiles = lax.axis_size("tile")
     half = row_count // 2
     blocks = planes // chans
+    order, sent = group_orders(planes)
     lateral_half = lateral_taps.shape[1] // 2
     skipped = half - 2 * ITERS * lateral_half
     window_rows = row_count + 2 * half
@@ -324,7 +334,7 @@
     chip = lax.ppermute(to_chip, "tile", chips)
     core = lax.ppermute(to_core, "tile", cores)
     bands = pl.pallas_call(
-        lambda *refs: bands_kernel(*refs, spans=spans, blocks=blocks),
+        lambda *refs: bands_kernel(*refs, spans=spans, blocks=blocks, order=order),
         out_shape=[
             jax.ShapeDtypeStruct((axial_taps.shape[1], GROUP, LANES), jnp.float32),
             jax.ShapeDtypeStruct((2, 2 * LANES, 2 * LANES), jnp.bfloat16),
@@ -344,13 +354,13 @@
         compiler_params=params(),
         name="pack",
     )(to_core, to_chip, core, chip, bands[0])
-    windows = lax.all_to_all(windows, "plane", 0, 0, tiled=True)
+    windows = lax.all_to_all(windows, "plane", 0, 0, axis_index_groups=[order], tiled=True)
 
     across = lax.ppermute(windows[:, :half, :], "tile", cores)
     along_z, along_x, *along_y = bands
     first, *rest = spans
     spread = pl.pallas_call(
-        lambda *refs: first_kernel(*refs, span=first, lateral_half=lateral_half),
+        lambda *refs: first_kernel(*refs, span=first, lateral_half=lateral_half, order=order),
         out_shape=jax.ShapeDtypeStruct((first[1], planes * LANES), jnp.float32),
         in_specs=[in_vmem()] * 4,
         out_specs=in_vmem(),
@@ -363,7 +373,15 @@
         name="first",
     )(windows, along_z, along_x, along_y[0])
     result = pl.pallas_call(
-        lambda *refs: second_kernel(*refs, spans=rest, lateral_half=lateral_half, skipped=skipped, blocks=blocks),
+        lambda *refs: second_kernel(
+            *refs,
+            spans=rest,
+            lateral_half=lateral_half,
+            skipped=skipped,
+            blocks=blocks,
+            order=order,
+            sent=sent,
+        ),
         out_shape=jax.ShapeDtypeStruct((planes, row_count * voxels // blocks // LANES, LANES), jnp.float32),
         in_specs=[in_vmem()] * (5 + len(rest)),
         out_specs=in_vmem(),
@@ -376,9 +394,9 @@
         compiler_params=params(),
         name="second",
     )(windows, across, spread, along_z, along_x, *along_y[1:])
-    received = lax.all_to_all(result, "plane", 0, 0, tiled=True)
+    received = lax.all_to_all(result, "plane", 0, 0, axis_index_groups=[sent], tiled=True)
     return pl.pallas_call(
-        lambda *refs: unpack_kernel(*refs, blocks=blocks),
+        lambda *refs: unpack_kernel(*refs, blocks=blocks, order=order, sent=sent),
         out_shape=jax.ShapeDtypeStruct(observed.shape, jnp.float32),
         in_specs=[in_vmem()],
         out_specs=in_vmem(),

time: 39.5 us -> 35.3 us (0.89)
  blocking collectives: 26.8 us -> 22 us
  starting transfers between devices: 4.97 us -> 5.62 us
    all_to_all x2, blocking collectives: 26.8 us -> 22 us  [the longest x1 13 us: shards(): lax.all_to_all(windows, 'plane', 0, 0, axis_index_groups=[order], tiled=T...]
    ppermute x1, starting transfers between devices: 3.8 us -> 4.45 us  [shards(): across = lax.ppermute(windows[:, :half, :], 'tile', cores)]
  transfers between devices with their start and end apart: 3 -> 3, of which waited for: 1 -> 1; matrix products, arithmetic and copies ran while one was open for 0% -> 0% of each run, Pallas kernels for 4% -> 5%
where the time goes in v6:
time: 35.3 us; the launch traced here: 35.1 us
  blocking collectives  22 us (62%)
  Pallas kernels  5.84 us (17%)
  starting transfers between devices  5.62 us (16%)
  between operations  1.4 us (4%)
    all_to_all x1, blocking collectives, shards(): lax.all_to_all(windows, 'plane', 0, 0, axis_index_groups=[order], tiled=T...  13 us
    all_to_all x1, blocking collectives, shards(): lax.all_to_all(result, 'plane', 0, 0, axis_index_groups=[sent], tiled=True)  8.97 us
    ppermute x1, starting transfers between devices, shards(): across = lax.ppermute(windows[:, :half, :], 'tile', cores)  4.45 us
    pallas_call x1, Pallas kernels, shards(): pl.pallas_call(lambda *refs: second_kernel(*refs, spans=rest, lateral_hal...  2.04 us
    pallas_call x1, Pallas kernels, shards(): pl.pallas_call(payload_kernel, out_shape=(payload, payload), in_specs=[pl...  0.91 us
    pallas_call x1, Pallas kernels, shards(): pl.pallas_call(lambda *refs: bands_kernel(*refs, spans=spans, blocks=bloc...  0.89 us
    pallas_call x1, Pallas kernels, shards(): pl.pallas_call(lambda *refs: first_kernel(*refs, span=first, lateral_half...  0.79 us
    pallas_call x1, Pallas kernels, shards(): pl.pallas_call(lambda *refs: unpack_kernel(*refs, blocks=blocks, order=or...  0.76 us
  transfers between devices with their start and end apart: 3, of which 1 were waited for; matrix products, arithmetic and copies ran while one was open for 0% of the time, Pallas kernels for 5%

profile of v6, /device:TPU:0, one launch (start us, length us, event | category | flops | bytes accessed | tf_op | source)
XLA Modules:
  0.0 35.1 jit_solution(15233864269279645669)
XLA Ops:
  1.3 0.9 %payload.1 = (f32[2,1,64,256]{3,2,1,0:T(8,128)S(1)}, f32[2,1,64,256]{3,2,1,0:T(8,128)S(1)}) custom-call(f32[2,1,64,256]{3,2,1,0:T(8,128)} %own.1, f32[2,1,32,256]{3,2,1,0:T(8,128)} %strip.1, s32[1]{0:T(128)S(6)} %copy.7.extents, s32[1]{0:T(128)S(6)} %copy.8.skews), custom_call_target="tpu_custom_call" | custom-call | tf_op jit(solution)/shard_map/payload/pallas_call | solution.py:325
  2.2 0.0 copy-start.1
  2.2 0.0 copy-start
  2.2 0.5 %collective-permute-start = (f32[2,1,64,256]{3,2,1,0:T(8,128)S(1)}, f32[2,1,64,256]{3,2,1,0:T(8,128)S(1)}, u32[]{:S(2)}, u32[]{:S(2)}) collective-permute-start(f32[2,1,64,256]{3,2,1,0:T(8,128)S(1)} %get-tuple-element.14.refs_0_), channel_id=1, source_target_pairs={{0,8},{8,0},{16,24},{24,16},{1,9},{9,1},{17,25},{25,17},{2,10},{10... | collective-permute-start | bytes 393224 | tf_op jit(solution)/shard_map/ppermute | solution.py:335
  2.8 0.7 %collective-permute-start.1 = (f32[2,1,64,256]{3,2,1,0:T(8,128)S(1)}, f32[2,1,64,256]{3,2,1,0:T(8,128)S(1)}, u32[]{:S(2)}, u32[]{:S(2)}) collective-permute-start(f32[2,1,64,256]{3,2,1,0:T(8,128)S(1)} %get-tuple-element.15.refs_1_), channel_id=1, source_target_pairs={{8,16},{16,8},{9,17},{17,9},{10,18},{18,10},{11,19},{19,11},{12,20... | collective-permute-start | bytes 393224 | tf_op jit(solution)/shard_map/ppermute | solution.py:334
  3.4 0.0 copy-done.1
  3.4 0.0 copy-done
  3.4 0.9 %bands.1 = (f32[41,8,128]{2,1,0:T(8,128)S(1)}, bf16[2,256,256]{2,1,0:T(8,128)(2,1)S(1)}, bf16[160,192]{1,0:T(8,128)(2,1)S(1)}, bf16[64,96]{1,0:T(8,128)(2,1)S(1)...) custom-call(f32[2,41]{1,0:T(2,128)S(1)} %copy-done, f32[2,15]{1,0:T(2,128)S(1)} %copy-done.1), custom_call_target="tpu_custom_call" | custom-call | flops 1048576 | bytes 1048576 | tf_op jit(solution)/shard_map/bands/pallas_call | solution.py:336
  4.3 0.0 collective-permute-done.refs_2_
  4.3 0.0 collective-permute-done.1.refs_3_
  4.4 0.5 %pack.1 = f32[8,96,128]{2,1,0:T(8,128)S(1)} custom-call(f32[2,1,64,256]{3,2,1,0:T(8,128)S(1)} %get-tuple-element.14.refs_0_, f32[2,1,64,256]{3,2,1,0:T(8,128)S(1)} %get-tuple-element.15.refs_1_, f32[2,1,64,256]{3,2,1,0:T(8,128)S(1)} %collective-permute-done.refs_2_, f32[2,1,64,256]{3,2,1,0:T(8,128)S(1)} %collective-permute-done.1.refs_3_, ...), custom_call_target="tpu_custom_call" | custom-call | tf_op jit(solution)/shard_map/pack/pallas_call | solution.py:349
  4.8 13.0 %all_to_all.10.refs_0_ = f32[8,96,128]{2,1,0:T(8,128)S(1)} all-to-all(f32[8,96,128]{2,1,0:T(8,128)S(1)} %pack.1), channel_id=1, replica_groups={{5,1,0,2,7,4,3,6},{13,9,8,10,15,12,11,14},{21,17,16,18,23,20,19,22},{29..., dimensions={0} | all-to-all | bytes 786432 | tf_op jit(solution)/shard_map/all_to_all | solution.py:357
  17.8 4.5 %collective-permute-start.2 = (f32[8,32,128]{2,1,0:T(8,128)S(1)}, f32[8,32,128]{2,1,0:T(8,128)S(1)}, u32[]{:S(2)}, u32[]{:S(2)}) collective-permute-start(f32[8,32,128]{2,1,0:T(8,128)S(1)} %slice.4), channel_id=1, source_target_pairs={{0,8},{8,0},{16,24},{24,16},{1,9},{9,1},{17,25},{25,17},{2,10},{10... | collective-permute-start | bytes 393224 | tf_op jit(solution)/shard_map/ppermute | solution.py:359
  22.3 0.8 %first.1.refs_2_ = f32[80,1024]{1,0:T(8,128)S(1)} custom-call(f32[8,96,128]{2,1,0:T(8,128)S(1)} %all_to_all.10.refs_0_, f32[41,8,128]{2,1,0:T(8,128)S(1)} %get-tuple-element.16.refs_4_.refs_1_.refs_3_, bf16[2,256,256]{2,1,0:T(8,128)(2,1)S(1)} %get-tuple-element.17.refs_2_.refs_4_, bf16[160,192]{1,0:T(8,128)(2,1)S(1)} %get-tuple-element.18.refs_3_), custom_call_target="tpu_custom_call" | custom-call | flops 536870912 | bytes 1048576 | tf_op jit(solution)/shard_map/first/pallas_call | solution.py:362
  23.1 0.2 collective-permute-done.2.refs_1_
  23.3 2.0 %second.1 = f32[8,32,128]{2,1,0:T(8,128)S(1)} custom-call(f32[8,96,128]{2,1,0:T(8,128)S(1)} %all_to_all.10.refs_0_, f32[8,32,128]{2,1,0:T(8,128)S(1)} %collective-permute-done.2.refs_1_, f32[80,1024]{1,0:T(8,128)S(1)} %first.1.refs_2_, f32[41,8,128]{2,1,0:T(8,128)S(1)} %get-tuple-element.16.refs_4_.refs_1_.refs_3_, ...), custom_call_target="tpu_custom_call" | custom-call | tf_op jit(solution)/shard_map/second/pallas_call | solution.py:375
  25.3 9.0 %all_to_all.11.refs_0_ = f32[8,32,128]{2,1,0:T(8,128)S(1)} all-to-all(f32[8,32,128]{2,1,0:T(8,128)S(1)} %second.1), channel_id=1, replica_groups={{5,1,0,2,7,4,3,6},{13,9,8,10,15,12,11,14},{21,17,16,18,23,20,19,22},{29..., dimensions={0} | all-to-all | bytes 262144 | tf_op jit(solution)/shard_map/all_to_all | solution.py:397
  34.3 0.8 %unpack.1 = f32[2,1,64,256]{3,2,1,0:T(8,128)} custom-call(f32[8,32,128]{2,1,0:T(8,128)S(1)} %all_to_all.11.refs_0_), custom_call_target="tpu_custom_call" | custom-call | tf_op jit(solution)/shard_map/unpack/pallas_call | solution.py:398
  (1 shorter events, 0.0 us)
Async XLA Ops:
  2.2 1.2 %copy-start.1 = (f32[2,15]{1,0:T(2,128)S(1)}, f32[2,15]{1,0:T(2,128)}, u32[]{:S(2)}) copy-start(f32[2,15]{1,0:T(2,128)} %refs_1_.1) | copy-start | bytes 364
  2.2 1.2 %copy-start = (f32[2,41]{1,0:T(2,128)S(1)}, f32[2,41]{1,0:T(2,128)}, u32[]{:S(2)}) copy-start(f32[2,41]{1,0:T(2,128)} %refs_0_.1) | copy-start | bytes 988
  2.2 2.1 %collective-permute-start = (f32[2,1,64,256]{3,2,1,0:T(8,128)S(1)}, f32[2,1,64,256]{3,2,1,0:T(8,128)S(1)}, u32[]{:S(2)}, u32[]{:S(2)}) collective-permute-start(f32[2,1,64,256]{3,2,1,0:T(8,128)S(1)} %get-tuple-element.14.refs_0_), channel_id=1, source_target_pairs={{0,8},{8,0},{16,24},{24,16},{1,9},{9,1},{17,25},{25,17},{2,10},{10... | collective-permute-start | bytes 393224 | tf_op jit(solution)/shard_map/ppermute | solution.py:335
  2.8 1.6 %collective-permute-start.1 = (f32[2,1,64,256]{3,2,1,0:T(8,128)S(1)}, f32[2,1,64,256]{3,2,1,0:T(8,128)S(1)}, u32[]{:S(2)}, u32[]{:S(2)}) collective-permute-start(f32[2,1,64,256]{3,2,1,0:T(8,128)S(1)} %get-tuple-element.15.refs_1_), channel_id=1, source_target_pairs={{8,16},{16,8},{9,17},{17,9},{10,18},{18,10},{11,19},{19,11},{12,20... | collective-permute-start | bytes 393224 | tf_op jit(solution)/shard_map/ppermute | solution.py:334
  17.8 5.4 %collective-permute-start.2 = (f32[8,32,128]{2,1,0:T(8,128)S(1)}, f32[8,32,128]{2,1,0:T(8,128)S(1)}, u32[]{:S(2)}, u32[]{:S(2)}) collective-permute-start(f32[8,32,128]{2,1,0:T(8,128)S(1)} %slice.4), channel_id=1, source_target_pairs={{0,8},{8,0},{16,24},{24,16},{1,9},{9,1},{17,25},{25,17},{2,10},{10... | collective-permute-start | bytes 393224 | tf_op jit(solution)/shard_map/ppermute | solution.py:359

commit v7 on v6

--- a/solution.py
+++ b/solution.py
@@ -96,19 +96,11 @@
             windows[c * blocks + j] = jnp.where(inside, window, 0.0)
 
 
-def stages(row_count, half, lateral_half):
-    def tiled(rows):
-        return -(-rows // 16) * 16
-
+def stages(row_count, half, skipped):
     known = row_count + half
-    skipped = half - 2 * ITERS * lateral_half
-    out = [(known, known - 16, 0, 0), (half + 16, half, 0, 0)]
-    read, rows, ahead = known + half - 16, known + half - 2 * skipped - 2 * lateral_half, skipped
-    for k in range(1, 2 * ITERS):
-        rows -= 2 * lateral_half
-        out.append((read, tiled(rows), ahead, k % 2))
-        read, ahead = tiled(rows), 0
-    return out
+    held = [(known, known - 16, 0, 0), (known - 16, known - 32, 0, 1)]
+    border = [(half + 16, half, 0, 0), (half + 16, half, 0, 1)]
+    return held, border, [(known, known - 16, skipped, 0), (known - 16, row_count, 0, 1)]
 
 
 def bands_kernel(axial, lateral, along_z, along_x, *along_y, spans, blocks, order):
@@ -193,7 +185,8 @@
             store(row, lanes, value)
 
 
-def first_kernel(own, axial, x_bands, y_band, spread, joined, work, *, span, lateral_half, order):
+def first_kernel(own, axial, x_bands, *refs, spans, lateral_half, order):
+    y_bands, (edge, estimate, joined, work) = refs[:2], refs[2:]
     half = own.shape[1] // 3
     lower = lax.axis_index("tile") % 2 == 1
     for k in range(3):
@@ -203,15 +196,22 @@
     columns = planes_of(planes)
     for lanes, value in zip(columns, blur_x([joined[p] for p in range(planes)], x_bands[0])):
         work[:, lanes] = value
-    blur_y(work, y_band, span)
+    blur_y(work, y_bands[0], spans[0])
 
     def store(row, lanes, value):
-        spread[row : row + GROUP, lanes] = value
-
-    quotient_along_z(work, joined, lateral_half, axial, order, span[1], store)
-
-
-def second_kernel(own, core, spread, axial, x_bands, *refs, spans, lateral_half, skipped, blocks, order, sent):
+        work[row : row + GROUP, lanes] = value
+
+    rows = spans[0][1]
+    quotient_along_z(work, joined, lateral_half, axial, order, rows, store)
+    edge[...] = jnp.where(lower, work[0:16, :], work[rows - 16 : rows, :])
+    blur_y(work, y_bands[1], spans[1])
+    rows = spans[1][1]
+    factor = blur_x([work[0:rows, lanes] for lanes in columns], x_bands[1])
+    for p, lanes in enumerate(columns):
+        estimate[:, lanes] = joined[p, 2 * lateral_half : 2 * lateral_half + rows, :] * factor[p]
+
+
+def second_kernel(own, core, edge, held, axial, x_bands, *refs, spans, lateral_half, blocks, order, sent):
     y_bands, (result, joined, border, work, estimate) = refs[: len(spans)], refs[len(spans) :]
     planes, half, _ = core.shape
     out_rows = 2 * half
@@ -221,64 +221,57 @@
         at = jnp.where(lower, place, 3 - place) * half
         joined[:, pl.ds(pl.multiple_of(at, half), half), :] = piece
 
-    border[:, 0:16, :] = jnp.where(lower, core[:, 0:16, :], own[:, half - 16 : half, :])
-    border[:, 16:half, :] = jnp.where(lower, core[:, 16:half, :], core[:, 0 : half - 16, :])
-    border[:, half:, :] = jnp.where(lower, own[:, 0:16, :], core[:, half - 16 :, :])
-    for lanes, value in zip(columns, blur_x([border[p] for p in range(planes)], x_bands[0])):
-        work[0 : half + 16, lanes] = value
+    border[:, 0:half, :] = jnp.where(lower, core[...], own[:, 0:half, :])
+    border[:, half:, :] = jnp.where(lower, own[:, 0:half, :], core[...])
+    read, rows = spans[0][:2]
+    source = [jnp.where(lower, border[p, 0:read, :], border[p, 16 : 16 + read, :]) for p in range(planes)]
+    for lanes, value in zip(columns, blur_x(source, x_bands[0])):
+        work[0:read, lanes] = value
     blur_y(work, y_bands[0], spans[0])
-    first = jnp.where(lower, 0, spread.shape[0])
-
-    def store(row, lanes, value):
-        work[pl.ds(pl.multiple_of(first + row, GROUP), GROUP), lanes] = value
-
-    held = [[work[row : row + GROUP, lanes] for lanes in columns] for row in range(0, half, GROUP)]
-    for i, mixed in enumerate(held):
-        row = i * GROUP
+    quotients = []
+    for row in range(0, rows, GROUP):
         quotient = []
-        for p, blurred in enumerate(blur_z(mixed, axial, False, order)):
-            value = border[p, row + lateral_half : row + lateral_half + GROUP, :]
+        for p, blurred in enumerate(blur_z([work[row : row + GROUP, lanes] for lanes in columns], axial, False, order)):
+            at = row + lateral_half
+            value = jnp.where(lower, border[p, at : at + GROUP, :], border[p, at + 16 : at + 16 + GROUP, :])
             quotient.append(value / jnp.where(value > 0.0, blurred, 1.0))
-        held[i] = blur_z(quotient, axial, True, order)
-    for i, values in enumerate(held):
-        for lanes, value in zip(columns, values):
-            store(i * GROUP, lanes, value)
-    others = jnp.where(lower, half, 0)
-    work[pl.ds(pl.multiple_of(others, GROUP), spread.shape[0]), :] = spread[...]
-
-    origin = skipped + lateral_half
-    for sweep in range(ITERS):
-        if sweep > 0:
-            read, written = spans[2 * sweep][:2]
-            source = [estimate[0:read, lanes] for lanes in columns]
-            for lanes, value in zip(columns, blur_x(source, x_bands[0])):
-                work[0:read, lanes] = value
-            blur_y(work, y_bands[2 * sweep], spans[2 * sweep])
-            origin += lateral_half
-
-            def replace(row, lanes, value):
-                work[row : row + GROUP, lanes] = value
-
-            quotient_along_z(work, joined, origin, axial, order, written, replace)
-        written = spans[2 * sweep + 1][1]
-        blur_y(work, y_bands[2 * sweep + 1], spans[2 * sweep + 1])
-        origin += lateral_half
-        factor = blur_x([work[0:written, lanes] for lanes in columns], x_bands[1])
-        for p, lanes in enumerate(columns):
-            if sweep == 0:
-                before = joined[p, origin : origin + written, :]
-            else:
-                before = estimate[2 * lateral_half : 2 * lateral_half + written, lanes]
-            estimate[0:written, lanes] = before * factor[p]
+        quotients.append(blur_z(quotient, axial, True, order))
+    for lanes, values in zip(columns, zip(*quotients)):
+        near, far = edge[:, lanes], jnp.concatenate(values, axis=0)
+        work[0:16, lanes] = jnp.where(lower, far[0:16], near)
+        work[16:rows, lanes] = jnp.where(lower, far[16:], far[: rows - 16])
+        work[rows:read, lanes] = jnp.where(lower, near, far[rows - 16 :])
+    blur_y(work, y_bands[1], spans[1])
+    factor = blur_x([work[0:rows, lanes] for lanes in columns], x_bands[1])
+    at = jnp.where(lower, 0, held.shape[0])
+    others = jnp.where(lower, rows, 0)
+    estimate[pl.ds(pl.multiple_of(others, 16), held.shape[0]), :] = held[...]
+    for p, lanes in enumerate(columns):
+        value = border[p, 2 * lateral_half : 2 * lateral_half + rows, :] * factor[p]
+        estimate[pl.ds(pl.multiple_of(at, 16), rows), lanes] = value
+
+    read, written = spans[2][:2]
+    for lanes, value in zip(columns, blur_x([estimate[0:read, lanes] for lanes in columns], x_bands[0])):
+        work[0:read, lanes] = value
+    blur_y(work, y_bands[2], spans[2])
+
+    def replace(row, lanes, value):
+        work[row : row + GROUP, lanes] = value
+
+    quotient_along_z(work, joined, half - lateral_half, axial, order, written, replace)
+    blur_y(work, y_bands[3], spans[3])
+    factor = blur_x([work[0:out_rows, lanes] for lanes in columns], x_bands[1])
     voxels = 2 * LANES // blocks
     parts = LANES // voxels
     tall = out_rows // parts
     side = (LANES - LANES // 2) // 2
     lane = lax.broadcasted_iota(jnp.int32, (1, LANES), 1)
+    first = half - 2 * lateral_half
     for p, lanes in enumerate(columns):
+        value = estimate[first : first + out_rows, lanes] * factor[p]
         packed = None
         for m in range(parts):
-            piece = pltpu.roll(estimate[m * tall : (m + 1) * tall, lanes], (m * voxels - side) % LANES, 1)
+            piece = pltpu.roll(value[m * tall : (m + 1) * tall], (m * voxels - side) % LANES, 1)
             packed = piece if packed is None else jnp.where(lane < m * voxels, packed, piece)
         result[sent.index(order[p])] = packed
 
@@ -303,7 +296,7 @@
 
 def group_orders(planes):
     if planes == 8:
-        return [5, 1, 0, 2, 7, 4, 3, 6], [5, 1, 0, 2, 7, 4, 3, 6]
+        return [5, 0, 4, 7, 1, 3, 2, 6], [5, 1, 0, 4, 7, 2, 3, 6]
     return list(range(planes)), list(range(planes))
 
 
@@ -317,7 +310,8 @@
     lateral_half = lateral_taps.shape[1] // 2
     skipped = half - 2 * ITERS * lateral_half
     window_rows = row_count + 2 * half
-    spans = stages(row_count, half, lateral_half)
+    held_spans, border_spans, whole_spans = stages(row_count, half, skipped)
+    spans = held_spans + border_spans + whole_spans
     cores = [(i, i ^ 1) for i in range(tiles)]
     chips = [pair for i in range(1, tiles - 1, 2) for pair in ((i, i + 1), (i + 1, i))]
 
@@ -358,42 +352,44 @@
 
     across = lax.ppermute(windows[:, :half, :], "tile", cores)
     along_z, along_x, *along_y = bands
-    first, *rest = spans
-    spread = pl.pallas_call(
-        lambda *refs: first_kernel(*refs, span=first, lateral_half=lateral_half, order=order),
-        out_shape=jax.ShapeDtypeStruct((first[1], planes * LANES), jnp.float32),
-        in_specs=[in_vmem()] * 4,
-        out_specs=in_vmem(),
+    known = row_count + half
+    edge, held = pl.pallas_call(
+        lambda *refs: first_kernel(*refs, spans=held_spans, lateral_half=lateral_half, order=order),
+        out_shape=(
+            jax.ShapeDtypeStruct((16, planes * LANES), jnp.float32),
+            jax.ShapeDtypeStruct((held_spans[1][1], planes * LANES), jnp.float32),
+        ),
+        in_specs=[in_vmem()] * 5,
+        out_specs=(in_vmem(), in_vmem()),
         scratch_shapes=[
-            pltpu.VMEM((planes, first[0], LANES), jnp.float32),
-            pltpu.VMEM((first[0], planes * LANES), jnp.float32),
+            pltpu.VMEM((planes, known, LANES), jnp.float32),
+            pltpu.VMEM((known, planes * LANES), jnp.float32),
         ],
         cost_estimate=pl.CostEstimate(flops=1 << 29, bytes_accessed=1 << 20, transcendentals=0),
         compiler_params=params(),
         name="first",
-    )(windows, along_z, along_x, along_y[0])
+    )(windows, along_z, along_x, *along_y[:2])
     result = pl.pallas_call(
         lambda *refs: second_kernel(
             *refs,
-            spans=rest,
+            spans=border_spans + whole_spans,
             lateral_half=lateral_half,
-            skipped=skipped,
             blocks=blocks,
             order=order,
             sent=sent,
         ),
         out_shape=jax.ShapeDtypeStruct((planes, row_count * voxels // blocks // LANES, LANES), jnp.float32),
-        in_specs=[in_vmem()] * (5 + len(rest)),
+        in_specs=[in_vmem()] * 10,
         out_specs=in_vmem(),
         scratch_shapes=[
             pltpu.VMEM((planes, window_rows, LANES), jnp.float32),
-            pltpu.VMEM((planes, half + 16, LANES), jnp.float32),
-            pltpu.VMEM((window_rows - 16, planes * LANES), jnp.float32),
-            pltpu.VMEM((rest[1][1], planes * LANES), jnp.float32),
+            pltpu.VMEM((planes, row_count, LANES), jnp.float32),
+            pltpu.VMEM((known, planes * LANES), jnp.float32),
+            pltpu.VMEM((known, planes * LANES), jnp.float32),
         ],
         compiler_params=params(),
         name="second",
-    )(windows, across, spread, along_z, along_x, *along_y[1:])
+    )(windows, across, edge, held, along_z, along_x, *along_y[2:])
     received = lax.all_to_all(result, "plane", 0, 0, axis_index_groups=[sent], tiled=True)
     return pl.pallas_call(
         lambda *refs: unpack_kernel(*refs, blocks=blocks, order=order, sent=sent),

time: 35.3 us -> 35.2 us (level)
  starting transfers between devices: 5.62 us -> 5.24 us
  Pallas kernels: 5.84 us -> 6.2 us
    ppermute x1, starting transfers between devices: 4.45 us -> 4.07 us  [shards(): across = lax.ppermute(windows[:, :half, :], 'tile', cores)]
  transfers between devices with their start and end apart: 3 -> 3, of which waited for: 1 -> 0; matrix products, arithmetic and copies ran while one was open for 0% -> 0% of each run, Pallas kernels for 5% -> 6%
where the time goes in v7:
time: 35.2 us; the launch traced here: 34.9 us
  blocking collectives  22 us (62%)
  Pallas kernels  6.2 us (18%)
  starting transfers between devices  5.24 us (15%)
  between operations  1.39 us (4%)
    all_to_all x1, blocking collectives, shards(): lax.all_to_all(windows, 'plane', 0, 0, axis_index_groups=[order], tiled=T...  13.2 us
    all_to_all x1, blocking collectives, shards(): lax.all_to_all(result, 'plane', 0, 0, axis_index_groups=[sent], tiled=True)  8.81 us
    ppermute x1, starting transfers between devices, shards(): across = lax.ppermute(windows[:, :half, :], 'tile', cores)  4.07 us
    pallas_call x1, Pallas kernels, shards(): pl.pallas_call(lambda *refs: second_kernel(*refs, spans=border_spans + wh...  1.99 us
    pallas_call x1, Pallas kernels, shards(): pl.pallas_call(lambda *refs: first_kernel(*refs, spans=held_spans, latera...  1.16 us
    pallas_call x1, Pallas kernels, shards(): pl.pallas_call(lambda *refs: bands_kernel(*refs, spans=spans, blocks=bloc...  0.93 us
    pallas_call x1, Pallas kernels, shards(): pl.pallas_call(payload_kernel, out_shape=(payload, payload), in_specs=[pl...  0.91 us
    pallas_call x1, Pallas kernels, shards(): pl.pallas_call(lambda *refs: unpack_kernel(*refs, blocks=blocks, order=or...  0.76 us
  transfers between devices with their start and end apart: 3, of which 0 were waited for; matrix products, arithmetic and copies ran while one was open for 0% of the time, Pallas kernels for 6%

profile of v7, /device:TPU:0, one launch (start us, length us, event | category | flops | bytes accessed | tf_op | source)
XLA Modules:
  0.0 34.9 jit_solution(6448620975497183626)
XLA Ops:
  1.3 0.9 %payload.1 = (f32[2,1,64,256]{3,2,1,0:T(8,128)S(1)}, f32[2,1,64,256]{3,2,1,0:T(8,128)S(1)}) custom-call(f32[2,1,64,256]{3,2,1,0:T(8,128)} %own.1, f32[2,1,32,256]{3,2,1,0:T(8,128)} %strip.1, s32[1]{0:T(128)S(6)} %copy.7.extents, s32[1]{0:T(128)S(6)} %copy.8.skews), custom_call_target="tpu_custom_call" | custom-call | tf_op jit(solution)/shard_map/payload/pallas_call | solution.py:319
  2.2 0.0 copy-start.1
  2.2 0.0 copy-start
  2.2 0.5 %collective-permute-start = (f32[2,1,64,256]{3,2,1,0:T(8,128)S(1)}, f32[2,1,64,256]{3,2,1,0:T(8,128)S(1)}, u32[]{:S(2)}, u32[]{:S(2)}) collective-permute-start(f32[2,1,64,256]{3,2,1,0:T(8,128)S(1)} %get-tuple-element.17.refs_0_), channel_id=1, source_target_pairs={{0,8},{8,0},{16,24},{24,16},{1,9},{9,1},{17,25},{25,17},{2,10},{10... | collective-permute-start | bytes 393224 | tf_op jit(solution)/shard_map/ppermute | solution.py:329
  2.8 0.7 %collective-permute-start.1 = (f32[2,1,64,256]{3,2,1,0:T(8,128)S(1)}, f32[2,1,64,256]{3,2,1,0:T(8,128)S(1)}, u32[]{:S(2)}, u32[]{:S(2)}) collective-permute-start(f32[2,1,64,256]{3,2,1,0:T(8,128)S(1)} %get-tuple-element.18.refs_1_), channel_id=1, source_target_pairs={{8,16},{16,8},{9,17},{17,9},{10,18},{18,10},{11,19},{19,11},{12,20... | collective-permute-start | bytes 393224 | tf_op jit(solution)/shard_map/ppermute | solution.py:328
  3.4 0.0 copy-done.1
  3.4 0.0 copy-done
  3.4 0.9 %bands.1 = (f32[41,8,128]{2,1,0:T(8,128)S(1)}, bf16[2,256,256]{2,1,0:T(8,128)(2,1)S(1)}, bf16[160,192]{1,0:T(8,128)(2,1)S(1)}, bf16[128,160]{1,0:T(8,128)(2,1)S(...) custom-call(f32[2,41]{1,0:T(2,128)S(1)} %copy-done, ...), custom_call_target="tpu_custom_call" | custom-call | flops 1048576 | bytes 1048576 | tf_op jit(solution)/shard_map/bands/pallas_call | solution.py:330
  4.4 0.0 collective-permute-done.refs_2_
  4.4 0.0 collective-permute-done.1.refs_3_
  4.4 0.5 %pack.1 = f32[8,96,128]{2,1,0:T(8,128)S(1)} custom-call(f32[2,1,64,256]{3,2,1,0:T(8,128)S(1)} %get-tuple-element.17.refs_0_, f32[2,1,64,256]{3,2,1,0:T(8,128)S(1)} %get-tuple-element.18.refs_1_, f32[2,1,64,256]{3,2,1,0:T(8,128)S(1)} %collective-permute-done.refs_2_, f32[2,1,64,256]{3,2,1,0:T(8,128)S(1)} %collective-permute-done.1.refs_3_, ...), custom_call_target="tpu_custom_call" | custom-call | tf_op jit(solution)/shard_map/pack/pallas_call | solution.py:343
  4.9 13.2 %all_to_all.10.refs_0_ = f32[8,96,128]{2,1,0:T(8,128)S(1)} all-to-all(f32[8,96,128]{2,1,0:T(8,128)S(1)} %pack.1), channel_id=1, replica_groups={{5,0,4,7,1,3,2,6},{13,8,12,15,9,11,10,14},{21,16,20,23,17,19,18,22},{29..., dimensions={0} | all-to-all | bytes 786432 | tf_op jit(solution)/shard_map/all_to_all | solution.py:351
  18.1 4.1 %collective-permute-start.2 = (f32[8,32,128]{2,1,0:T(8,128)S(1)}, f32[8,32,128]{2,1,0:T(8,128)S(1)}, u32[]{:S(2)}, u32[]{:S(2)}) collective-permute-start(f32[8,32,128]{2,1,0:T(8,128)S(1)} %slice.4), channel_id=1, source_target_pairs={{0,8},{8,0},{16,24},{24,16},{1,9},{9,1},{17,25},{25,17},{2,10},{10... | collective-permute-start | bytes 393224 | tf_op jit(solution)/shard_map/ppermute | solution.py:353
  22.2 1.2 %first.1 = (f32[16,1024]{1,0:T(8,128)S(1)}, f32[64,1024]{1,0:T(8,128)S(1)}) custom-call(f32[8,96,128]{2,1,0:T(8,128)S(1)} %all_to_all.10.refs_0_, f32[41,8,128]{2,1,0:T(8,128)S(1)} %get-tuple-element.19.refs_4_.refs_1_, bf16[2,256,256]{2,1,0:T(8,128)(2,1)S(1)} %get-tuple-element.20.refs_2_.refs_5_, bf16[160,192]{1,0:T(8,128)(2,1)S(1)} %get-tuple-element.21.refs_3_, ...), custom_call_target="tpu_custom_call" | custom-call | flops 536870912 | bytes 1048576 | tf_op jit(solution)/shard_map/first/pallas_call | solution.py:356
  23.3 0.0 collective-permute-done.2.refs_1_
  23.3 2.0 %second.1 = f32[8,32,128]{2,1,0:T(8,128)S(1)} custom-call(f32[8,96,128]{2,1,0:T(8,128)S(1)} %all_to_all.10.refs_0_, f32[8,32,128]{2,1,0:T(8,128)S(1)} %collective-permute-done.2.refs_1_, f32[16,1024]{1,0:T(8,128)S(1)} %get-tuple-element.23.refs_2_, f32[64,1024]{1,0:T(8,128)S(1)} %get-tuple-element.24.refs_3_, ...), custom_call_target="tpu_custom_call" | custom-call | tf_op jit(solution)/shard_map/second/pallas_call | solution.py:372
  25.3 8.8 %all_to_all.11.refs_0_ = f32[8,32,128]{2,1,0:T(8,128)S(1)} all-to-all(f32[8,32,128]{2,1,0:T(8,128)S(1)} %second.1), channel_id=1, replica_groups={{5,1,0,4,7,2,3,6},{13,9,8,12,15,10,11,14},{21,17,16,20,23,18,19,22},{29..., dimensions={0} | all-to-all | bytes 262144 | tf_op jit(solution)/shard_map/all_to_all | solution.py:393
  34.1 0.8 %unpack.1 = f32[2,1,64,256]{3,2,1,0:T(8,128)} custom-call(f32[8,32,128]{2,1,0:T(8,128)S(1)} %all_to_all.11.refs_0_), custom_call_target="tpu_custom_call" | custom-call | tf_op jit(solution)/shard_map/unpack/pallas_call | solution.py:394
  (1 shorter events, 0.0 us)
Async XLA Ops:
  2.2 1.2 %copy-start.1 = (f32[2,15]{1,0:T(2,128)S(1)}, f32[2,15]{1,0:T(2,128)}, u32[]{:S(2)}) copy-start(f32[2,15]{1,0:T(2,128)} %refs_1_.1) | copy-start | bytes 364
  2.2 1.2 %copy-start = (f32[2,41]{1,0:T(2,128)S(1)}, f32[2,41]{1,0:T(2,128)}, u32[]{:S(2)}) copy-start(f32[2,41]{1,0:T(2,128)} %refs_0_.1) | copy-start | bytes 988
  2.2 2.1 %collective-permute-start = (f32[2,1,64,256]{3,2,1,0:T(8,128)S(1)}, f32[2,1,64,256]{3,2,1,0:T(8,128)S(1)}, u32[]{:S(2)}, u32[]{:S(2)}) collective-permute-start(f32[2,1,64,256]{3,2,1,0:T(8,128)S(1)} %get-tuple-element.17.refs_0_), channel_id=1, source_target_pairs={{0,8},{8,0},{16,24},{24,16},{1,9},{9,1},{17,25},{25,17},{2,10},{10... | collective-permute-start | bytes 393224 | tf_op jit(solution)/shard_map/ppermute | solution.py:329
  2.8 1.6 %collective-permute-start.1 = (f32[2,1,64,256]{3,2,1,0:T(8,128)S(1)}, f32[2,1,64,256]{3,2,1,0:T(8,128)S(1)}, u32[]{:S(2)}, u32[]{:S(2)}) collective-permute-start(f32[2,1,64,256]{3,2,1,0:T(8,128)S(1)} %get-tuple-element.18.refs_1_), channel_id=1, source_target_pairs={{8,16},{16,8},{9,17},{17,9},{10,18},{18,10},{11,19},{19,11},{12,20... | collective-permute-start | bytes 393224 | tf_op jit(solution)/shard_map/ppermute | solution.py:328
  18.1 5.2 %collective-permute-start.2 = (f32[8,32,128]{2,1,0:T(8,128)S(1)}, f32[8,32,128]{2,1,0:T(8,128)S(1)}, u32[]{:S(2)}, u32[]{:S(2)}) collective-permute-start(f32[8,32,128]{2,1,0:T(8,128)S(1)} %slice.4), channel_id=1, source_target_pairs={{0,8},{8,0},{16,24},{24,16},{1,9},{9,1},{17,25},{25,17},{2,10},{10... | collective-permute-start | bytes 393224 | tf_op jit(solution)/shard_map/ppermute | solution.py:353

commit v8 on v3

--- a/solution.py
+++ b/solution.py
@@ -23,37 +23,38 @@
     return pl.BlockSpec(memory_space=pltpu.SMEM)
 
 
-def payload_kernel(facts, own, strip, to_core, to_chip, sems):
+def payload_kernel(own, strip, extents, skews, to_core, to_chip, sems):
     strip_rows = strip.shape[2]
+    tile = lax.axis_index("tile")
     low, high = slice(0, strip_rows), slice(strip_rows, 2 * strip_rows)
 
     def fill(up, down):
-        copies = []
+        pieces = []
         for c in range(strip.shape[0]):
-            pieces = (
+            pieces += [
                 (strip.at[c], up.at[c, :, low, :]),
                 (own.at[c, :, own.shape[2] - strip_rows :, :], up.at[c, :, high, :]),
                 (own.at[c, :, low, :], down.at[c, :, low, :]),
-            )
-            for source, target in pieces:
-                copies.append(pltpu.make_async_copy(source, target, sems.at[len(copies)]))
+            ]
+        copies = [pltpu.make_async_copy(source, target, sems.at[i]) for i, (source, target) in enumerate(pieces)]
         for copy in copies:
             copy.start()
+        extent = jnp.where(tile == 0, 0, extents[0])
         column = lax.broadcasted_iota(jnp.int32, strip.shape, 3)
-        down[:, :, high, :] = jnp.where(column < LANES, facts[1], facts[2]).astype(jnp.float32)
+        down[:, :, high, :] = jnp.where(column < LANES, extent, skews[0]).astype(jnp.float32)
         for copy in copies:
             copy.wait()
 
-    @pl.when(facts[0] == 1)
+    @pl.when(tile % 2 == 1)
     def _():
         fill(to_chip, to_core)
 
-    @pl.when(facts[0] == 0)
+    @pl.when(tile % 2 == 0)
     def _():
         fill(to_core, to_chip)
 
 
-def pack_kernel(facts, to_core, to_chip, core, chip, windows, rows, *, reach, blocks, row_blocks):
+def pack_kernel(to_core, to_chip, core, chip, _, windows, rows, *, reach, blocks, row_blocks):
     chans, _, row_count, voxels = core.shape
     strip_rows = row_count // 2
     lane = lax.broadcasted_iota(jnp.int32, (1, LANES), 1)
@@ -61,19 +62,23 @@
     edge = LANES // 4
     block_rows = row_count // row_blocks
     window_rows = block_rows + 2 * reach
-    lower = facts[0] == 1
+    lower = lax.axis_index("tile") % 2 == 1
 
     def pick(low, high, c, part):
         at = slice(part * strip_rows, (part + 1) * strip_rows)
         return jnp.where(lower, low[c, 0, at, :], high[c, 0, at, :])
 
-    numbers = pick(chip, core, 0, 1)[0:GROUP].astype(jnp.int32)
-    next_extent, next_skew = jnp.max(numbers[:, :LANES]), jnp.max(numbers[:, LANES:])
+    def numbers(low, high):
+        both = pick(low, high, 0, 1)[0:GROUP].astype(jnp.int32)
+        return jnp.max(both[:, :LANES]), jnp.max(both[:, LANES:])
+
+    extent, skew = numbers(to_core, to_chip)
+    next_extent, next_skew = numbers(chip, core)
     for c in range(chans):
         rows[c, 0:reach, :] = pick(core, chip, c, 1)[strip_rows - reach :]
-        turned = pltpu.roll(pick(core, chip, c, 0), facts[2], 1)
+        turned = pltpu.roll(pick(core, chip, c, 0), skew, 1)
         top = pick(to_core, to_chip, c, 0)
-        rows[c, reach : reach + strip_rows, :] = jnp.where(tall < facts[1], 0.5 * (top + turned), top)
+        rows[c, reach : reach + strip_rows, :] = jnp.where(tall < extent, 0.5 * (top + turned), top)
         rows[c, reach + strip_rows : reach + row_count, :] = pick(to_chip, to_core, c, 1)
         turned = pltpu.roll(pick(to_chip, to_core, c, 0), next_skew, 1)
         top = pick(chip, core, c, 0)
@@ -112,11 +117,15 @@
     ]
 
 
-def bands_kernel(chan, axial, lateral, along_z, along_x, *along_y, spans):
+def bands_kernel(axial, lateral, along_z, along_x, *along_y, spans, share, order):
     width = lateral.shape[1]
-    taps = [lateral[chan[0], j] for j in range(width)]
+    plane = lax.axis_index("plane")
+    chan = jnp.int32(0)
+    for place, owner in enumerate(order):
+        chan = jnp.where(plane == owner, place // share, chan)
+    taps = [lateral[chan, j] for j in range(width)]
     for j in range(axial.shape[1]):
-        along_z[j] = jnp.full((GROUP, LANES), axial[chan[0], j], jnp.float32)
+        along_z[j] = jnp.full((GROUP, LANES), axial[chan, j], jnp.float32)
     offset = lax.broadcasted_iota(jnp.int32, (LANES, LANES), 0) - lax.broadcasted_iota(jnp.int32, (LANES, LANES), 1)
 
     def band(order, where, first):
@@ -140,7 +149,7 @@
             along_y[k][written:] = jnp.concatenate([bottom, jnp.zeros_like(bottom)], axis=1)
 
 
-def deconvolve_kernel(windows, axial, x_bands, *refs, spans, lateral_half, out_rows):
+def deconvolve_kernel(windows, axial, x_bands, *refs, spans, lateral_half, out_rows, order, sent):
     y_bands, (result, blurred, estimate) = refs[: len(spans)], refs[len(spans) :]
     planes, window_rows, _ = windows.shape
     axial_half = axial.shape[0] // 2
@@ -168,7 +177,7 @@
         for p in range(planes):
             total = None
             for q in range(planes):
-                at = (p - q if flipped else q - p) + axial_half
+                at = (order[p] - order[q] if flipped else order[q] - order[p]) + axial_half
                 if 0 <= at < 2 * axial_half + 1:
                     term = axial[at] * values[q]
                     total = term if total is None else total + term
@@ -213,10 +222,10 @@
     for p in range(planes):
         first = pltpu.roll(estimate[0:half, columns[p]], LANES - side, 1)
         second = pltpu.roll(estimate[half:out_rows, columns[p]], side, 1)
-        result[p] = jnp.where(lane < LANES // 2, first, second)
-
-
-def unpack_kernel(received, out, *, blocks, row_blocks):
+        result[sent.index(order[p])] = jnp.where(lane < LANES // 2, first, second)
+
+
+def unpack_kernel(received, out, *, blocks, row_blocks, order, sent):
     chans, _, row_count, voxels = out.shape
     half = received.shape[1]
     lane = lax.broadcasted_iota(jnp.int32, (1, LANES), 1)
@@ -224,11 +233,17 @@
         for b in range(row_blocks):
             for pair in range(blocks // 2):
                 at = (c * row_blocks + b) * blocks + 2 * pair
-                even, odd = received[at], received[at + 1]
+                even, odd = received[sent.index(order[at])], received[sent.index(order[at + 1])]
                 row = b * 2 * half
                 columns = slice(pair * LANES, (pair + 1) * LANES)
                 out[c, 0, row : row + half, columns] = jnp.where(lane < LANES // 2, even, pltpu.roll(odd, LANES // 2, 1))
                 out[c, 0, row + half : row + 2 * half, columns] = jnp.where(lane < LANES // 2, pltpu.roll(even, LANES // 2, 1), odd)
+
+
+def group_orders(planes):
+    if planes == 8:
+        return [5, 0, 4, 7, 1, 3, 2, 6], [5, 1, 0, 4, 7, 2, 3, 6]
+    return list(range(planes)), list(range(planes))
 
 
 def shards(observed, intersection_strip, axial_taps, lateral_taps, extents, section_skews):
@@ -236,6 +251,7 @@
     strip_rows = intersection_strip.shape[2]
     planes = lax.axis_size("plane")
     tiles = lax.axis_size("tile")
+    order, sent = group_orders(planes)
     lateral_half = lateral_taps.shape[1] // 2
     reach = 2 * ITERS * lateral_half
     blocks = voxels // (LANES // 2)
@@ -245,48 +261,45 @@
     cores = [(i, i ^ 1) for i in range(tiles)]
     chips = [pair for i in range(1, tiles - 1, 2) for pair in ((i, i + 1), (i + 1, i))]
 
-    tile = lax.axis_index("tile")
-    facts = jnp.stack([tile % 2, jnp.where(tile == 0, 0, extents[0]), section_skews[0]]).astype(jnp.int32)
     payload = jax.ShapeDtypeStruct((chans, 1, 2 * strip_rows, voxels), jnp.float32)
     to_core, to_chip = pl.pallas_call(
         payload_kernel,
         out_shape=(payload, payload),
-        in_specs=[in_smem(), pl.BlockSpec(memory_space=pltpu.HBM), pl.BlockSpec(memory_space=pltpu.HBM)],
+        in_specs=[pl.BlockSpec(memory_space=pltpu.HBM)] * 2 + [in_smem()] * 2,
         out_specs=(in_vmem(), in_vmem()),
         scratch_shapes=[pltpu.SemaphoreType.DMA((3 * chans,))],
         compiler_params=params(),
         name="payload",
-    )(facts, pltpu.with_memory_space_constraint(observed, pltpu.HBM), pltpu.with_memory_space_constraint(intersection_strip, pltpu.HBM))
+    )(*(pltpu.with_memory_space_constraint(array, pltpu.HBM) for array in (observed, intersection_strip)), extents, section_skews)
     chip = lax.ppermute(to_chip, "tile", chips)
     core = lax.ppermute(to_core, "tile", cores)
-    windows = pl.pallas_call(
-        lambda *refs: pack_kernel(*refs, reach=reach, blocks=blocks, row_blocks=row_blocks),
-        out_shape=jax.ShapeDtypeStruct((planes, window_rows, LANES), jnp.float32),
-        in_specs=[in_smem()] + [in_vmem()] * 4,
-        out_specs=in_vmem(),
-        scratch_shapes=[pltpu.VMEM((chans, row_count + 2 * reach, voxels), jnp.float32)],
-        compiler_params=params(),
-        name="pack",
-    )(facts, to_core, to_chip, core, chip)
-    windows = lax.all_to_all(windows, "plane", 0, 0, tiled=True)
-
-    channel = (lax.axis_index("plane") // (planes // chans)).astype(jnp.int32).reshape(1)
     spans = stages(window_rows, lateral_half)
     bands = pl.pallas_call(
-        lambda *refs: bands_kernel(*refs, spans=spans),
+        lambda *refs: bands_kernel(*refs, spans=spans, share=planes // chans, order=order),
         out_shape=[
             jax.ShapeDtypeStruct((axial_taps.shape[1], GROUP, LANES), jnp.float32),
             jax.ShapeDtypeStruct((2, 2 * LANES, 2 * LANES), jnp.bfloat16),
         ]
         + [jax.ShapeDtypeStruct((2 * written, 2 * read), jnp.bfloat16) for read, written in spans],
-        in_specs=[in_smem()] * 3,
+        in_specs=[in_smem()] * 2,
         out_specs=[in_vmem()] * (2 + len(spans)),
         cost_estimate=pl.CostEstimate(flops=1 << 20, bytes_accessed=1 << 20, transcendentals=0),
         compiler_params=params(),
         name="bands",
-    )(channel, axial_taps, lateral_taps)
+    )(axial_taps, lateral_taps)
+    windows = pl.pallas_call(
+        lambda *refs: pack_kernel(*refs, reach=reach, blocks=blocks, row_blocks=row_blocks),
+        out_shape=jax.ShapeDtypeStruct((planes, window_rows, LANES), jnp.float32),
+        in_specs=[in_vmem()] * 4 + [pl.BlockSpec(memory_space=pl.ANY)],
+        out_specs=in_vmem(),
+        scratch_shapes=[pltpu.VMEM((chans, row_count + 2 * reach, voxels), jnp.float32)],
+        compiler_params=params(),
+        name="pack",
+    )(to_core, to_chip, core, chip, bands[0])
+    windows = lax.all_to_all(windows, "plane", 0, 0, axis_index_groups=[order], tiled=True)
+
     result = pl.pallas_call(
-        lambda *refs: deconvolve_kernel(*refs, spans=spans, lateral_half=lateral_half, out_rows=out_rows),
+        lambda *refs: deconvolve_kernel(*refs, spans=spans, lateral_half=lateral_half, out_rows=out_rows, order=order, sent=sent),
         out_shape=jax.ShapeDtypeStruct((planes, out_rows // 2, LANES), jnp.float32),
         in_specs=[in_vmem()] * (3 + len(spans)),
         out_specs=in_vmem(),
@@ -297,9 +310,9 @@
         compiler_params=params(),
         name="deconvolve",
     )(windows, *bands)
-    received = lax.all_to_all(result, "plane", 0, 0, tiled=True)
+    received = lax.all_to_all(result, "plane", 0, 0, axis_index_groups=[sent], tiled=True)
     return pl.pallas_call(
-        lambda *refs: unpack_kernel(*refs, blocks=blocks, row_blocks=row_blocks),
+        lambda *refs: unpack_kernel(*refs, blocks=blocks, row_blocks=row_blocks, order=order, sent=sent),
         out_shape=jax.ShapeDtypeStruct(observed.shape, jnp.float32),
         in_specs=[in_vmem()],
         out_specs=in_vmem(),

time: 42 us -> 34.8 us (0.83)
  the two profiles are of different devices: /device:TPU:0 before, /device:TPU:6 now
where the time goes in v8:
time: 34.8 us; the launch traced here: 34.5 us
  blocking collectives  22.2 us (64%)
  Pallas kernels  5.43 us (16%)
  waiting for transfers between devices  2.87 us (8%)
  starting transfers between devices  2.58 us (7%)
  between operations  1.39 us (4%)
    all_to_all x1, blocking collectives, shards(): lax.all_to_all(windows, 'plane', 0, 0, axis_index_groups=[order], tiled=T...  13.4 us
    all_to_all x1, blocking collectives, shards(): lax.all_to_all(result, 'plane', 0, 0, axis_index_groups=[sent], tiled=True)  8.8 us
    ppermute x1, waiting for transfers between devices, shards(): chip = lax.ppermute(to_chip, 'tile', chips)  2.87 us
    ppermute x1, starting transfers between devices, shards(): chip = lax.ppermute(to_chip, 'tile', chips)  2.5 us
    pallas_call x1, Pallas kernels, shards(): pl.pallas_call(lambda *refs: deconvolve_kernel(*refs, spans=spans, latera...  2.45 us
    pallas_call x1, Pallas kernels, shards(): pl.pallas_call(payload_kernel, out_shape=(payload, payload), in_specs=[pl...  0.91 us
    pallas_call x1, Pallas kernels, shards(): pl.pallas_call(lambda *refs: bands_kernel(*refs, spans=spans, share=plane...  0.87 us
    pallas_call x1, Pallas kernels, shards(): pl.pallas_call(lambda *refs: unpack_kernel(*refs, blocks=blocks, row_bloc...  0.76 us
  transfers between devices with their start and end apart: 2, of which 1 were waited for; matrix products, arithmetic and copies ran while one was open for 0% of the time, Pallas kernels for 3%

profile of v8, /device:TPU:6, one launch (start us, length us, event | category | flops | bytes accessed | tf_op | source)
XLA Modules:
  0.0 34.5 jit_solution(8070704669659762863)
XLA Ops:
  1.3 0.9 %payload.1 = (f32[2,1,64,256]{3,2,1,0:T(8,128)S(1)}, f32[2,1,64,256]{3,2,1,0:T(8,128)S(1)}) custom-call(f32[2,1,64,256]{3,2,1,0:T(8,128)} %own.1, f32[2,1,32,256]{3,2,1,0:T(8,128)} %strip.1, s32[1]{0:T(128)S(6)} %copy.7.extents, s32[1]{0:T(128)S(6)} %copy.8.skews), custom_call_target="tpu_custom_call" | custom-call | tf_op jit(solution)/shard_map/payload/pallas_call | solution.py:265
  2.2 0.0 copy-start.1
  2.2 0.0 copy-start
  2.2 0.1 collective-permute-start
  2.3 2.5 %collective-permute-start.1 = (f32[2,1,64,256]{3,2,1,0:T(8,128)S(1)}, f32[2,1,64,256]{3,2,1,0:T(8,128)S(1)}, u32[]{:S(2)}, u32[]{:S(2)}) collective-permute-start(f32[2,1,64,256]{3,2,1,0:T(8,128)S(1)} %get-tuple-element.14.refs_1_), channel_id=1, source_target_pairs={{8,16},{16,8},{9,17},{17,9},{10,18},{18,10},{11,19},{19,11},{12,20... | collective-permute-start | bytes 393224 | tf_op jit(solution)/shard_map/ppermute | solution.py:274
  4.8 0.0 copy-done.1
  4.8 0.0 copy-done
  4.9 0.9 %bands.1 = (f32[41,8,128]{2,1,0:T(8,128)S(1)}, bf16[2,256,256]{2,1,0:T(8,128)(2,1)S(1)}, bf16[224,256]{1,0:T(8,128)(2,1)S(1)}, bf16[192,224]{1,0:T(8,128)(2,1)S(...) custom-call(f32[2,41]{1,0:T(2,128)S(1)} %copy-done, f32[2,15]{1,0:T(2,128)S(1)} %copy-done.1), custom_call_target="tpu_custom_call" | custom-call | flops 1048576 | bytes 1048576 | tf_op jit(solution)/shard_map/bands/pallas_call | solution.py:277
  5.7 0.0 collective-permute-done.refs_2_
  5.7 2.9 %collective-permute-done.1.refs_3_ = f32[2,1,64,256]{3,2,1,0:T(8,128)S(1)} collective-permute-done((f32[2,1,64,256]{3,2,1,0:T(8,128)S(1)}, f32[2,1,64,256]{3,2,1,0:T(8,128)S(1)}, u32[]{:S(2)}, u32[]{:S(2)}) %collective-permute-start.1) | collective-permute-done | bytes 131104 | tf_op jit(solution)/shard_map/ppermute | solution.py:274
  8.6 0.4 %pack.1 = f32[8,120,128]{2,1,0:T(8,128)S(1)} custom-call(f32[2,1,64,256]{3,2,1,0:T(8,128)S(1)} %get-tuple-element.13.refs_0_, f32[2,1,64,256]{3,2,1,0:T(8,128)S(1)} %get-tuple-element.14.refs_1_, f32[2,1,64,256]{3,2,1,0:T(8,128)S(1)} %collective-permute-done.refs_2_, f32[2,1,64,256]{3,2,1,0:T(8,128)S(1)} %collective-permute-done.1.refs_3_, ...), custom_call_target="tpu_custom_call" | custom-call | tf_op jit(solution)/shard_map/pack/pallas_call | solution.py:290
  9.1 13.4 %all_to_all.10.refs_0_ = f32[8,120,128]{2,1,0:T(8,128)S(1)} all-to-all(f32[8,120,128]{2,1,0:T(8,128)S(1)} %pack.1), channel_id=1, replica_groups={{5,0,4,7,1,3,2,6},{13,8,12,15,9,11,10,14},{21,16,20,23,17,19,18,22},{29..., dimensions={0} | all-to-all | bytes 983040 | tf_op jit(solution)/shard_map/all_to_all | solution.py:299
  22.5 2.4 %deconvolve.1 = f32[8,32,128]{2,1,0:T(8,128)S(1)} custom-call(f32[8,120,128]{2,1,0:T(8,128)S(1)} %all_to_all.10.refs_0_, f32[41,8,128]{2,1,0:T(8,128)S(1)} %get-tuple-element.15.refs_4_.refs_1_, bf16[2,256,256]{2,1,0:T(8,128)(2,1)S(1)} %get-tuple-element.16.refs_2_, bf16[224,256]{1,0:T(8,128)(2,1)S(1)} %get-tuple-element.17.refs_3_, ...), custom_call_target="tpu_custom_call" | custom-call | tf_op jit(solution)/shard_map/deconvolve/pallas_call | solution.py:301
  24.9 8.8 %all_to_all.11.refs_0_ = f32[8,32,128]{2,1,0:T(8,128)S(1)} all-to-all(f32[8,32,128]{2,1,0:T(8,128)S(1)} %deconvolve.1), channel_id=1, replica_groups={{5,1,0,4,7,2,3,6},{13,9,8,12,15,10,11,14},{21,17,16,20,23,18,19,22},{29..., dimensions={0} | all-to-all | bytes 262144 | tf_op jit(solution)/shard_map/all_to_all | solution.py:313
  33.7 0.8 %unpack.1 = f32[2,1,64,256]{3,2,1,0:T(8,128)} custom-call(f32[8,32,128]{2,1,0:T(8,128)S(1)} %all_to_all.11.refs_0_), custom_call_target="tpu_custom_call" | custom-call | tf_op jit(solution)/shard_map/unpack/pallas_call | solution.py:314
Async XLA Ops:
  2.2 2.6 %copy-start.1 = (f32[2,15]{1,0:T(2,128)S(1)}, f32[2,15]{1,0:T(2,128)}, u32[]{:S(2)}) copy-start(f32[2,15]{1,0:T(2,128)} %refs_1_.1) | copy-start | bytes 364
  2.2 2.6 %copy-start = (f32[2,41]{1,0:T(2,128)S(1)}, f32[2,41]{1,0:T(2,128)}, u32[]{:S(2)}) copy-start(f32[2,41]{1,0:T(2,128)} %refs_0_.1) | copy-start | bytes 988
  2.2 3.5 %collective-permute-start = (f32[2,1,64,256]{3,2,1,0:T(8,128)S(1)}, f32[2,1,64,256]{3,2,1,0:T(8,128)S(1)}, u32[]{:S(2)}, u32[]{:S(2)}) collective-permute-start(f32[2,1,64,256]{3,2,1,0:T(8,128)S(1)} %get-tuple-element.13.refs_0_), channel_id=1, source_target_pairs={{0,8},{8,0},{16,24},{24,16},{1,9},{9,1},{17,25},{25,17},{2,10},{10... | collective-permute-start | bytes 393224 | tf_op jit(solution)/shard_map/ppermute | solution.py:275
  2.3 6.3 %collective-permute-start.1 = (f32[2,1,64,256]{3,2,1,0:T(8,128)S(1)}, f32[2,1,64,256]{3,2,1,0:T(8,128)S(1)}, u32[]{:S(2)}, u32[]{:S(2)}) collective-permute-start(f32[2,1,64,256]{3,2,1,0:T(8,128)S(1)} %get-tuple-element.14.refs_1_), channel_id=1, source_target_pairs={{8,16},{16,8},{9,17},{17,9},{10,18},{18,10},{11,19},{19,11},{12,20... | collective-permute-start | bytes 393224 | tf_op jit(solution)/shard_map/ppermute | solution.py:274

commit v9 on v8

--- a/solution.py
+++ b/solution.py
@@ -156,21 +156,17 @@
     columns = [slice(q * LANES, (q + 1) * LANES) for q in range(planes)]
 
     def along_x(values, which):
-        out = []
-        for q in range(0, planes, 2):
-            pair = jnp.concatenate(values[q : q + 2], axis=0)
-            product = jnp.dot(jnp.concatenate(split(pair), axis=1), x_bands[which], preferred_element_type=jnp.float32)
-            product = product[:, :LANES] + product[:, LANES:]
-            out += [product[: pair.shape[0] // 2], product[pair.shape[0] // 2 :]]
-        return out
+        rows = values[0].shape[0]
+        both = jnp.concatenate(split(jnp.concatenate(values, axis=0)), axis=1)
+        product = jnp.dot(both, x_bands[which], preferred_element_type=jnp.float32)
+        product = product[:, :LANES] + product[:, LANES:]
+        return [product[q * rows : (q + 1) * rows] for q in range(planes)]
 
     def along_y(k):
         read, written = spans[k]
-        for q in range(0, planes, 2):
-            pair = slice(q * LANES, (q + 2) * LANES)
-            both = jnp.concatenate(split(blurred[0:read, pair]), axis=0)
-            product = jnp.dot(y_bands[k][...], both, preferred_element_type=jnp.float32)
-            blurred[0:written, pair] = product[:written] + product[written:]
+        both = jnp.concatenate(split(blurred[0:read, :]), axis=0)
+        product = jnp.dot(y_bands[k][...], both, preferred_element_type=jnp.float32)
+        blurred[0:written, :] = product[:written] + product[written:]
 
     def along_z(values, flipped):
         out = []
@@ -242,7 +238,7 @@
 
 def group_orders(planes):
     if planes == 8:
-        return [5, 0, 4, 7, 1, 3, 2, 6], [5, 1, 0, 4, 7, 2, 3, 6]
+        return [5, 0, 4, 7, 3, 1, 2, 6], [5, 1, 0, 4, 7, 2, 3, 6]
     return list(range(planes)), list(range(planes))
 
 

time: 34.8 us -> 34.8 us (level)
  no operation moved by 1% of the time
where the time goes in v9:
time: 34.8 us; the launch traced here: 34.5 us
  blocking collectives  22.2 us (64%)
  Pallas kernels  5.46 us (16%)
  waiting for transfers between devices  2.87 us (8%)
  starting transfers between devices  2.58 us (7%)
  between operations  1.39 us (4%)
    all_to_all x1, blocking collectives, shards(): lax.all_to_all(windows, 'plane', 0, 0, axis_index_groups=[order], tiled=T...  13.1 us
    all_to_all x1, blocking collectives, shards(): lax.all_to_all(result, 'plane', 0, 0, axis_index_groups=[sent], tiled=True)  9.11 us
    ppermute x1, waiting for transfers between devices, shards(): chip = lax.ppermute(to_chip, 'tile', chips)  2.87 us
    ppermute x1, starting transfers between devices, shards(): chip = lax.ppermute(to_chip, 'tile', chips)  2.5 us
    pallas_call x1, Pallas kernels, shards(): pl.pallas_call(lambda *refs: deconvolve_kernel(*refs, spans=spans, latera...  2.48 us
    pallas_call x1, Pallas kernels, shards(): pl.pallas_call(payload_kernel, out_shape=(payload, payload), in_specs=[pl...  0.91 us
    pallas_call x1, Pallas kernels, shards(): pl.pallas_call(lambda *refs: bands_kernel(*refs, spans=spans, share=plane...  0.87 us
    pallas_call x1, Pallas kernels, shards(): pl.pallas_call(lambda *refs: unpack_kernel(*refs, blocks=blocks, row_bloc...  0.76 us
  transfers between devices with their start and end apart: 2, of which 1 were waited for; matrix products, arithmetic and copies ran while one was open for 0% of the time, Pallas kernels for 3%

profile of v9, /device:TPU:6, one launch (start us, length us, event | category | flops | bytes accessed | tf_op | source)
XLA Modules:
  0.0 34.5 jit_solution(10403700992223480751)
XLA Ops:
  1.3 0.9 %payload.1 = (f32[2,1,64,256]{3,2,1,0:T(8,128)S(1)}, f32[2,1,64,256]{3,2,1,0:T(8,128)S(1)}) custom-call(f32[2,1,64,256]{3,2,1,0:T(8,128)} %own.1, f32[2,1,32,256]{3,2,1,0:T(8,128)} %strip.1, s32[1]{0:T(128)S(6)} %copy.7.extents, s32[1]{0:T(128)S(6)} %copy.8.skews), custom_call_target="tpu_custom_call" | custom-call | tf_op jit(solution)/shard_map/payload/pallas_call | solution.py:261
  2.2 0.0 copy-start.1
  2.2 0.0 copy-start
  2.2 0.1 collective-permute-start
  2.3 2.5 %collective-permute-start.1 = (f32[2,1,64,256]{3,2,1,0:T(8,128)S(1)}, f32[2,1,64,256]{3,2,1,0:T(8,128)S(1)}, u32[]{:S(2)}, u32[]{:S(2)}) collective-permute-start(f32[2,1,64,256]{3,2,1,0:T(8,128)S(1)} %get-tuple-element.14.refs_1_), channel_id=1, source_target_pairs={{8,16},{16,8},{9,17},{17,9},{10,18},{18,10},{11,19},{19,11},{12,20... | collective-permute-start | bytes 393224 | tf_op jit(solution)/shard_map/ppermute | solution.py:270
  4.8 0.0 copy-done.1
  4.8 0.0 copy-done
  4.9 0.9 %bands.1 = (f32[41,8,128]{2,1,0:T(8,128)S(1)}, bf16[2,256,256]{2,1,0:T(8,128)(2,1)S(1)}, bf16[224,256]{1,0:T(8,128)(2,1)S(1)}, bf16[192,224]{1,0:T(8,128)(2,1)S(...) custom-call(f32[2,41]{1,0:T(2,128)S(1)} %copy-done, f32[2,15]{1,0:T(2,128)S(1)} %copy-done.1), custom_call_target="tpu_custom_call" | custom-call | flops 1048576 | bytes 1048576 | tf_op jit(solution)/shard_map/bands/pallas_call | solution.py:273
  5.7 0.0 collective-permute-done.refs_2_
  5.7 2.9 %collective-permute-done.1.refs_3_ = f32[2,1,64,256]{3,2,1,0:T(8,128)S(1)} collective-permute-done((f32[2,1,64,256]{3,2,1,0:T(8,128)S(1)}, f32[2,1,64,256]{3,2,1,0:T(8,128)S(1)}, u32[]{:S(2)}, u32[]{:S(2)}) %collective-permute-start.1) | collective-permute-done | bytes 131104 | tf_op jit(solution)/shard_map/ppermute | solution.py:270
  8.6 0.4 %pack.1 = f32[8,120,128]{2,1,0:T(8,128)S(1)} custom-call(f32[2,1,64,256]{3,2,1,0:T(8,128)S(1)} %get-tuple-element.13.refs_0_, f32[2,1,64,256]{3,2,1,0:T(8,128)S(1)} %get-tuple-element.14.refs_1_, f32[2,1,64,256]{3,2,1,0:T(8,128)S(1)} %collective-permute-done.refs_2_, f32[2,1,64,256]{3,2,1,0:T(8,128)S(1)} %collective-permute-done.1.refs_3_, ...), custom_call_target="tpu_custom_call" | custom-call | tf_op jit(solution)/shard_map/pack/pallas_call | solution.py:286
  9.1 13.1 %all_to_all.10.refs_0_ = f32[8,120,128]{2,1,0:T(8,128)S(1)} all-to-all(f32[8,120,128]{2,1,0:T(8,128)S(1)} %pack.1), channel_id=1, replica_groups={{5,0,4,7,3,1,2,6},{13,8,12,15,11,9,10,14},{21,16,20,23,19,17,18,22},{29..., dimensions={0} | all-to-all | bytes 983040 | tf_op jit(solution)/shard_map/all_to_all | solution.py:295
  22.2 2.5 %deconvolve.1 = f32[8,32,128]{2,1,0:T(8,128)S(1)} custom-call(f32[8,120,128]{2,1,0:T(8,128)S(1)} %all_to_all.10.refs_0_, f32[41,8,128]{2,1,0:T(8,128)S(1)} %get-tuple-element.15.refs_4_.refs_1_, bf16[2,256,256]{2,1,0:T(8,128)(2,1)S(1)} %get-tuple-element.16.refs_2_, bf16[224,256]{1,0:T(8,128)(2,1)S(1)} %get-tuple-element.17.refs_3_, ...), custom_call_target="tpu_custom_call" | custom-call | tf_op jit(solution)/shard_map/deconvolve/pallas_call | solution.py:297
  24.6 9.1 %all_to_all.11.refs_0_ = f32[8,32,128]{2,1,0:T(8,128)S(1)} all-to-all(f32[8,32,128]{2,1,0:T(8,128)S(1)} %deconvolve.1), channel_id=1, replica_groups={{5,1,0,4,7,2,3,6},{13,9,8,12,15,10,11,14},{21,17,16,20,23,18,19,22},{29..., dimensions={0} | all-to-all | bytes 262144 | tf_op jit(solution)/shard_map/all_to_all | solution.py:309
  33.8 0.8 %unpack.1 = f32[2,1,64,256]{3,2,1,0:T(8,128)} custom-call(f32[8,32,128]{2,1,0:T(8,128)S(1)} %all_to_all.11.refs_0_), custom_call_target="tpu_custom_call" | custom-call | tf_op jit(solution)/shard_map/unpack/pallas_call | solution.py:310
Async XLA Ops:
  2.2 2.6 %copy-start.1 = (f32[2,15]{1,0:T(2,128)S(1)}, f32[2,15]{1,0:T(2,128)}, u32[]{:S(2)}) copy-start(f32[2,15]{1,0:T(2,128)} %refs_1_.1) | copy-start | bytes 364
  2.2 2.6 %copy-start = (f32[2,41]{1,0:T(2,128)S(1)}, f32[2,41]{1,0:T(2,128)}, u32[]{:S(2)}) copy-start(f32[2,41]{1,0:T(2,128)} %refs_0_.1) | copy-start | bytes 988
  2.2 3.5 %collective-permute-start = (f32[2,1,64,256]{3,2,1,0:T(8,128)S(1)}, f32[2,1,64,256]{3,2,1,0:T(8,128)S(1)}, u32[]{:S(2)}, u32[]{:S(2)}) collective-permute-start(f32[2,1,64,256]{3,2,1,0:T(8,128)S(1)} %get-tuple-element.13.refs_0_), channel_id=1, source_target_pairs={{0,8},{8,0},{16,24},{24,16},{1,9},{9,1},{17,25},{25,17},{2,10},{10... | collective-permute-start | bytes 393224 | tf_op jit(solution)/shard_map/ppermute | solution.py:271
  2.3 6.3 %collective-permute-start.1 = (f32[2,1,64,256]{3,2,1,0:T(8,128)S(1)}, f32[2,1,64,256]{3,2,1,0:T(8,128)S(1)}, u32[]{:S(2)}, u32[]{:S(2)}) collective-permute-start(f32[2,1,64,256]{3,2,1,0:T(8,128)S(1)} %get-tuple-element.14.refs_1_), channel_id=1, source_target_pairs={{8,16},{16,8},{9,17},{17,9},{10,18},{18,10},{11,19},{19,11},{12,20... | collective-permute-start | bytes 393224 | tf_op jit(solution)/shard_map/ppermute | solution.py:270
